TPU v7x, 32 devices: a whole 2x2x4 slice. The times are simulated.
32 devices in a mesh: gx: 8 (over y, x, core), gy: 4 (over z).
Axes of the slice: x: 2, y: 2, z: 4, core: 2. Of those that a mesh axis runs over, the one named last changes fastest.
Arguments:
- spectrum: bfloat16 [32, 512, 1152], P('gx', 'gy'), may hold values from 0.099609375 to 2
- ocean_state: float32 [3, 16, 32, 512], P(None, None, 'gx', 'gy'), may hold values from -3 to 3
- sea_mask: int32 [32, 512], P('gx', 'gy'), may hold values from 0 to 1, as said below
Outputs:
- new_spectrum: bfloat16 [32, 512, 1152], P('gx', 'gy')
- new_ocean: float32 [3, 16, 32, 512], P(None, None, 'gx', 'gy')
Inputs may be any that keep to these rules, and one draw needn't show every extreme that they name: `sea_mask`: 1 marks a sea cell, 0 a land cell.
All inputs are finite; a program needn't handle non-finite values.
Results may differ from a plain program's by a relative error of at most 0.0043.
Values may be sent and summed in bfloat16 or wider, within the bound.
No kernel may reach another device: no remote copies, remote signals or barrier semaphores. Data moves between devices by JAX's collectives and lax.ppermute only.
A program may use at most 64 MiB of HBM per device.

v0:
```python
import math

import jax
import jax.numpy as jnp
from jax import lax
from jax.sharding import PartitionSpec as P

NF = 32
NDIR = 36
STEPS = 2


COURANT = 0.4
RATIO = 0.93
TURN = 0.1
STRESS = 0.1
CORIOLIS = 0.2
PRESS = 0.1
VISC = 0.15
ADVECT = 0.5
DIFFUSE = 0.15


def with_halo(array, sides, width):
    for axis, dim in sides:
        devices, length = (lax.axis_size(axis), array.shape[dim])
        up = [(i, (i + 1) % devices) for i in range(devices - 1)]
        down = [(j, i) for i, j in up]
        last = lax.slice_in_dim(array, length - width, length, axis=dim)
        initial = lax.slice_in_dim(array, 0, width, axis=dim)
        before = lax.ppermute(last, axis, up)
        after = lax.ppermute(initial, axis, down)
        array = jnp.concatenate([before, array, after], axis=dim)
    return array


def bin_tables(n_freq, n_dir):
    positions = jnp.arange(n_freq * n_dir, dtype=jnp.int32)
    dir_index = positions % n_dir
    freq_index = (positions // n_dir).astype(jnp.float32)
    speeds = COURANT * RATIO**freq_index
    angles = -0.5 * math.pi + (dir_index.astype(jnp.float32) + 0.5) * (2.0 * math.pi / n_dir)
    return (speeds, jnp.cos(angles), jnp.sin(angles), dir_index)


def beam_warming(courant, center, near_cell, far_cell):
    return -0.5 * courant * (
        3.0 * center - 4.0 * near_cell + far_cell
    ) + 0.5 * courant * courant * (center - 2.0 * near_cell + far_cell)


def turning_rate(cosines, sines, zonal_xgrad, zonal_ygrad, north_xgrad, north_ygrad):
    return TURN * (
        cosines * sines * (zonal_xgrad - north_ygrad)
        + sines * sines * north_xgrad
        - cosines * cosines * zonal_ygrad
    )


def stencil_terms(padded):
    middle = padded[..., 1:-1, 1:-1]
    grad_x = (padded[..., 2:, 1:-1] - padded[..., :-2, 1:-1]) * 0.5
    grad_y = (padded[..., 1:-1, 2:] - padded[..., 1:-1, :-2]) * 0.5
    laplace = (
        padded[..., 2:, 1:-1]
        + padded[..., :-2, 1:-1]
        + padded[..., 1:-1, 2:]
        + padded[..., 1:-1, :-2]
        - 4.0 * middle
    )
    return (middle, grad_x, grad_y, laplace)


def ocean_step(padded, stress, wet_cells):
    zonal, zonal_xgrad, zonal_ygrad, zonal_spread = stencil_terms(padded[0])
    north, north_xgrad, north_ygrad, north_spread = stencil_terms(padded[1])
    heat, heat_xgrad, heat_ygrad, heat_spread = stencil_terms(padded[2])
    push_x = PRESS * jnp.cumsum(heat_xgrad, axis=0)
    push_y = PRESS * jnp.cumsum(heat_ygrad, axis=0)
    surface = (jnp.arange(zonal.shape[0]) == 0).astype(jnp.float32)[:, None, None]
    zonal_next = wet_cells * (
        zonal + CORIOLIS * north - push_x + VISC * zonal_spread + surface * stress[0]
    )
    north_next = wet_cells * (
        north - CORIOLIS * zonal - push_y + VISC * north_spread + surface * stress[1]
    )
    heat_next = heat + wet_cells * (
        -ADVECT * (zonal * heat_xgrad + north * heat_ygrad) + DIFFUSE * heat_spread
    )
    return jnp.stack([zonal_next, north_next, heat_next])


def advance_all(spectrum_now, along_x, along_y, padded_ocean, wet_cells, tables, weights):
    tile_rows, tile_cols, n_bins = spectrum_now.shape
    speeds, cosines, sines, dir_index = tables
    half_dirs = NDIR // 2
    quarter = NDIR // 4
    _, zonal_xgrad, zonal_ygrad, _ = stencil_terms(padded_ocean[0, 0])
    _, north_xgrad, north_ygrad, _ = stencil_terms(padded_ocean[1, 0])
    east_side = dir_index >= half_dirs
    north_side = (dir_index < quarter) | (dir_index >= 3 * quarter)
    near_x = jnp.where(east_side, along_x[3 : tile_rows + 3], along_x[1 : tile_rows + 1]).astype(
        jnp.float32
    )
    far_x = jnp.where(east_side, along_x[4 : tile_rows + 4], along_x[0:tile_rows]).astype(
        jnp.float32
    )
    near_y = jnp.where(
        north_side, along_y[:, 3 : tile_cols + 3], along_y[:, 1 : tile_cols + 1]
    ).astype(jnp.float32)
    far_y = jnp.where(north_side, along_y[:, 4 : tile_cols + 4], along_y[:, 0:tile_cols]).astype(
        jnp.float32
    )
    center = spectrum_now.astype(jnp.float32)
    courant_x = speeds * jnp.abs(cosines)
    courant_y = speeds * jnp.abs(sines)
    turn_rate = turning_rate(
        cosines,
        sines,
        zonal_xgrad[:, :, None],
        zonal_ygrad[:, :, None],
        north_xgrad[:, :, None],
        north_ygrad[:, :, None],
    )
    previous = jnp.where(
        dir_index == 0, jnp.roll(center, -(NDIR - 1), axis=2), jnp.roll(center, 1, axis=2)
    )
    following = jnp.where(
        dir_index == NDIR - 1, jnp.roll(center, NDIR - 1, axis=2), jnp.roll(center, -1, axis=2)
    )
    turning = -(
        jnp.maximum(turn_rate, 0.0) * (center - previous)
        + jnp.minimum(turn_rate, 0.0) * (following - center)
    )
    updated = wet_cells[:, :, None] * (
        center
        + beam_warming(courant_x, center, near_x, far_x)
        + beam_warming(courant_y, center, near_y, far_y)
        + turning
    )
    flat_stress = jnp.dot(
        spectrum_now.reshape(tile_rows * tile_cols, n_bins),
        weights,
        preferred_element_type=jnp.float32,
    )
    stress = flat_stress.T.reshape(2, tile_rows, tile_cols)
    ocean_next = ocean_step(padded_ocean, stress, wet_cells)
    return (updated.astype(jnp.bfloat16), ocean_next)


def local(spectrum, ocean_state, sea_mask):
    wet_cells = sea_mask.astype(jnp.float32)
    spectrum_now = spectrum * sea_mask.astype(jnp.bfloat16)[:, :, None]
    ocean_now = ocean_state
    tables = bin_tables(NF, NDIR)
    speeds, cosines, sines, _ = tables
    weights = (STRESS * speeds[None, :] * jnp.stack([cosines, sines])).astype(jnp.bfloat16).T
    for step_index in range(STEPS):
        padded_ocean = with_halo(ocean_now, (("gx", 2), ("gy", 3)), 1)
        padded = with_halo(spectrum_now, (("gx", 0), ("gy", 1)), 2)
        along_x = padded[:, 2:-2]
        along_y = padded[2:-2]

        def advance(current=spectrum_now, rims_x=along_x, rims_y=along_y, faces=padded_ocean):
            return advance_all(current, rims_x, rims_y, faces, wet_cells, tables, weights)

        spectrum_now, ocean_now = advance()
    return (spectrum_now, ocean_now)


def solution(mesh):
    placed = (P("gx", "gy", None), P(None, None, "gx", "gy"), P("gx", "gy"))
    return jax.shard_map(
        local,
        mesh=mesh,
        in_specs=placed,
        out_specs=(P("gx", "gy", None), P(None, None, "gx", "gy")),
        check_vma=False,
    )
```

profile of v0, /device:TPU:22, one launch (start us, length us, event | category | flops | bytes accessed | tf_op | source)
XLA Modules:
  0.0 101.4 jit_solution(11936357432295831615)
XLA Ops:
  0.6 1.0 fusion.139
  1.6 1.9 %collective-permute-start.4 = (f32[3,16,1,128]{3,2,1,0:T(1,128)S(1)}, f32[3,16,1,128]{3,2,1,0:T(1,128)S(1)}, u32[]{:S(2)}, u32[]{:S(2)}) collective-permute-start(f32[3,16,1,128]{3,2,1,0:T(1,128)S(1)} %get-tuple-element.42), channel_id=1, source_target_pairs={{0,4},{4,8},{8,12},{12,16},{16,20},{20,24},{24,28},{1,5},{5,9},{9,... | collective-permute-start | bytes 73736 | tf_op jit(solution)/shard_map/ppermute | solution.py:31
  3.6 3.6 %collective-permute-start.5 = (f32[3,16,1,128]{3,2,1,0:T(1,128)S(1)}, f32[3,16,1,128]{3,2,1,0:T(1,128)S(1)}, u32[]{:S(2)}, u32[]{:S(2)}) collective-permute-start(f32[3,16,1,128]{3,2,1,0:T(1,128)S(1)} %get-tuple-element.43), channel_id=1, source_target_pairs={{4,0},{8,4},{12,8},{16,12},{20,16},{24,20},{28,24},{5,1},{9,5},{13... | collective-permute-start | bytes 73736 | tf_op jit(solution)/shard_map/ppermute | solution.py:32
  7.2 0.8 fusion.142
  8.0 1.5 %broadcast_multiply_fusion = bf16[4,128,1152]{2,1,0:T(8,128)(2,1)S(1)} fusion(bf16[4,128,1152]{2,1,0:T(8,128)(2,1)} %param.3, bf16[4,128]{1,0:T(4,128)(2,1)S(1)} %get-tuple-element.55), kind=kLoop, calls=%fused_computation.124 | loop fusion | flops 589824 | bytes 2360320 | tf_op jit(solution)/shard_map/mul | solution.py:153
  9.5 1.9 %collective-permute-start = (bf16[2,128,1152]{2,1,0:T(8,128)(2,1)S(1)}, bf16[2,128,1152]{2,1,0:T(8,128)(2,1)S(1)}, u32[]{:S(2)}, u32[]{:S(2)}) collective-permute-start(bf16[2,128,1152]{2,1,0:T(8,128)(2,1)S(1)} %get-tuple-element.16), channel_id=1, source_target_pairs={{4,0},{8,4},{12,8},{16,12},{20,16},{24,20},{28,24},{5,1},{9,5},{13... | collective-permute-start | bytes 1769480 | tf_op jit(solution)/shard_map/ppermute | solution.py:32
  11.5 2.4 %collective-permute-start.1 = (bf16[2,128,1152]{2,1,0:T(8,128)(2,1)S(1)}, bf16[2,128,1152]{2,1,0:T(8,128)(2,1)S(1)}, u32[]{:S(2)}, u32[]{:S(2)}) collective-permute-start(bf16[2,128,1152]{2,1,0:T(8,128)(2,1)S(1)} %get-tuple-element.17), channel_id=1, source_target_pairs={{0,4},{4,8},{8,12},{12,16},{16,20},{20,24},{24,28},{1,5},{5,9},{9,... | collective-permute-start | bytes 1769480 | tf_op jit(solution)/shard_map/ppermute | solution.py:31
  15.2 0.7 fusion.133
  16.6 3.5 %collective-permute-start.6 = (f32[3,16,6,1]{3,2,1,0:T(8,128)S(1)}, f32[3,16,6,1]{3,2,1,0:T(8,128)S(1)}, u32[]{:S(2)}, u32[]{:S(2)}) collective-permute-start(f32[3,16,6,1]{3,2,1,0:T(8,128)S(1)} %get-tuple-element.38), channel_id=1, source_target_pairs={{0,1},{1,2},{2,3},{4,5},{5,6},{6,7},{8,9},{9,10},{10,11},{12,13},{... | collective-permute-start | bytes 3464 | tf_op jit(solution)/shard_map/ppermute | solution.py:31
  20.0 2.4 %collective-permute-start.7 = (f32[3,16,6,1]{3,2,1,0:T(8,128)S(1)}, f32[3,16,6,1]{3,2,1,0:T(8,128)S(1)}, u32[]{:S(2)}, u32[]{:S(2)}) collective-permute-start(f32[3,16,6,1]{3,2,1,0:T(8,128)S(1)} %get-tuple-element.39), channel_id=1, source_target_pairs={{1,0},{2,1},{3,2},{5,4},{6,5},{7,6},{9,8},{10,9},{11,10},{13,12},{... | collective-permute-start | bytes 3464 | tf_op jit(solution)/shard_map/ppermute | solution.py:32
  22.4 2.2 %collective-permute-done.6 = f32[3,16,6,1]{3,2,1,0:T(8,128)S(1)} collective-permute-done((f32[3,16,6,1]{3,2,1,0:T(8,128)S(1)}, f32[3,16,6,1]{3,2,1,0:T(8,128)S(1)}, u32[]{:S(2)}, u32[]{:S(2)}) %collective-permute-start.6) | collective-permute-done | bytes 1184 | tf_op jit(solution)/shard_map/ppermute | solution.py:31
  24.6 3.2 %collective-permute-done.7 = f32[3,16,6,1]{3,2,1,0:T(8,128)S(1)} collective-permute-done((f32[3,16,6,1]{3,2,1,0:T(8,128)S(1)}, f32[3,16,6,1]{3,2,1,0:T(8,128)S(1)}, u32[]{:S(2)}, u32[]{:S(2)}) %collective-permute-start.7) | collective-permute-done | bytes 1184 | tf_op jit(solution)/shard_map/ppermute | solution.py:32
  29.0 1.9 %collective-permute-start.12 = (f32[3,16,1,128]{3,2,1,0:T(1,128)S(1)}, f32[3,16,1,128]{3,2,1,0:T(1,128)S(1)}, u32[]{:S(2)}, u32[]{:S(2)}) collective-permute-start(f32[3,16,1,128]{3,2,1,0:T(1,128)S(1)} %get-tuple-element.40), channel_id=1, source_target_pairs={{0,4},{4,8},{8,12},{12,16},{16,20},{20,24},{24,28},{1,5},{5,9},{9,... | collective-permute-start | bytes 73736 | tf_op jit(solution)/shard_map/ppermute | solution.py:31
  30.9 3.6 %collective-permute-start.13 = (f32[3,16,1,128]{3,2,1,0:T(1,128)S(1)}, f32[3,16,1,128]{3,2,1,0:T(1,128)S(1)}, u32[]{:S(2)}, u32[]{:S(2)}) collective-permute-start(f32[3,16,1,128]{3,2,1,0:T(1,128)S(1)} %get-tuple-element.41), channel_id=1, source_target_pairs={{4,0},{8,4},{12,8},{16,12},{20,16},{24,20},{28,24},{5,1},{9,5},{13... | collective-permute-start | bytes 73736 | tf_op jit(solution)/shard_map/ppermute | solution.py:32
  34.6 1.4 %collective-permute-done.13 = f32[3,16,1,128]{3,2,1,0:T(1,128)S(1)} collective-permute-done((f32[3,16,1,128]{3,2,1,0:T(1,128)S(1)}, f32[3,16,1,128]{3,2,1,0:T(1,128)S(1)}, u32[]{:S(2)}, u32[]{:S(2)}) %collective-permute-start.13) | collective-permute-done | bytes 24608 | tf_op jit(solution)/shard_map/ppermute | solution.py:32
  36.2 1.9 %collective-permute-start.14 = (f32[3,16,6,1]{3,2,1,0:T(8,128)S(1)}, f32[3,16,6,1]{3,2,1,0:T(8,128)S(1)}, u32[]{:S(2)}, u32[]{:S(2)}) collective-permute-start(f32[3,16,6,1]{3,2,1,0:T(8,128)S(1)} %get-tuple-element.36), channel_id=1, source_target_pairs={{0,1},{1,2},{2,3},{4,5},{5,6},{6,7},{8,9},{9,10},{10,11},{12,13},{... | collective-permute-start | bytes 3464 | tf_op jit(solution)/shard_map/ppermute | solution.py:31
  38.1 3.9 %collective-permute-start.15 = (f32[3,16,6,1]{3,2,1,0:T(8,128)S(1)}, f32[3,16,6,1]{3,2,1,0:T(8,128)S(1)}, u32[]{:S(2)}, u32[]{:S(2)}) collective-permute-start(f32[3,16,6,1]{3,2,1,0:T(8,128)S(1)} %get-tuple-element.37), channel_id=1, source_target_pairs={{1,0},{2,1},{3,2},{5,4},{6,5},{7,6},{9,8},{10,9},{11,10},{13,12},{... | collective-permute-start | bytes 3464 | tf_op jit(solution)/shard_map/ppermute | solution.py:32
  42.2 1.6 %collective-permute-done.14 = f32[3,16,6,1]{3,2,1,0:T(8,128)S(1)} collective-permute-done((f32[3,16,6,1]{3,2,1,0:T(8,128)S(1)}, f32[3,16,6,1]{3,2,1,0:T(8,128)S(1)}, u32[]{:S(2)}, u32[]{:S(2)}) %collective-permute-start.14) | collective-permute-done | bytes 1184 | tf_op jit(solution)/shard_map/ppermute | solution.py:31
  43.8 1.9 %collective-permute-done.15 = f32[3,16,6,1]{3,2,1,0:T(8,128)S(1)} collective-permute-done((f32[3,16,6,1]{3,2,1,0:T(8,128)S(1)}, f32[3,16,6,1]{3,2,1,0:T(8,128)S(1)}, u32[]{:S(2)}, u32[]{:S(2)}) %collective-permute-start.15) | collective-permute-done | bytes 1184 | tf_op jit(solution)/shard_map/ppermute | solution.py:32
  46.5 3.9 %collective-permute-start.2 = (bf16[8,2,1152]{2,1,0:T(2,128)(2,1)S(1)}, bf16[8,2,1152]{2,1,0:T(2,128)(2,1)S(1)}, u32[]{:S(2)}, u32[]{:S(2)}) collective-permute-start(bf16[8,2,1152]{2,1,0:T(2,128)(2,1)S(1)} %get-tuple-element.4), channel_id=1, source_target_pairs={{1,0},{2,1},{3,2},{5,4},{6,5},{7,6},{9,8},{10,9},{11,10},{13,12},{... | collective-permute-start | bytes 110600 | tf_op jit(solution)/shard_map/ppermute | solution.py:32
  50.5 1.9 %collective-permute-start.3 = (bf16[8,2,1152]{2,1,0:T(2,128)(2,1)S(1)}, bf16[8,2,1152]{2,1,0:T(2,128)(2,1)S(1)}, u32[]{:S(2)}, u32[]{:S(2)}) collective-permute-start(bf16[8,2,1152]{2,1,0:T(2,128)(2,1)S(1)} %get-tuple-element.5), channel_id=1, source_target_pairs={{0,1},{1,2},{2,3},{4,5},{5,6},{6,7},{8,9},{9,10},{10,11},{12,13},{... | collective-permute-start | bytes 110600 | tf_op jit(solution)/shard_map/ppermute | solution.py:31
  52.5 3.8 %collective-permute-done.3 = bf16[8,2,1152]{2,1,0:T(2,128)(2,1)S(1)} collective-permute-done((bf16[8,2,1152]{2,1,0:T(2,128)(2,1)S(1)}, bf16[8,2,1152]{2,1,0:T(2,128)(2,1)S(1)}, u32[]{:S(2)}, u32[]{:S(2)}) %collective-permute-start.3) | collective-permute-done | bytes 36896 | tf_op jit(solution)/shard_map/ppermute | solution.py:31
  56.3 7.5 %fusion.12 = bf16[4,128,1152]{2,1,0:T(8,128)(2,1)S(1)} fusion(bf16[4,128,1152]{2,1,0:T(8,128)(2,1)S(1)} %broadcast_multiply_fusion, f32[4,128,35]{2,1,0:T(8,128)S(1)} %get-tuple-element.23, f32[4,128,1117]{2,1,0:T(8,128)S(1)} %get-tuple-element.25, f32[4,128,1151]{2,1,0:T(8,128)S(1)} %get-tuple-element.19, f32[4,128,1]{2,1,0:T(8,128)S(1)} %get-tuple-element.21, ...), kind=kLoop, calls=%fused_computation.40 | loop fusion | flops 59572224 | bytes 13094912 | tf_op jit(solution)/shard_map/convert_element_type | solution.py:148
  65.6 1.9 %collective-permute-start.8 = (bf16[2,128,1152]{2,1,0:T(8,128)(2,1)S(1)}, bf16[2,128,1152]{2,1,0:T(8,128)(2,1)S(1)}, u32[]{:S(2)}, u32[]{:S(2)}) collective-permute-start(bf16[2,128,1152]{2,1,0:T(8,128)(2,1)S(1)} %get-tuple-element.6), channel_id=1, source_target_pairs={{4,0},{8,4},{12,8},{16,12},{20,16},{24,20},{28,24},{5,1},{9,5},{13... | collective-permute-start | bytes 1769480 | tf_op jit(solution)/shard_map/ppermute | solution.py:32
  67.5 2.4 %collective-permute-start.9 = (bf16[2,128,1152]{2,1,0:T(8,128)(2,1)S(1)}, bf16[2,128,1152]{2,1,0:T(8,128)(2,1)S(1)}, u32[]{:S(2)}, u32[]{:S(2)}) collective-permute-start(bf16[2,128,1152]{2,1,0:T(8,128)(2,1)S(1)} %get-tuple-element.7), channel_id=1, source_target_pairs={{0,4},{4,8},{8,12},{12,16},{16,20},{20,24},{24,28},{1,5},{5,9},{9,... | collective-permute-start | bytes 1769480 | tf_op jit(solution)/shard_map/ppermute | solution.py:31
  69.9 0.7 fusion.128
  70.6 4.3 %collective-permute-done.8 = bf16[2,128,1152]{2,1,0:T(8,128)(2,1)S(1)} collective-permute-done((bf16[2,128,1152]{2,1,0:T(8,128)(2,1)S(1)}, bf16[2,128,1152]{2,1,0:T(8,128)(2,1)S(1)}, u32[]{:S(2)}, u32[]{:S(2)}) %collective-permute-start.8) | collective-permute-done | bytes 589856 | tf_op jit(solution)/shard_map/ppermute | solution.py:32
  74.9 9.9 %collective-permute-done.9 = bf16[2,128,1152]{2,1,0:T(8,128)(2,1)S(1)} collective-permute-done((bf16[2,128,1152]{2,1,0:T(8,128)(2,1)S(1)}, bf16[2,128,1152]{2,1,0:T(8,128)(2,1)S(1)}, u32[]{:S(2)}, u32[]{:S(2)}) %collective-permute-start.9) | collective-permute-done | bytes 589856 | tf_op jit(solution)/shard_map/ppermute | solution.py:31
  84.9 2.4 %collective-permute-start.10 = (bf16[8,2,1152]{2,1,0:T(2,128)(2,1)S(1)}, bf16[8,2,1152]{2,1,0:T(2,128)(2,1)S(1)}, u32[]{:S(2)}, u32[]{:S(2)}) collective-permute-start(bf16[8,2,1152]{2,1,0:T(2,128)(2,1)S(1)} %get-tuple-element.2), channel_id=1, source_target_pairs={{1,0},{2,1},{3,2},{5,4},{6,5},{7,6},{9,8},{10,9},{11,10},{13,12},{... | collective-permute-start | bytes 110600 | tf_op jit(solution)/shard_map/ppermute | solution.py:32
  87.2 3.5 %collective-permute-start.11 = (bf16[8,2,1152]{2,1,0:T(2,128)(2,1)S(1)}, bf16[8,2,1152]{2,1,0:T(2,128)(2,1)S(1)}, u32[]{:S(2)}, u32[]{:S(2)}) collective-permute-start(bf16[8,2,1152]{2,1,0:T(2,128)(2,1)S(1)} %get-tuple-element.3), channel_id=1, source_target_pairs={{0,1},{1,2},{2,3},{4,5},{5,6},{6,7},{8,9},{9,10},{10,11},{12,13},{... | collective-permute-start | bytes 110600 | tf_op jit(solution)/shard_map/ppermute | solution.py:31
  91.4 1.7 %collective-permute-done.11 = bf16[8,2,1152]{2,1,0:T(2,128)(2,1)S(1)} collective-permute-done((bf16[8,2,1152]{2,1,0:T(2,128)(2,1)S(1)}, bf16[8,2,1152]{2,1,0:T(2,128)(2,1)S(1)}, u32[]{:S(2)}, u32[]{:S(2)}) %collective-permute-start.11) | collective-permute-done | bytes 36896 | tf_op jit(solution)/shard_map/ppermute | solution.py:31
  93.1 8.3 %fusion.22 = bf16[4,128,1152]{2,1,0:T(8,128)(2,1)} fusion(bf16[4,128,1152]{2,1,0:T(8,128)(2,1)S(1)} %fusion.12, f32[4,128,35]{2,1,0:T(8,128)S(1)} %get-tuple-element.13, f32[4,128,1117]{2,1,0:T(8,128)S(1)} %get-tuple-element.15, f32[4,128,1151]{2,1,0:T(8,128)S(1)} %get-tuple-element.9, f32[4,128,1]{2,1,0:T(8,128)S(1)} %get-tuple-element.11, ...), kind=kLoop, calls=%fused_computation.50 | loop fusion | flops 59572224 | bytes 13094912 | tf_op jit(solution)/shard_map/convert_element_type | solution.py:148
  (52 shorter events, 6.6 us)
Async XLA Ops:
  1.6 14.7 %collective-permute-start.4 = (f32[3,16,1,128]{3,2,1,0:T(1,128)S(1)}, f32[3,16,1,128]{3,2,1,0:T(1,128)S(1)}, u32[]{:S(2)}, u32[]{:S(2)}) collective-permute-start(f32[3,16,1,128]{3,2,1,0:T(1,128)S(1)} %get-tuple-element.42), channel_id=1, source_target_pairs={{0,4},{4,8},{8,12},{12,16},{16,20},{20,24},{24,28},{1,5},{5,9},{9,... | collective-permute-start | bytes 73736 | tf_op jit(solution)/shard_map/ppermute | solution.py:31
  3.6 12.8 %collective-permute-start.5 = (f32[3,16,1,128]{3,2,1,0:T(1,128)S(1)}, f32[3,16,1,128]{3,2,1,0:T(1,128)S(1)}, u32[]{:S(2)}, u32[]{:S(2)}) collective-permute-start(f32[3,16,1,128]{3,2,1,0:T(1,128)S(1)} %get-tuple-element.43), channel_id=1, source_target_pairs={{4,0},{8,4},{12,8},{16,12},{20,16},{24,20},{28,24},{5,1},{9,5},{13... | collective-permute-start | bytes 73736 | tf_op jit(solution)/shard_map/ppermute | solution.py:32
  9.5 36.9 %collective-permute-start = (bf16[2,128,1152]{2,1,0:T(8,128)(2,1)S(1)}, bf16[2,128,1152]{2,1,0:T(8,128)(2,1)S(1)}, u32[]{:S(2)}, u32[]{:S(2)}) collective-permute-start(bf16[2,128,1152]{2,1,0:T(8,128)(2,1)S(1)} %get-tuple-element.16), channel_id=1, source_target_pairs={{4,0},{8,4},{12,8},{16,12},{20,16},{24,20},{28,24},{5,1},{9,5},{13... | collective-permute-start | bytes 1769480 | tf_op jit(solution)/shard_map/ppermute | solution.py:32
  11.5 35.0 %collective-permute-start.1 = (bf16[2,128,1152]{2,1,0:T(8,128)(2,1)S(1)}, bf16[2,128,1152]{2,1,0:T(8,128)(2,1)S(1)}, u32[]{:S(2)}, u32[]{:S(2)}) collective-permute-start(bf16[2,128,1152]{2,1,0:T(8,128)(2,1)S(1)} %get-tuple-element.17), channel_id=1, source_target_pairs={{0,4},{4,8},{8,12},{12,16},{16,20},{20,24},{24,28},{1,5},{5,9},{9,... | collective-permute-start | bytes 1769480 | tf_op jit(solution)/shard_map/ppermute | solution.py:31
  15.2 1.2 %copy-start = (f32[3,16,4,128]{3,2,1,0:T(4,128)S(1)}, f32[3,16,4,128]{3,2,1,0:T(4,128)}, u32[]{:S(2)}) copy-start(f32[3,16,4,128]{3,2,1,0:T(4,128)} %param.4) | copy-start | bytes 294916
  16.6 8.1 %collective-permute-start.6 = (f32[3,16,6,1]{3,2,1,0:T(8,128)S(1)}, f32[3,16,6,1]{3,2,1,0:T(8,128)S(1)}, u32[]{:S(2)}, u32[]{:S(2)}) collective-permute-start(f32[3,16,6,1]{3,2,1,0:T(8,128)S(1)} %get-tuple-element.38), channel_id=1, source_target_pairs={{0,1},{1,2},{2,3},{4,5},{5,6},{6,7},{8,9},{9,10},{10,11},{12,13},{... | collective-permute-start | bytes 3464 | tf_op jit(solution)/shard_map/ppermute | solution.py:31
  20.0 7.8 %collective-permute-start.7 = (f32[3,16,6,1]{3,2,1,0:T(8,128)S(1)}, f32[3,16,6,1]{3,2,1,0:T(8,128)S(1)}, u32[]{:S(2)}, u32[]{:S(2)}) collective-permute-start(f32[3,16,6,1]{3,2,1,0:T(8,128)S(1)} %get-tuple-element.39), channel_id=1, source_target_pairs={{1,0},{2,1},{3,2},{5,4},{6,5},{7,6},{9,8},{10,9},{11,10},{13,12},{... | collective-permute-start | bytes 3464 | tf_op jit(solution)/shard_map/ppermute | solution.py:32
  29.0 5.7 %collective-permute-start.12 = (f32[3,16,1,128]{3,2,1,0:T(1,128)S(1)}, f32[3,16,1,128]{3,2,1,0:T(1,128)S(1)}, u32[]{:S(2)}, u32[]{:S(2)}) collective-permute-start(f32[3,16,1,128]{3,2,1,0:T(1,128)S(1)} %get-tuple-element.40), channel_id=1, source_target_pairs={{0,4},{4,8},{8,12},{12,16},{16,20},{20,24},{24,28},{1,5},{5,9},{9,... | collective-permute-start | bytes 73736 | tf_op jit(solution)/shard_map/ppermute | solution.py:31
  30.9 5.1 %collective-permute-start.13 = (f32[3,16,1,128]{3,2,1,0:T(1,128)S(1)}, f32[3,16,1,128]{3,2,1,0:T(1,128)S(1)}, u32[]{:S(2)}, u32[]{:S(2)}) collective-permute-start(f32[3,16,1,128]{3,2,1,0:T(1,128)S(1)} %get-tuple-element.41), channel_id=1, source_target_pairs={{4,0},{8,4},{12,8},{16,12},{20,16},{24,20},{28,24},{5,1},{9,5},{13... | collective-permute-start | bytes 73736 | tf_op jit(solution)/shard_map/ppermute | solution.py:32
  36.2 7.6 %collective-permute-start.14 = (f32[3,16,6,1]{3,2,1,0:T(8,128)S(1)}, f32[3,16,6,1]{3,2,1,0:T(8,128)S(1)}, u32[]{:S(2)}, u32[]{:S(2)}) collective-permute-start(f32[3,16,6,1]{3,2,1,0:T(8,128)S(1)} %get-tuple-element.36), channel_id=1, source_target_pairs={{0,1},{1,2},{2,3},{4,5},{5,6},{6,7},{8,9},{9,10},{10,11},{12,13},{... | collective-permute-start | bytes 3464 | tf_op jit(solution)/shard_map/ppermute | solution.py:31
  38.1 7.6 %collective-permute-start.15 = (f32[3,16,6,1]{3,2,1,0:T(8,128)S(1)}, f32[3,16,6,1]{3,2,1,0:T(8,128)S(1)}, u32[]{:S(2)}, u32[]{:S(2)}) collective-permute-start(f32[3,16,6,1]{3,2,1,0:T(8,128)S(1)} %get-tuple-element.37), channel_id=1, source_target_pairs={{1,0},{2,1},{3,2},{5,4},{6,5},{7,6},{9,8},{10,9},{11,10},{13,12},{... | collective-permute-start | bytes 3464 | tf_op jit(solution)/shard_map/ppermute | solution.py:32
  46.5 5.9 %collective-permute-start.2 = (bf16[8,2,1152]{2,1,0:T(2,128)(2,1)S(1)}, bf16[8,2,1152]{2,1,0:T(2,128)(2,1)S(1)}, u32[]{:S(2)}, u32[]{:S(2)}) collective-permute-start(bf16[8,2,1152]{2,1,0:T(2,128)(2,1)S(1)} %get-tuple-element.4), channel_id=1, source_target_pairs={{1,0},{2,1},{3,2},{5,4},{6,5},{7,6},{9,8},{10,9},{11,10},{13,12},{... | collective-permute-start | bytes 110600 | tf_op jit(solution)/shard_map/ppermute | solution.py:32
  50.5 5.9 %collective-permute-start.3 = (bf16[8,2,1152]{2,1,0:T(2,128)(2,1)S(1)}, bf16[8,2,1152]{2,1,0:T(2,128)(2,1)S(1)}, u32[]{:S(2)}, u32[]{:S(2)}) collective-permute-start(bf16[8,2,1152]{2,1,0:T(2,128)(2,1)S(1)} %get-tuple-element.5), channel_id=1, source_target_pairs={{0,1},{1,2},{2,3},{4,5},{5,6},{6,7},{8,9},{9,10},{10,11},{12,13},{... | collective-permute-start | bytes 110600 | tf_op jit(solution)/shard_map/ppermute | solution.py:31
  65.6 9.3 %collective-permute-start.8 = (bf16[2,128,1152]{2,1,0:T(8,128)(2,1)S(1)}, bf16[2,128,1152]{2,1,0:T(8,128)(2,1)S(1)}, u32[]{:S(2)}, u32[]{:S(2)}) collective-permute-start(bf16[2,128,1152]{2,1,0:T(8,128)(2,1)S(1)} %get-tuple-element.6), channel_id=1, source_target_pairs={{4,0},{8,4},{12,8},{16,12},{20,16},{24,20},{28,24},{5,1},{9,5},{13... | collective-permute-start | bytes 1769480 | tf_op jit(solution)/shard_map/ppermute | solution.py:32
  67.5 17.3 %collective-permute-start.9 = (bf16[2,128,1152]{2,1,0:T(8,128)(2,1)S(1)}, bf16[2,128,1152]{2,1,0:T(8,128)(2,1)S(1)}, u32[]{:S(2)}, u32[]{:S(2)}) collective-permute-start(bf16[2,128,1152]{2,1,0:T(8,128)(2,1)S(1)} %get-tuple-element.7), channel_id=1, source_target_pairs={{0,4},{4,8},{8,12},{12,16},{16,20},{20,24},{24,28},{1,5},{5,9},{9,... | collective-permute-start | bytes 1769480 | tf_op jit(solution)/shard_map/ppermute | solution.py:31
  84.9 6.5 %collective-permute-start.10 = (bf16[8,2,1152]{2,1,0:T(2,128)(2,1)S(1)}, bf16[8,2,1152]{2,1,0:T(2,128)(2,1)S(1)}, u32[]{:S(2)}, u32[]{:S(2)}) collective-permute-start(bf16[8,2,1152]{2,1,0:T(2,128)(2,1)S(1)} %get-tuple-element.2), channel_id=1, source_target_pairs={{1,0},{2,1},{3,2},{5,4},{6,5},{7,6},{9,8},{10,9},{11,10},{13,12},{... | collective-permute-start | bytes 110600 | tf_op jit(solution)/shard_map/ppermute | solution.py:32
  87.2 5.9 %collective-permute-start.11 = (bf16[8,2,1152]{2,1,0:T(2,128)(2,1)S(1)}, bf16[8,2,1152]{2,1,0:T(2,128)(2,1)S(1)}, u32[]{:S(2)}, u32[]{:S(2)}) collective-permute-start(bf16[8,2,1152]{2,1,0:T(2,128)(2,1)S(1)} %get-tuple-element.3), channel_id=1, source_target_pairs={{0,1},{1,2},{2,3},{4,5},{5,6},{6,7},{8,9},{9,10},{10,11},{12,13},{... | collective-permute-start | bytes 110600 | tf_op jit(solution)/shard_map/ppermute | solution.py:31
where the time goes:
time: 102 us; the launch traced here: 101 us
  starting transfers between devices  43.2 us (42%)
  waiting for transfers between devices  30.1 us (30%)
  other arithmetic  21.8 us (21%)
  local copies, waits for them, and re-layouts  4.4 us (4%)
  between operations  1.07 us (1%)
    ppermute x8, starting transfers between devices, with_halo(): after = lax.ppermute(initial, axis, down)  23.7 us
    ppermute x8, starting transfers between devices, with_halo(): before = lax.ppermute(last, axis, up)  19.5 us
    ppermute x8, waiting for transfers between devices, with_halo(): before = lax.ppermute(last, axis, up)  19.3 us
    convert_element_type x2, other arithmetic, advance_all(): return (updated.astype(jnp.bfloat16), ocean_next)  15.8 us
    ppermute x8, waiting for transfers between devices, with_halo(): after = lax.ppermute(initial, axis, down)  10.8 us
  transfers between devices with their start and end apart: 16, of which 9 were waited for; matrix products, arithmetic and copies ran while one was open for 8% of the time, Pallas kernels for 0%

commit v1 on v0

v1 whole, which is shorter than its diff:
```python
import math

import jax
import jax.numpy as jnp
import numpy as np
from jax import lax
from jax.experimental import pallas as pl
from jax.experimental.pallas import tpu as pltpu
from jax.sharding import PartitionSpec as P

NF = 32
NDIR = 36
NZ = 16
HALF = NDIR // 2
QUARTER = NDIR // 4
ROWS = 4
LANES = 128
BINS = NF * NDIR

COURANT = 0.4
RATIO = 0.93
TURN = 0.1
STRESS = 0.1
CORIOLIS = 0.2
PRESS = 0.1
VISC = 0.15
ADVECT = 0.5
DIFFUSE = 0.15

F32 = jnp.float32
BF16 = jnp.bfloat16
VM = pl.BlockSpec(memory_space=pltpu.VMEM)
PARAMS = pltpu.CompilerParams(vmem_limit_bytes=48 * 1024 * 1024)

SPECTRA = 2 * HALF * NF
OCEAN = 3 * NZ
XROWS = SPECTRA + 2 * OCEAN
YROWS = HALF * 8 + 16

ANGLES = -0.5 * math.pi + (np.arange(NDIR, dtype=np.float32) + np.float32(0.5)) * np.float32(
    2.0 * math.pi / NDIR
)
COS = np.cos(ANGLES).astype(np.float32)
SIN = np.sin(ANGLES).astype(np.float32)
SPEEDS = (COURANT * RATIO ** np.arange(NF, dtype=np.float64)).astype(np.float32)


def stress_table():
    table = np.zeros((ROWS, 16, NDIR, NF), np.float32)
    for c, part in enumerate((COS, SIN)):
        weights = np.float32(STRESS) * SPEEDS[None, :] * part[:, None]
        for x in range(ROWS):
            table[x, c * 8 + 1 + x] = weights
    return table.reshape(ROWS, 16, BINS)


def is_even(axis):
    return lax.rem(lax.axis_index(axis), 2) == 0


def split(v):
    high = v.astype(BF16).astype(F32)
    return high, v - high


def roll(v, shift, axis):
    return pltpu.roll(v, shift % v.shape[axis], axis)


def lane_of(shape):
    return lax.broadcasted_iota(jnp.int32, shape, len(shape) - 1)


def pack_y_edges(cells, k, south, out_ref, lanes):
    start = LANES - 2 if south else 0
    packed = jnp.zeros((8, LANES), F32)
    for x in range(ROWS):
        for g in range(4):
            at = 8 * g + 2 * x
            moved = roll(cells[x][8 * g : 8 * g + 8], at - start, 1)
            packed = jnp.where((lanes >= at) & (lanes < at + 2), moved, packed)
    out_ref[k] = packed


def pack_ocean_columns(blocks, lanes):
    first = jnp.zeros((8, LANES), F32)
    last = jnp.zeros((8, LANES), F32)
    for c in range(3):
        for z in range(NZ):
            block = blocks[c][8 * z : 8 * z + 8]
            at = c * NZ + z
            first = jnp.where(lanes == at, roll(block, at, 1), first)
            last = jnp.where(lanes == at, roll(block, at - (LANES - 1), 1), last)
    return first, last


def send_x(n_ref, ocean_rows, mine_ref, low_side):
    row = jnp.where(low_side, 0, 2)
    first = jnp.where(low_side, HALF, 0)
    edge = n_ref[pl.ds(row, 2), pl.ds(first, HALF)]
    mine_ref[0:SPECTRA, :] = edge.reshape(SPECTRA, LANES).astype(BF16)
    low, high = ocean_rows
    whole, rest = split(jnp.where(low_side, low, high))
    mine_ref[SPECTRA : SPECTRA + OCEAN, :] = whole.astype(BF16)
    mine_ref[SPECTRA + OCEAN : XROWS, :] = rest.astype(BF16)


def send_y(edges_ref, first, last, even, outs):
    for slot, out_ref in enumerate(outs):
        takes_last = even if slot == 0 else jnp.logical_not(even)
        which = takes_last.astype(jnp.int32)
        out_ref[0 : HALF * 8, :] = edges_ref[which].reshape(HALF * 8, LANES).astype(BF16)
        whole, rest = split(jnp.where(takes_last, last, first))
        out_ref[HALF * 8 : YROWS, :] = jnp.concatenate([whole, rest], 0).astype(BF16)


def start_kernel(s_ref, o_ref, mask_ref, n_ref, xe_ref, xo_ref, ye_ref, yo_ref, t_ref, e_ref):
    lanes = lane_of((8, LANES))
    wet = mask_ref[...].astype(F32)
    for x in range(ROWS):
        t_ref[x] = jnp.transpose(s_ref[x].astype(F32))

    def pack(south, shift):
        def body(k, carry):
            cells = []
            for x in range(ROWS):
                cell = t_ref[x, pl.ds(k, NF, stride=NDIR), :] * wet[x : x + 1]
                n_ref[x, k] = cell
                cells.append(cell)
            pack_y_edges(cells, k - shift, south, e_ref.at[1 if south else 0], lanes)
            return carry

        return body

    lax.fori_loop(0, QUARTER, pack(False, 0), 0)
    lax.fori_loop(QUARTER, 3 * QUARTER, pack(True, QUARTER), 0)
    lax.fori_loop(3 * QUARTER, NDIR, pack(False, HALF), 0)
    even_x, even_y = is_even("gx"), is_even("gy")
    rows = tuple(o_ref[:, :, r, :].reshape(OCEAN, LANES) for r in (0, ROWS - 1))
    send_x(n_ref, rows, xe_ref, jnp.logical_not(even_x))
    send_x(n_ref, rows, xo_ref, even_x)
    pad = jnp.zeros((1, LANES), F32)
    blocks = [
        jnp.concatenate(
            [part for z in range(NZ) for part in (pad, o_ref[c, z], pad, pad, pad)], 0
        )
        for c in range(3)
    ]
    first, last = pack_ocean_columns(blocks, lanes)
    send_y(e_ref, first, last, even_y, (ye_ref, yo_ref))


def tables_kernel(speed_ref, tab_ref):
    speed = speed_ref[...]
    for k in range(NDIR):
        cx, cy = speed * abs(float(COS[k])), speed * abs(float(SIN[k]))
        near_x, far_x = cx * (2.0 - cx), (0.5 * cx) * (cx - 1.0)
        near_y, far_y = cy * (2.0 - cy), (0.5 * cy) * (cy - 1.0)
        tab_ref[0, k] = 1.0 - ((near_x + far_x) + (near_y + far_y))
        tab_ref[1, k] = near_x
        tab_ref[2, k] = far_x
        tab_ref[3, k] = near_y
        tab_ref[4, k] = far_y


def land_halos(even_x, even_y, xe_ref, xo_ref, ye_ref, yo_ref, xh_ref, yh_ref):
    side = even_x.astype(jnp.int32)
    shape = (2, HALF, NF, LANES)
    xh_ref[side] = xe_ref[0:SPECTRA, :].astype(F32).reshape(shape)
    xh_ref[1 - side] = xo_ref[0:SPECTRA, :].astype(F32).reshape(shape)

    def rows(ref):
        return ref[SPECTRA : SPECTRA + OCEAN, :].astype(F32) + ref[SPECTRA + OCEAN : XROWS, :].astype(F32)

    a, b = rows(xe_ref), rows(xo_ref)
    left, right = jnp.where(even_x, b, a), jnp.where(even_x, a, b)
    side = 1 - even_y.astype(jnp.int32)
    shape = (HALF, 8, LANES)
    yh_ref[side] = ye_ref[0 : HALF * 8, :].astype(F32).reshape(shape)
    yh_ref[1 - side] = yo_ref[0 : HALF * 8, :].astype(F32).reshape(shape)

    def columns(ref):
        both = ref[HALF * 8 : YROWS, :].astype(F32)
        return both[0:8] + both[8:16]

    a, b = columns(ye_ref), columns(yo_ref)
    above, below = jnp.where(even_y, a, b), jnp.where(even_y, b, a)
    return left, right, below, above


def extend_ocean(o_ref, left, right, ext_ref):
    for c in range(3):
        for z in range(NZ):
            at = c * NZ + z
            ext_ref[c, 8 * z : 8 * z + 1, :] = left[at : at + 1]
            ext_ref[c, 8 * z + 1 : 8 * z + 5, :] = o_ref[c, z]
            ext_ref[c, 8 * z + 5 : 8 * z + 6, :] = right[at : at + 1]
            ext_ref[c, 8 * z + 6 : 8 * z + 8, :] = jnp.zeros((2, LANES), F32)


def neighbours(c, q, below, above, levels):
    lanes = lane_of(q.shape)
    low = jnp.concatenate([roll(below, -(c * NZ + z), 1) for z in range(levels)], 0)
    high = jnp.concatenate([roll(above, LANES - 1 - (c * NZ + z), 1) for z in range(levels)], 0)
    return (
        roll(q, 1, 0),
        roll(q, -1, 0),
        jnp.where(lanes == 0, low, roll(q, 1, 1)),
        jnp.where(lanes == LANES - 1, high, roll(q, -1, 1)),
    )


def refraction_rates(ext_ref, below, above, rate_ref):
    grads = []
    for c in range(2):
        xm, xp, ym, yp = neighbours(c, ext_ref[c, 0:8, :], below, above, 1)
        grads.append(((xp - xm) * 0.5, (yp - ym) * 0.5))
    (ux, uy), (vx, vy) = grads
    stretch = ux - vy
    for k in range(NDIR):
        c, s = float(COS[k]), float(SIN[k])
        rate_ref[k] = (TURN * c * s) * stretch + (TURN * s * s) * vx - (TURN * c * c) * uy


def advance_ocean(ext_ref, below, above, stress, wet8, out_ref):
    zonal, north, heat = (ext_ref[c] for c in range(3))
    wet = jnp.concatenate([wet8] * NZ, 0)

    def stencil(c, q):
        xm, xp, ym, yp = neighbours(c, q, below, above, NZ)
        return (xp - xm) * 0.5, (yp - ym) * 0.5, xp + xm + yp + ym - 4.0 * q

    _, _, zonal_lap = stencil(0, zonal)
    _, _, north_lap = stencil(1, north)
    heat_x, heat_y, heat_lap = stencil(2, heat)

    def running(v):
        total = v[0:8]
        sums = [total]
        for z in range(1, NZ):
            total = total + v[8 * z : 8 * z + 8]
            sums.append(total)
        return jnp.concatenate(sums, 0)

    rest = jnp.zeros((8 * (NZ - 1), LANES), F32)
    push_u = jnp.concatenate([stress[0:8], rest], 0)
    push_v = jnp.concatenate([stress[8:16], rest], 0)
    new = (
        wet * (zonal + CORIOLIS * north - PRESS * running(heat_x) + VISC * zonal_lap + push_u),
        wet * (north - CORIOLIS * zonal - PRESS * running(heat_y) + VISC * north_lap + push_v),
        heat + wet * (DIFFUSE * heat_lap - ADVECT * (zonal * heat_x + north * heat_y)),
    )
    for c in range(3):
        for z in range(NZ):
            out_ref[c, z] = new[c][8 * z + 1 : 8 * z + 5]
    return new


def stress_of(n_ref, weights_ref):
    total = jnp.zeros((16, LANES), F32)
    for x in range(ROWS):
        cells = n_ref[x].reshape(BINS, LANES).astype(BF16)
        total = total + jnp.dot(weights_ref[x], cells, preferred_element_type=F32)
    return total


def advance_waves(n_ref, xh_ref, yh_ref, rate_ref, wet, tab_ref, quarter, rows, emit):
    half = quarter // 2
    south = quarter in (1, 2)
    lanes = lane_of((NF, LANES))

    def body(j, carry):
        k = quarter * QUARTER + j
        below = jnp.where(k == 0, NDIR - 1, k - 1) if quarter == 0 else k - 1
        above = jnp.where(k == NDIR - 1, 0, k + 1) if quarter == 3 else k + 1
        kk = k - half * HALF
        edge = yh_ref[1, k - QUARTER] if south else yh_ref[0, k if quarter == 0 else k - HALF]
        weights = [tab_ref[t, k] for t in range(5)]

        def row(r):
            if r < 0:
                return xh_ref[0, r + 2, kk]
            return n_ref[r, k] if r < ROWS else xh_ref[1, r - ROWS, kk]

        results = []
        for x in rows:
            cell = n_ref[x, k]
            step = 1 if half else -1
            start = LANES - 2 if south else 0
            halo = jnp.concatenate(
                [roll(edge, start - (8 * g + 2 * x), 1) for g in range(4)], 0
            )
            if south:
                near_y = roll(jnp.where(lanes == LANES - 1, halo, cell), 1, 1)
                far_y = roll(jnp.where(lanes >= LANES - 2, halo, cell), 2, 1)
            else:
                near_y = roll(jnp.where(lanes == 0, halo, cell), -1, 1)
                far_y = roll(jnp.where(lanes < 2, halo, cell), -2, 1)
            rate = jnp.broadcast_to(rate_ref[k, x + 1 : x + 2, :], (NF, LANES))
            upwind = jnp.where(rate > 0.0, n_ref[x, below], n_ref[x, above])
            total = cell * weights[0] + row(x + step) * weights[1] + row(x + 2 * step) * weights[2]
            total = total + (near_y * weights[3] + far_y * weights[4])
            total = total + jnp.abs(rate) * (upwind - cell)
            results.append((x, total * wet[x]))
        emit(k, results)
        return carry

    lax.fori_loop(0, QUARTER, body, 0)


def wet_rows(mask_ref):
    wet = mask_ref[...].astype(F32)
    pad = jnp.zeros((1, LANES), F32)
    wet8 = jnp.concatenate([pad, wet, pad, pad, pad], 0)
    return [jnp.broadcast_to(wet[x : x + 1], (NF, LANES)) for x in range(ROWS)], wet8


def middle_kernel(n_ref, o_ref, mask_ref, tab_ref, w_ref, xe_in, xo_in, ye_in, yo_in,
                  new_ref, ocean_ref, xe_ref, xo_ref, ye_ref, yo_ref,
                  xh_ref, yh_ref, ext_ref, rate_ref, e_ref):
    lanes = lane_of((8, LANES))
    even_x, even_y = is_even("gx"), is_even("gy")
    wet, wet8 = wet_rows(mask_ref)
    left, right, below, above = land_halos(even_x, even_y, xe_in, xo_in, ye_in, yo_in, xh_ref, yh_ref)
    extend_ocean(o_ref, left, right, ext_ref)
    refraction_rates(ext_ref, below, above, rate_ref)
    for quarter in range(4):
        south = quarter in (1, 2)
        shift = QUARTER if south else (0 if quarter == 0 else HALF)

        def emit(k, results, south=south, shift=shift):
            cells = [v.astype(BF16).astype(F32) for _, v in results]
            for x, cell in enumerate(cells):
                new_ref[x, k] = cell
            pack_y_edges(cells, k - shift, south, e_ref.at[1 if south else 0], lanes)

        advance_waves(n_ref, xh_ref, yh_ref, rate_ref, wet, tab_ref, quarter, range(ROWS), emit)
    new = advance_ocean(ext_ref, below, above, stress_of(n_ref, w_ref), wet8, ocean_ref)
    rows = tuple(
        jnp.concatenate([new[c][8 * z + r : 8 * z + r + 1] for c in range(3) for z in range(NZ)], 0)
        for r in (1, ROWS)
    )
    send_x(new_ref, rows, xe_ref, jnp.logical_not(even_x))
    send_x(new_ref, rows, xo_ref, even_x)
    first, last = pack_ocean_columns(new, lanes)
    send_y(e_ref, first, last, even_y, (ye_ref, yo_ref))


def last_kernel(n_ref, o_ref, mask_ref, tab_ref, w_ref, xe_in, xo_in, ye_in, yo_in,
                out_ref, ocean_ref, xh_ref, yh_ref, ext_ref, rate_ref, t_ref):
    even_x, even_y = is_even("gx"), is_even("gy")
    wet, wet8 = wet_rows(mask_ref)
    left, right, below, above = land_halos(even_x, even_y, xe_in, xo_in, ye_in, yo_in, xh_ref, yh_ref)
    extend_ocean(o_ref, left, right, ext_ref)
    refraction_rates(ext_ref, below, above, rate_ref)

    def emit(k, results):
        for x, cell in results:
            t_ref[x, pl.ds(k, NF, stride=NDIR), :] = cell

    for quarter in range(4):
        advance_waves(n_ref, xh_ref, yh_ref, rate_ref, wet, tab_ref, quarter, range(ROWS), emit)
    advance_ocean(ext_ref, below, above, stress_of(n_ref, w_ref), wet8, ocean_ref)
    for x in range(ROWS):
        out_ref[x] = jnp.transpose(t_ref[x]).astype(BF16)


def swap_pairs(axis, odd):
    size = lax.axis_size(axis)
    pairs = []
    for i in range(odd, size - 1, 2):
        pairs += [(i, i + 1), (i + 1, i)]
    return pairs


def exchange(xe, xo, ye, yo):
    xo = lax.ppermute(xo, "gx", swap_pairs("gx", 1))
    xe = lax.ppermute(xe, "gx", swap_pairs("gx", 0))
    ye = lax.ppermute(ye, "gy", swap_pairs("gy", 0))
    yo = lax.ppermute(yo, "gy", swap_pairs("gy", 1))
    return xe, xo, ye, yo


def shapes(*wanted):
    return [jax.ShapeDtypeStruct(shape, dtype) for shape, dtype in wanted]


EDGES = (((XROWS, LANES), BF16), ((XROWS, LANES), BF16), ((YROWS, LANES), BF16), ((YROWS, LANES), BF16))
GRID = ((ROWS, NDIR, NF, LANES), F32)
SCRATCH = [
    pltpu.VMEM((2, 2, HALF, NF, LANES), F32),
    pltpu.VMEM((2, HALF, 8, LANES), F32),
    pltpu.VMEM((3, 8 * NZ, LANES), F32),
    pltpu.VMEM((NDIR, 8, LANES), F32),
]


def local(spectrum, ocean_state, sea_mask):
    ocean_shape = (ocean_state.shape, F32)
    n, *edges = pl.pallas_call(
        start_kernel,
        out_shape=shapes(GRID, *EDGES),
        in_specs=[VM] * 3,
        out_specs=[VM] * 5,
        scratch_shapes=[pltpu.VMEM((ROWS, BINS, LANES), F32), pltpu.VMEM((2, HALF, 8, LANES), F32)],
        compiler_params=PARAMS,
        name="start",
    )(spectrum, ocean_state, sea_mask)
    speed = jnp.asarray(np.broadcast_to(SPEEDS[:, None], (NF, LANES)))
    weights = jnp.asarray(stress_table(), dtype=BF16)
    tab = pl.pallas_call(
        tables_kernel,
        out_shape=shapes(((5, NDIR, NF, LANES), F32))[0],
        in_specs=[VM],
        out_specs=VM,
        compiler_params=PARAMS,
        name="tables",
    )(speed)
    edges = exchange(*edges)
    n, ocean, *edges = pl.pallas_call(
        middle_kernel,
        out_shape=shapes(GRID, ocean_shape, *EDGES),
        in_specs=[VM] * 9,
        out_specs=[VM] * 6,
        scratch_shapes=SCRATCH + [pltpu.VMEM((2, HALF, 8, LANES), F32)],
        compiler_params=PARAMS,
        name="middle",
    )(n, ocean_state, sea_mask, tab, weights, *edges)
    edges = exchange(*edges)
    return pl.pallas_call(
        last_kernel,
        out_shape=shapes((spectrum.shape, BF16), ocean_shape),
        in_specs=[VM] * 9,
        out_specs=[VM] * 2,
        scratch_shapes=SCRATCH + [pltpu.VMEM((ROWS, BINS, LANES), F32)],
        compiler_params=PARAMS,
        name="last",
    )(n, ocean, sea_mask, tab, weights, *edges)


def solution(mesh):
    placed = (P("gx", "gy", None), P(None, None, "gx", "gy"), P("gx", "gy"))
    return jax.shard_map(
        local,
        mesh=mesh,
        in_specs=placed,
        out_specs=(P("gx", "gy", None), P(None, None, "gx", "gy")),
        check_vma=False,
    )
```

time: 102 us -> 56.2 us (0.55)
  the two profiles are of different devices: /device:TPU:22 before, /device:TPU:1 now
where the time goes in v1:
time: 56.2 us; the launch traced here: 55.9 us
  Pallas kernels  26.2 us (47%)
  starting transfers between devices  13.9 us (25%)
  waiting for transfers between devices  8.49 us (15%)
  local copies, waits for them, and re-layouts  6.61 us (12%)
  between operations  0.73 us (1%)
    pallas_call x1, Pallas kernels, local(): pl.pallas_call(middle_kernel, out_shape=shapes(GRID, ocean_shape, *EDGES)...  12.1 us
    pallas_call x1, Pallas kernels, local(): pl.pallas_call(last_kernel, out_shape=shapes((spectrum.shape, BF16), ocea...  10 us
    ppermute x2, starting transfers between devices, exchange(): xo = lax.ppermute(xo, 'gx', swap_pairs('gx', 1))  9.73 us
    ppermute x2, waiting for transfers between devices, exchange(): xo = lax.ppermute(xo, 'gx', swap_pairs('gx', 1))  7.58 us
    unnamed x16, local copies, waits for them, and re-layouts  5.88 us
    pallas_call x1, Pallas kernels, local(): pl.pallas_call(start_kernel, out_shape=shapes(GRID, *EDGES), in_specs=[VM...  3.87 us
    ppermute x2, starting transfers between devices, exchange(): ye = lax.ppermute(ye, 'gy', swap_pairs('gy', 0))  2.72 us
    ppermute x2, starting transfers between devices, exchange(): yo = lax.ppermute(yo, 'gy', swap_pairs('gy', 1))  1.3 us
  transfers between devices with their start and end apart: 8, of which 3 were waited for; matrix products, arithmetic and copies ran while one was open for 1% of the time, Pallas kernels for 0%

profile of v1, /device:TPU:1, one launch (start us, length us, event | category | flops | bytes accessed | tf_op | source)
XLA Modules:
  0.0 55.9 jit_solution(14479636642251819994)
XLA Ops:
  0.6 0.0 copy-start.2
  0.6 1.3 %copy-done.2 = bf16[4,128,1152]{2,1,0:T(8,128)(2,1)S(1)} copy-done((bf16[4,128,1152]{2,1,0:T(8,128)(2,1)S(1)}, bf16[4,128,1152]{2,1,0:T(8,128)(2,1)}, u32[]{:S(2)}) %copy-start.2) | copy-done | bytes 1179672
  1.9 0.9 %copy-done.4 = f32[3,16,4,128]{3,2,1,0:T(4,128)S(1)} copy-done((f32[3,16,4,128]{3,2,1,0:T(4,128)S(1)}, f32[3,16,4,128]{3,2,1,0:T(4,128)}, u32[]{:S(2)}) %copy-start.4) | copy-done | bytes 98328
  2.8 0.7 %copy-done.6 = s32[4,128]{1,0:T(4,128)S(1)} copy-done((s32[4,128]{1,0:T(4,128)S(1)}, s32[4,128]{1,0:T(4,128)}, u32[]{:S(2)}) %copy-start.6) | copy-done | bytes 2072
  3.5 3.9 %start.1 = (f32[4,36,32,128]{3,2,1,0:T(8,128)S(1)}, bf16[1248,128]{1,0:T(8,128)(2,1)S(1)}, bf16[1248,128]{1,0:T(8,128)(2,1)S(1)}, bf16[160,128]{1,0:T(8,128)(2,1)S(1)}, bf16[160,128]{1,0:T(8,128)(2,1)S(1)}) custom-call(bf16[4,128,1152]{2,1,0:T(8,128)(2,1)S(1)} %copy-done.2, f32[3,16,4,128]{3,2,1,0:T(4,128)S(1)} %copy-done.4, s32[4,128]{1,0:T(4,128)S(1)} %copy-done.6), custom_call_target="tpu_custom_call" | custom-call | tf_op jit(solution)/shard_map/start/pallas_call | solution.py:400
  7.4 0.0 copy-start.1
  7.4 1.4 %copy-done.1 = f32[4,36,32,128]{3,2,1,0:T(8,128)} copy-done((f32[4,36,32,128]{3,2,1,0:T(8,128)}, f32[4,36,32,128]{3,2,1,0:T(8,128)S(1)}, u32[]{:S(2)}) %copy-start.1) | copy-done | bytes 2359320
  8.8 0.1 collective-permute-start
  8.9 4.4 %collective-permute-start.1 = (bf16[1248,128]{1,0:T(8,128)(2,1)S(1)}, bf16[1248,128]{1,0:T(8,128)(2,1)S(1)}, u32[]{:S(2)}, u32[]{:S(2)}) collective-permute-start(bf16[1248,128]{1,0:T(8,128)(2,1)S(1)} %get-tuple-element.15), channel_id=1, source_target_pairs={{4,8},{8,4},{12,16},{16,12},{20,24},{24,20},{5,9},{9,5},{13,17},{1... | collective-permute-start | bytes 958472 | tf_op jit(solution)/shard_map/ppermute | solution.py:377
  13.3 1.4 %collective-permute-start.2 = (bf16[160,128]{1,0:T(8,128)(2,1)S(1)}, bf16[160,128]{1,0:T(8,128)(2,1)S(1)}, u32[]{:S(2)}, u32[]{:S(2)}) collective-permute-start(bf16[160,128]{1,0:T(8,128)(2,1)S(1)} %get-tuple-element.16), channel_id=1, source_target_pairs={{0,1},{1,0},{2,3},{3,2},{4,5},{5,4},{6,7},{7,6},{8,9},{9,8},{10,11... | collective-permute-start | bytes 122888 | tf_op jit(solution)/shard_map/ppermute | solution.py:379
  14.7 0.7 %collective-permute-start.3 = (bf16[160,128]{1,0:T(8,128)(2,1)S(1)}, bf16[160,128]{1,0:T(8,128)(2,1)S(1)}, u32[]{:S(2)}, u32[]{:S(2)}) collective-permute-start(bf16[160,128]{1,0:T(8,128)(2,1)S(1)} %get-tuple-element.17), channel_id=1, source_target_pairs={{1,2},{2,1},{5,6},{6,5},{9,10},{10,9},{13,14},{14,13},{17,18},{18,... | collective-permute-start | bytes 122888 | tf_op jit(solution)/shard_map/ppermute | solution.py:380
  15.3 0.7 %jit_solution_.3.speed_ref = f32[32,128]{1,0:T(8,128)S(1)} broadcast(f32[32]{0:T(128)} %constant.4.clone), dimensions={0} | broadcast | bytes 16512 | tf_op jit(solution)
  16.1 0.2 tables.1.tab_ref
  16.3 0.0 copy-start
  16.3 1.6 %copy-done = f32[5,36,32,128]{3,2,1,0:T(8,128)} copy-done((f32[5,36,32,128]{3,2,1,0:T(8,128)}, f32[5,36,32,128]{3,2,1,0:T(8,128)S(1)}, u32[]{:S(2)}) %copy-start) | copy-done | bytes 2949144
  17.9 0.0 collective-permute-done.2.ye_in
  17.9 0.0 collective-permute-done.3.yo_in
  17.9 0.0 collective-permute-done.xe_in
  17.9 2.6 %collective-permute-done.1.xo_in = bf16[1248,128]{1,0:T(8,128)(2,1)S(1)} collective-permute-done((bf16[1248,128]{1,0:T(8,128)(2,1)S(1)}, bf16[1248,128]{1,0:T(8,128)(2,1)S(1)}, u32[]{:S(2)}, u32[]{:S(2)}) %collective-permute-start.1) | collective-permute-done | bytes 319520 | tf_op jit(solution)/shard_map/ppermute | solution.py:377
  20.5 0.0 copy-done.3
  20.5 0.0 copy-done.5
  20.5 0.0 copy-done.7
  20.5 12.1 %middle.1 = (f32[4,36,32,128]{3,2,1,0:T(8,128)S(1)}, f32[3,16,4,128]{3,2,1,0:T(4,128)S(1)}, bf16[1248,128]{1,0:T(8,128)(2,1)S(1)}, bf16[1248,128]{1,0:T(8,128)(2...) custom-call(f32[4,36,32,128]{3,2,1,0:T(8,128)} %copy-done.1, f32[3,16,4,128]{3,2,1,0:T(4,128)S(1)} %copy-done.5, ...), custom_call_target="tpu_custom_call" | custom-call | tf_op jit(solution)/shard_map/middle/pallas_call | solution.py:420
  32.6 0.1 collective-permute-start.4
  32.7 5.3 %collective-permute-start.5 = (bf16[1248,128]{1,0:T(8,128)(2,1)S(1)}, bf16[1248,128]{1,0:T(8,128)(2,1)S(1)}, u32[]{:S(2)}, u32[]{:S(2)}) collective-permute-start(bf16[1248,128]{1,0:T(8,128)(2,1)S(1)} %get-tuple-element.21), channel_id=1, source_target_pairs={{4,8},{8,4},{12,16},{16,12},{20,24},{24,20},{5,9},{9,5},{13,17},{1... | collective-permute-start | bytes 958472 | tf_op jit(solution)/shard_map/ppermute | solution.py:377
  38.0 1.4 %collective-permute-start.6 = (bf16[160,128]{1,0:T(8,128)(2,1)S(1)}, bf16[160,128]{1,0:T(8,128)(2,1)S(1)}, u32[]{:S(2)}, u32[]{:S(2)}) collective-permute-start(bf16[160,128]{1,0:T(8,128)(2,1)S(1)} %get-tuple-element.22), channel_id=1, source_target_pairs={{0,1},{1,0},{2,3},{3,2},{4,5},{5,4},{6,7},{7,6},{8,9},{9,8},{10,11... | collective-permute-start | bytes 122888 | tf_op jit(solution)/shard_map/ppermute | solution.py:379
  39.3 0.7 %collective-permute-start.7 = (bf16[160,128]{1,0:T(8,128)(2,1)S(1)}, bf16[160,128]{1,0:T(8,128)(2,1)S(1)}, u32[]{:S(2)}, u32[]{:S(2)}) collective-permute-start(bf16[160,128]{1,0:T(8,128)(2,1)S(1)} %get-tuple-element.23), channel_id=1, source_target_pairs={{1,2},{2,1},{5,6},{6,5},{9,10},{10,9},{13,14},{14,13},{17,18},{18,... | collective-permute-start | bytes 122888 | tf_op jit(solution)/shard_map/ppermute | solution.py:380
  40.0 0.9 %collective-permute-done.6.ye_in = bf16[160,128]{1,0:T(8,128)(2,1)S(1)} collective-permute-done((bf16[160,128]{1,0:T(8,128)(2,1)S(1)}, bf16[160,128]{1,0:T(8,128)(2,1)S(1)}, u32[]{:S(2)}, u32[]{:S(2)}) %collective-permute-start.6) | collective-permute-done | bytes 40992 | tf_op jit(solution)/shard_map/ppermute | solution.py:379
  40.9 0.0 collective-permute-done.7.yo_in
  40.9 0.0 collective-permute-done.4.xe_in
  40.9 5.0 %collective-permute-done.5.xo_in = bf16[1248,128]{1,0:T(8,128)(2,1)S(1)} collective-permute-done((bf16[1248,128]{1,0:T(8,128)(2,1)S(1)}, bf16[1248,128]{1,0:T(8,128)(2,1)S(1)}, u32[]{:S(2)}, u32[]{:S(2)}) %collective-permute-start.5) | collective-permute-done | bytes 319520 | tf_op jit(solution)/shard_map/ppermute | solution.py:377
  45.9 10.0 %last.1 = (bf16[4,128,1152]{2,1,0:T(8,128)(2,1)}, f32[3,16,4,128]{3,2,1,0:T(4,128)}) custom-call(f32[4,36,32,128]{3,2,1,0:T(8,128)S(1)} %get-tuple-element.18.n_ref, f32[3,16,4,128]{3,2,1,0:T(4,128)S(1)} %get-tuple-element.19.o_ref, s32[4,128]{1,0:T(4,128)S(1)} %copy-done.7, f32[5,36,32,128]{3,2,1,0:T(8,128)} %copy-done, bf16[4,16,1152]{2,1,0:T(8,128)(2,1)S(1)} %copy-done.3, ...), custom_call_target="tpu_custom_call" | custom-call | tf_op jit(solution)/shard_map/last/pallas_call | solution.py:430
  (5 shorter events, 0.0 us)
Async XLA Ops:
  0.6 1.3 %copy-start.2 = (bf16[4,128,1152]{2,1,0:T(8,128)(2,1)S(1)}, bf16[4,128,1152]{2,1,0:T(8,128)(2,1)}, u32[]{:S(2)}) copy-start(bf16[4,128,1152]{2,1,0:T(8,128)(2,1)} %s_ref.1) | copy-start | bytes 3538948
  1.9 0.9 %copy-start.4 = (f32[3,16,4,128]{3,2,1,0:T(4,128)S(1)}, f32[3,16,4,128]{3,2,1,0:T(4,128)}, u32[]{:S(2)}) copy-start(f32[3,16,4,128]{3,2,1,0:T(4,128)} %o_ref.3) | copy-start | bytes 294916
  2.8 0.7 %copy-start.6 = (s32[4,128]{1,0:T(4,128)S(1)}, s32[4,128]{1,0:T(4,128)}, u32[]{:S(2)}) copy-start(s32[4,128]{1,0:T(4,128)} %mask_ref.5) | copy-start | bytes 6148
  3.5 17.0 %copy-start.3 = (bf16[4,16,1152]{2,1,0:T(8,128)(2,1)S(1)}, bf16[4,16,1152]{2,1,0:T(8,128)(2,1)}, u32[]{:S(2)}) copy-start(bf16[4,16,1152]{2,1,0:T(8,128)(2,1)} %constant.5.clone.w_ref) | copy-start | bytes 442372
  3.5 17.0 %copy-start.5 = (f32[3,16,4,128]{3,2,1,0:T(4,128)S(1)}, f32[3,16,4,128]{3,2,1,0:T(4,128)}, u32[]{:S(2)}) copy-start(f32[3,16,4,128]{3,2,1,0:T(4,128)} %o_ref.3) | copy-start | bytes 294916
  3.5 17.0 %copy-start.7 = (s32[4,128]{1,0:T(4,128)S(1)}, s32[4,128]{1,0:T(4,128)}, u32[]{:S(2)}) copy-start(s32[4,128]{1,0:T(4,128)} %mask_ref.5) | copy-start | bytes 6148
  7.4 1.5 %copy-start.1 = (f32[4,36,32,128]{3,2,1,0:T(8,128)}, f32[4,36,32,128]{3,2,1,0:T(8,128)S(1)}, u32[]{:S(2)}) copy-start(f32[4,36,32,128]{3,2,1,0:T(8,128)S(1)} %get-tuple-element.13.n_ref) | copy-start | bytes 7077892
  8.8 9.1 %collective-permute-start = (bf16[1248,128]{1,0:T(8,128)(2,1)S(1)}, bf16[1248,128]{1,0:T(8,128)(2,1)S(1)}, u32[]{:S(2)}, u32[]{:S(2)}) collective-permute-start(bf16[1248,128]{1,0:T(8,128)(2,1)S(1)} %get-tuple-element.14), channel_id=1, source_target_pairs={{0,4},{4,0},{8,12},{12,8},{16,20},{20,16},{24,28},{28,24},{1,5},{5... | collective-permute-start | bytes 958472 | tf_op jit(solution)/shard_map/ppermute | solution.py:378
  8.9 11.6 %collective-permute-start.1 = (bf16[1248,128]{1,0:T(8,128)(2,1)S(1)}, bf16[1248,128]{1,0:T(8,128)(2,1)S(1)}, u32[]{:S(2)}, u32[]{:S(2)}) collective-permute-start(bf16[1248,128]{1,0:T(8,128)(2,1)S(1)} %get-tuple-element.15), channel_id=1, source_target_pairs={{4,8},{8,4},{12,16},{16,12},{20,24},{24,20},{5,9},{9,5},{13,17},{1... | collective-permute-start | bytes 958472 | tf_op jit(solution)/shard_map/ppermute | solution.py:377
  13.3 4.6 %collective-permute-start.2 = (bf16[160,128]{1,0:T(8,128)(2,1)S(1)}, bf16[160,128]{1,0:T(8,128)(2,1)S(1)}, u32[]{:S(2)}, u32[]{:S(2)}) collective-permute-start(bf16[160,128]{1,0:T(8,128)(2,1)S(1)} %get-tuple-element.16), channel_id=1, source_target_pairs={{0,1},{1,0},{2,3},{3,2},{4,5},{5,4},{6,7},{7,6},{8,9},{9,8},{10,11... | collective-permute-start | bytes 122888 | tf_op jit(solution)/shard_map/ppermute | solution.py:379
  14.7 3.2 %collective-permute-start.3 = (bf16[160,128]{1,0:T(8,128)(2,1)S(1)}, bf16[160,128]{1,0:T(8,128)(2,1)S(1)}, u32[]{:S(2)}, u32[]{:S(2)}) collective-permute-start(bf16[160,128]{1,0:T(8,128)(2,1)S(1)} %get-tuple-element.17), channel_id=1, source_target_pairs={{1,2},{2,1},{5,6},{6,5},{9,10},{10,9},{13,14},{14,13},{17,18},{18,... | collective-permute-start | bytes 122888 | tf_op jit(solution)/shard_map/ppermute | solution.py:380
  16.3 1.6 %copy-start = (f32[5,36,32,128]{3,2,1,0:T(8,128)}, f32[5,36,32,128]{3,2,1,0:T(8,128)S(1)}, u32[]{:S(2)}) copy-start(f32[5,36,32,128]{3,2,1,0:T(8,128)S(1)} %tables.1.tab_ref) | copy-start | bytes 8847364
  32.6 8.3 %collective-permute-start.4 = (bf16[1248,128]{1,0:T(8,128)(2,1)S(1)}, bf16[1248,128]{1,0:T(8,128)(2,1)S(1)}, u32[]{:S(2)}, u32[]{:S(2)}) collective-permute-start(bf16[1248,128]{1,0:T(8,128)(2,1)S(1)} %get-tuple-element.20), channel_id=1, source_target_pairs={{0,4},{4,0},{8,12},{12,8},{16,20},{20,16},{24,28},{28,24},{1,5},{5... | collective-permute-start | bytes 958472 | tf_op jit(solution)/shard_map/ppermute | solution.py:378
  32.7 13.2 %collective-permute-start.5 = (bf16[1248,128]{1,0:T(8,128)(2,1)S(1)}, bf16[1248,128]{1,0:T(8,128)(2,1)S(1)}, u32[]{:S(2)}, u32[]{:S(2)}) collective-permute-start(bf16[1248,128]{1,0:T(8,128)(2,1)S(1)} %get-tuple-element.21), channel_id=1, source_target_pairs={{4,8},{8,4},{12,16},{16,12},{20,24},{24,20},{5,9},{9,5},{13,17},{1... | collective-permute-start | bytes 958472 | tf_op jit(solution)/shard_map/ppermute | solution.py:377
  38.0 2.9 %collective-permute-start.6 = (bf16[160,128]{1,0:T(8,128)(2,1)S(1)}, bf16[160,128]{1,0:T(8,128)(2,1)S(1)}, u32[]{:S(2)}, u32[]{:S(2)}) collective-permute-start(bf16[160,128]{1,0:T(8,128)(2,1)S(1)} %get-tuple-element.22), channel_id=1, source_target_pairs={{0,1},{1,0},{2,3},{3,2},{4,5},{5,4},{6,7},{7,6},{8,9},{9,8},{10,11... | collective-permute-start | bytes 122888 | tf_op jit(solution)/shard_map/ppermute | solution.py:379
  39.3 1.6 %collective-permute-start.7 = (bf16[160,128]{1,0:T(8,128)(2,1)S(1)}, bf16[160,128]{1,0:T(8,128)(2,1)S(1)}, u32[]{:S(2)}, u32[]{:S(2)}) collective-permute-start(bf16[160,128]{1,0:T(8,128)(2,1)S(1)} %get-tuple-element.23), channel_id=1, source_target_pairs={{1,2},{2,1},{5,6},{6,5},{9,10},{10,9},{13,14},{14,13},{17,18},{18,... | collective-permute-start | bytes 122888 | tf_op jit(solution)/shard_map/ppermute | solution.py:380

commit v2 on v1

--- a/solution.py
+++ b/solution.py
@@ -30,7 +30,7 @@
 F32 = jnp.float32
 BF16 = jnp.bfloat16
 VM = pl.BlockSpec(memory_space=pltpu.VMEM)
-PARAMS = pltpu.CompilerParams(vmem_limit_bytes=48 * 1024 * 1024)
+PARAMS = pltpu.CompilerParams(vmem_limit_bytes=16 * 1024 * 1024)
 
 SPECTRA = 2 * HALF * NF
 OCEAN = 3 * NZ
@@ -71,15 +71,47 @@
     return lax.broadcasted_iota(jnp.int32, shape, len(shape) - 1)
 
 
-def pack_y_edges(cells, k, south, out_ref, lanes):
-    start = LANES - 2 if south else 0
-    packed = jnp.zeros((8, LANES), F32)
-    for x in range(ROWS):
-        for g in range(4):
-            at = 8 * g + 2 * x
-            moved = roll(cells[x][8 * g : 8 * g + 8], at - start, 1)
-            packed = jnp.where((lanes >= at) & (lanes < at + 2), moved, packed)
-    out_ref[k] = packed
+def edge_tables():
+    table = np.zeros((2, ROWS, LANES, LANES), np.float32)
+    for side, start in enumerate((0, LANES - 2)):
+        for x in range(ROWS):
+            for g in range(4):
+                for j in range(2):
+                    table[side, x, start + j, 8 * g + 2 * x + j] = 1.0
+    return table.reshape(2, ROWS * LANES, LANES)
+
+
+def shift_tables():
+    table = np.zeros((2, ROWS, 2 * LANES, 2 * LANES), np.float32)
+    for side, sign in enumerate((1, -1)):
+        for x in range(ROWS):
+            for far in range(2):
+                for lane in range(LANES):
+                    source = lane + sign * (1 + far)
+                    if 0 <= source < LANES:
+                        table[side, x, source, far * LANES + lane] = 1.0
+                    else:
+                        j = source - LANES if sign > 0 else source + 2
+                        for g in range(4):
+                            table[side, x, LANES + 8 * g + 2 * x + j, far * LANES + lane] = 1.0
+    return table
+
+
+def pack_y_edges(n_ref, quarter, tables_ref, out_ref):
+    south = quarter in (1, 2)
+    first = quarter * QUARTER
+    rows = [
+        n_ref[x, first : first + QUARTER].reshape(QUARTER * NF, LANES).astype(BF16) for x in range(ROWS)
+    ]
+    found = jnp.dot(
+        jnp.concatenate(rows, 1), tables_ref[1 if south else 0], preferred_element_type=F32
+    ).reshape(QUARTER, 4, 8, LANES)
+    group = lane_of((QUARTER, 8, LANES)) // 8
+    packed = found[:, 0]
+    for g in range(1, 4):
+        packed = jnp.where(group == g, found[:, g], packed)
+    at = 0 if quarter < 2 else QUARTER
+    out_ref[1 if south else 0, at : at + QUARTER] = packed
 
 
 def pack_ocean_columns(blocks, lanes):
@@ -114,31 +146,36 @@
         out_ref[HALF * 8 : YROWS, :] = jnp.concatenate([whole, rest], 0).astype(BF16)
 
 
-def start_kernel(s_ref, o_ref, mask_ref, n_ref, xe_ref, xo_ref, ye_ref, yo_ref, t_ref, e_ref):
-    lanes = lane_of((8, LANES))
+def start_kernel(s_hbm, o_hbm, mask_hbm, edge_hbm, n_ref, xe_ref, xo_ref, ye_ref, yo_ref,
+                 s_ref, o_ref, mask_ref, edge_ref, t_ref, e_ref, sems):
+    copies = [pltpu.make_async_copy(mask_hbm, mask_ref, sems.at[ROWS])]
+    copies += [pltpu.make_async_copy(s_hbm.at[x], s_ref.at[x], sems.at[x]) for x in range(ROWS)]
+    copies += [
+        pltpu.make_async_copy(o_hbm, o_ref, sems.at[ROWS + 1]),
+        pltpu.make_async_copy(edge_hbm, edge_ref, sems.at[ROWS + 2]),
+    ]
+    for copy in copies:
+        copy.start()
+    copies[0].wait()
     wet = mask_ref[...].astype(F32)
     for x in range(ROWS):
+        copies[1 + x].wait()
         t_ref[x] = jnp.transpose(s_ref[x].astype(F32))
 
-    def pack(south, shift):
-        def body(k, carry):
-            cells = []
-            for x in range(ROWS):
-                cell = t_ref[x, pl.ds(k, NF, stride=NDIR), :] * wet[x : x + 1]
-                n_ref[x, k] = cell
-                cells.append(cell)
-            pack_y_edges(cells, k - shift, south, e_ref.at[1 if south else 0], lanes)
-            return carry
-
-        return body
-
-    lax.fori_loop(0, QUARTER, pack(False, 0), 0)
-    lax.fori_loop(QUARTER, 3 * QUARTER, pack(True, QUARTER), 0)
-    lax.fori_loop(3 * QUARTER, NDIR, pack(False, HALF), 0)
+    def body(k, carry):
+        for x in range(ROWS):
+            n_ref[x, k] = t_ref[x, pl.ds(k, NF, stride=NDIR), :] * wet[x : x + 1]
+        return carry
+
+    lax.fori_loop(0, NDIR, body, 0, unroll=2)
     even_x, even_y = is_even("gx"), is_even("gy")
+    copies[-2].wait()
     rows = tuple(o_ref[:, :, r, :].reshape(OCEAN, LANES) for r in (0, ROWS - 1))
     send_x(n_ref, rows, xe_ref, jnp.logical_not(even_x))
     send_x(n_ref, rows, xo_ref, even_x)
+    copies[-1].wait()
+    for quarter in range(4):
+        pack_y_edges(n_ref, quarter, edge_ref, e_ref)
     pad = jnp.zeros((1, LANES), F32)
     blocks = [
         jnp.concatenate(
@@ -146,7 +183,7 @@
         )
         for c in range(3)
     ]
-    first, last = pack_ocean_columns(blocks, lanes)
+    first, last = pack_ocean_columns(blocks, lane_of((8, LANES)))
     send_y(e_ref, first, last, even_y, (ye_ref, yo_ref))
 
 
@@ -174,10 +211,14 @@
 
     a, b = rows(xe_ref), rows(xo_ref)
     left, right = jnp.where(even_x, b, a), jnp.where(even_x, a, b)
-    side = 1 - even_y.astype(jnp.int32)
     shape = (HALF, 8, LANES)
-    yh_ref[side] = ye_ref[0 : HALF * 8, :].astype(F32).reshape(shape)
-    yh_ref[1 - side] = yo_ref[0 : HALF * 8, :].astype(F32).reshape(shape)
+    a = ye_ref[0 : HALF * 8, :].astype(F32)
+    b = yo_ref[0 : HALF * 8, :].astype(F32)
+    group = lane_of(shape) // 8
+    for to, pair in ((0, (a, b)), (1, (b, a))):
+        edge = jnp.where(even_y, *pair).reshape(shape)
+        parts = [jnp.where(group == g, edge, 0.0)[:, None] for g in range(4)]
+        yh_ref[to] = jnp.concatenate(parts, 1).reshape(HALF * NF, LANES).astype(BF16)
 
     def columns(ref):
         both = ref[HALF * 8 : YROWS, :].astype(F32)
@@ -264,18 +305,25 @@
     return total
 
 
-def advance_waves(n_ref, xh_ref, yh_ref, rate_ref, wet, tab_ref, quarter, rows, emit):
+def advance_waves(n_ref, xh_ref, yh_ref, rate_ref, wet, tab_ref, shift_ref, ys_ref, quarter, rows, emit):
     half = quarter // 2
-    south = quarter in (1, 2)
-    lanes = lane_of((NF, LANES))
+    side = 1 if quarter in (1, 2) else 0
+    size = QUARTER * NF
+    first = quarter * QUARTER
+    edges = yh_ref[side, 0:size, :] if quarter < 2 else yh_ref[side, size : 2 * size, :]
+    for x in rows:
+        cells = n_ref[x, first : first + QUARTER].reshape(size, LANES).astype(BF16)
+        ys_ref[x] = jnp.dot(
+            jnp.concatenate([cells, edges], 1), shift_ref[side, x], preferred_element_type=F32
+        )
 
     def body(j, carry):
-        k = quarter * QUARTER + j
+        k = first + j
         below = jnp.where(k == 0, NDIR - 1, k - 1) if quarter == 0 else k - 1
         above = jnp.where(k == NDIR - 1, 0, k + 1) if quarter == 3 else k + 1
         kk = k - half * HALF
-        edge = yh_ref[1, k - QUARTER] if south else yh_ref[0, k if quarter == 0 else k - HALF]
         weights = [tab_ref[t, k] for t in range(5)]
+        at = pl.ds(pl.multiple_of(j * NF, NF), NF)
 
         def row(r):
             if r < 0:
@@ -286,16 +334,7 @@
         for x in rows:
             cell = n_ref[x, k]
             step = 1 if half else -1
-            start = LANES - 2 if south else 0
-            halo = jnp.concatenate(
-                [roll(edge, start - (8 * g + 2 * x), 1) for g in range(4)], 0
-            )
-            if south:
-                near_y = roll(jnp.where(lanes == LANES - 1, halo, cell), 1, 1)
-                far_y = roll(jnp.where(lanes >= LANES - 2, halo, cell), 2, 1)
-            else:
-                near_y = roll(jnp.where(lanes == 0, halo, cell), -1, 1)
-                far_y = roll(jnp.where(lanes < 2, halo, cell), -2, 1)
+            near_y, far_y = ys_ref[x, at, 0:LANES], ys_ref[x, at, LANES : 2 * LANES]
             rate = jnp.broadcast_to(rate_ref[k, x + 1 : x + 2, :], (NF, LANES))
             upwind = jnp.where(rate > 0.0, n_ref[x, below], n_ref[x, above])
             total = cell * weights[0] + row(x + step) * weights[1] + row(x + 2 * step) * weights[2]
@@ -315,26 +354,22 @@
     return [jnp.broadcast_to(wet[x : x + 1], (NF, LANES)) for x in range(ROWS)], wet8
 
 
-def middle_kernel(n_ref, o_ref, mask_ref, tab_ref, w_ref, xe_in, xo_in, ye_in, yo_in,
+def middle_kernel(n_ref, o_ref, mask_ref, tab_ref, w_ref, shift_ref, edge_ref, xe_in, xo_in, ye_in, yo_in,
                   new_ref, ocean_ref, xe_ref, xo_ref, ye_ref, yo_ref,
-                  xh_ref, yh_ref, ext_ref, rate_ref, e_ref):
+                  xh_ref, yh_ref, ext_ref, rate_ref, ys_ref, e_ref):
     lanes = lane_of((8, LANES))
     even_x, even_y = is_even("gx"), is_even("gy")
     wet, wet8 = wet_rows(mask_ref)
     left, right, below, above = land_halos(even_x, even_y, xe_in, xo_in, ye_in, yo_in, xh_ref, yh_ref)
     extend_ocean(o_ref, left, right, ext_ref)
     refraction_rates(ext_ref, below, above, rate_ref)
+    def emit(k, results):
+        for x, cell in results:
+            new_ref[x, k] = cell.astype(BF16).astype(F32)
+
     for quarter in range(4):
-        south = quarter in (1, 2)
-        shift = QUARTER if south else (0 if quarter == 0 else HALF)
-
-        def emit(k, results, south=south, shift=shift):
-            cells = [v.astype(BF16).astype(F32) for _, v in results]
-            for x, cell in enumerate(cells):
-                new_ref[x, k] = cell
-            pack_y_edges(cells, k - shift, south, e_ref.at[1 if south else 0], lanes)
-
-        advance_waves(n_ref, xh_ref, yh_ref, rate_ref, wet, tab_ref, quarter, range(ROWS), emit)
+        advance_waves(n_ref, xh_ref, yh_ref, rate_ref, wet, tab_ref, shift_ref, ys_ref, quarter, range(ROWS), emit)
+        pack_y_edges(new_ref, quarter, edge_ref, e_ref)
     new = advance_ocean(ext_ref, below, above, stress_of(n_ref, w_ref), wet8, ocean_ref)
     rows = tuple(
         jnp.concatenate([new[c][8 * z + r : 8 * z + r + 1] for c in range(3) for z in range(NZ)], 0)
@@ -346,8 +381,8 @@
     send_y(e_ref, first, last, even_y, (ye_ref, yo_ref))
 
 
-def last_kernel(n_ref, o_ref, mask_ref, tab_ref, w_ref, xe_in, xo_in, ye_in, yo_in,
-                out_ref, ocean_ref, xh_ref, yh_ref, ext_ref, rate_ref, t_ref):
+def last_kernel(n_ref, o_ref, mask_ref, tab_ref, w_ref, shift_ref, xe_in, xo_in, ye_in, yo_in,
+                out_ref, ocean_ref, xh_ref, yh_ref, ext_ref, rate_ref, ys_ref, t_ref):
     even_x, even_y = is_even("gx"), is_even("gy")
     wet, wet8 = wet_rows(mask_ref)
     left, right, below, above = land_halos(even_x, even_y, xe_in, xo_in, ye_in, yo_in, xh_ref, yh_ref)
@@ -359,7 +394,7 @@
             t_ref[x, pl.ds(k, NF, stride=NDIR), :] = cell
 
     for quarter in range(4):
-        advance_waves(n_ref, xh_ref, yh_ref, rate_ref, wet, tab_ref, quarter, range(ROWS), emit)
+        advance_waves(n_ref, xh_ref, yh_ref, rate_ref, wet, tab_ref, shift_ref, ys_ref, quarter, range(ROWS), emit)
     advance_ocean(ext_ref, below, above, stress_of(n_ref, w_ref), wet8, ocean_ref)
     for x in range(ROWS):
         out_ref[x] = jnp.transpose(t_ref[x]).astype(BF16)
@@ -389,25 +424,36 @@
 GRID = ((ROWS, NDIR, NF, LANES), F32)
 SCRATCH = [
     pltpu.VMEM((2, 2, HALF, NF, LANES), F32),
-    pltpu.VMEM((2, HALF, 8, LANES), F32),
+    pltpu.VMEM((2, HALF * NF, LANES), BF16),
     pltpu.VMEM((3, 8 * NZ, LANES), F32),
     pltpu.VMEM((NDIR, 8, LANES), F32),
+    pltpu.VMEM((ROWS, QUARTER * NF, 2 * LANES), F32),
 ]
 
 
 def local(spectrum, ocean_state, sea_mask):
     ocean_shape = (ocean_state.shape, F32)
+    edge_table = jnp.asarray(edge_tables(), dtype=BF16)
     n, *edges = pl.pallas_call(
         start_kernel,
         out_shape=shapes(GRID, *EDGES),
-        in_specs=[VM] * 3,
+        in_specs=[pl.BlockSpec(memory_space=pl.ANY)] * 4,
         out_specs=[VM] * 5,
-        scratch_shapes=[pltpu.VMEM((ROWS, BINS, LANES), F32), pltpu.VMEM((2, HALF, 8, LANES), F32)],
-        compiler_params=PARAMS,
+        scratch_shapes=[
+            pltpu.VMEM(spectrum.shape, BF16),
+            pltpu.VMEM(ocean_state.shape, F32),
+            pltpu.VMEM(sea_mask.shape, jnp.int32),
+            pltpu.VMEM(edge_table.shape, BF16),
+            pltpu.VMEM((ROWS, BINS, LANES), F32),
+            pltpu.VMEM((2, HALF, 8, LANES), F32),
+            pltpu.SemaphoreType.DMA((ROWS + 3,)),
+        ],
+        compiler_params=pltpu.CompilerParams(vmem_limit_bytes=56 * 1024 * 1024),
         name="start",
-    )(spectrum, ocean_state, sea_mask)
-    speed = jnp.asarray(np.broadcast_to(SPEEDS[:, None], (NF, LANES)))
+    )(spectrum, ocean_state, sea_mask, edge_table)
+    speed = jnp.asarray(np.broadcast_to(SPEEDS[:, None], (NF, LANES)).copy())
     weights = jnp.asarray(stress_table(), dtype=BF16)
+    shift_table = jnp.asarray(shift_tables(), dtype=BF16)
     tab = pl.pallas_call(
         tables_kernel,
         out_shape=shapes(((5, NDIR, NF, LANES), F32))[0],
@@ -420,22 +466,22 @@
     n, ocean, *edges = pl.pallas_call(
         middle_kernel,
         out_shape=shapes(GRID, ocean_shape, *EDGES),
-        in_specs=[VM] * 9,
+        in_specs=[VM] * 11,
         out_specs=[VM] * 6,
         scratch_shapes=SCRATCH + [pltpu.VMEM((2, HALF, 8, LANES), F32)],
         compiler_params=PARAMS,
         name="middle",
-    )(n, ocean_state, sea_mask, tab, weights, *edges)
+    )(n, ocean_state, sea_mask, tab, weights, shift_table, edge_table, *edges)
     edges = exchange(*edges)
     return pl.pallas_call(
         last_kernel,
         out_shape=shapes((spectrum.shape, BF16), ocean_shape),
-        in_specs=[VM] * 9,
+        in_specs=[VM] * 10,
         out_specs=[VM] * 2,
         scratch_shapes=SCRATCH + [pltpu.VMEM((ROWS, BINS, LANES), F32)],
         compiler_params=PARAMS,
         name="last",
-    )(n, ocean, sea_mask, tab, weights, *edges)
+    )(n, ocean, sea_mask, tab, weights, shift_table, *edges)
 
 
 def solution(mesh):

time: 56.2 us -> 39.2 us (0.70)
  Pallas kernels: 26.2 us -> 13 us
  local copies, waits for them, and re-layouts: 6.61 us -> 0.75 us
  waiting for transfers between devices: 8.49 us -> 10.3 us
    pallas_call x1, Pallas kernels: 12.1 us -> 3.94 us  [local(): pl.pallas_call(middle_kernel, out_shape=shapes(GRID, ocean_shape, *EDGES)...]
    pallas_call x1, Pallas kernels: 10 us -> 4.62 us  [local(): pl.pallas_call(last_kernel, out_shape=shapes((spectrum.shape, BF16), ocea...]
    unnamed x16 -> x14, local copies, waits for them, and re-layouts: 5.88 us -> 0.75 us
    ppermute x2, waiting for transfers between devices: 7.58 us -> 9.27 us  [exchange(): xo = lax.ppermute(xo, 'gx', swap_pairs('gx', 1))]
    another operation x1 -> x0, local copies, waits for them, and re-layouts: 0.73 us -> none
  transfers between devices with their start and end apart: 8 -> 8, of which waited for: 3 -> 4; matrix products, arithmetic and copies ran while one was open for 1% -> 0% of each run, Pallas kernels for 0% -> 1%
where the time goes in v2:
time: 39.2 us; the launch traced here: 38.9 us
  starting transfers between devices  14.1 us (36%)
  Pallas kernels  13 us (33%)
  waiting for transfers between devices  10.3 us (26%)
  between operations  0.78 us (2%)
  local copies, waits for them, and re-layouts  0.75 us (2%)
    ppermute x2, starting transfers between devices, exchange(): xo = lax.ppermute(xo, 'gx', swap_pairs('gx', 1))  9.88 us
    ppermute x2, waiting for transfers between devices, exchange(): xo = lax.ppermute(xo, 'gx', swap_pairs('gx', 1))  9.27 us
    pallas_call x1, Pallas kernels, local(): pl.pallas_call(last_kernel, out_shape=shapes((spectrum.shape, BF16), ocea...  4.62 us
    pallas_call x1, Pallas kernels, local(): pl.pallas_call(start_kernel, out_shape=shapes(GRID, *EDGES), in_specs=[pl...  4.16 us
    pallas_call x1, Pallas kernels, local(): pl.pallas_call(middle_kernel, out_shape=shapes(GRID, ocean_shape, *EDGES)...  3.94 us
    ppermute x2, starting transfers between devices, exchange(): ye = lax.ppermute(ye, 'gy', swap_pairs('gy', 0))  2.72 us
    ppermute x2, starting transfers between devices, exchange(): yo = lax.ppermute(yo, 'gy', swap_pairs('gy', 1))  1.3 us
    ppermute x2, waiting for transfers between devices, exchange(): ye = lax.ppermute(ye, 'gy', swap_pairs('gy', 0))  1.03 us
  transfers between devices with their start and end apart: 8, of which 4 were waited for; matrix products, arithmetic and copies ran while one was open for 0% of the time, Pallas kernels for 1%

profile of v2, /device:TPU:1, one launch (start us, length us, event | category | flops | bytes accessed | tf_op | source)
XLA Modules:
  0.0 38.9 jit_solution(17070373060363206995)
XLA Ops:
  0.6 0.0 copy-start.2
  0.6 0.0 copy-start
  0.7 0.0 copy-start.3
  0.7 0.0 copy-start.5
  0.7 0.0 copy-start.4
  0.7 4.2 %start.1 = (f32[4,36,32,128]{3,2,1,0:T(8,128)}, bf16[1248,128]{1,0:T(8,128)(2,1)}, bf16[1248,128]{1,0:T(8,128)(2,1)}, bf16[160,128]{1,0:T(8,128)(2,1)}, bf16[160,128]{1,0:T(8,128)(2,1)}) custom-call(bf16[4,128,1152]{2,1,0:T(8,128)(2,1)} %s_hbm.1, f32[3,16,4,128]{3,2,1,0:T(4,128)} %o_ref.1, s32[4,128]{1,0:T(4,128)} %mask_ref.3, ...), custom_call_target="tpu_custom_call" | custom-call | tf_op jit(solution)/shard_map/start/pallas_call | solution.py:437
  4.9 0.0 copy-start.1
  4.9 0.1 collective-permute-start
  5.0 4.6 %collective-permute-start.1 = (bf16[1248,128]{1,0:T(8,128)(2,1)}, bf16[1248,128]{1,0:T(8,128)(2,1)S(1)}, u32[]{:S(2)}, u32[]{:S(2)}) collective-permute-start(bf16[1248,128]{1,0:T(8,128)(2,1)} %get-tuple-element.15), channel_id=1, source_target_pairs={{4,8},{8,4},{12,16},{16,12},{20,24},{24,20},{5,9},{9,5},{13,17},{1... | collective-permute-start | bytes 958472 | tf_op jit(solution)/shard_map/ppermute | solution.py:412
  9.6 1.4 %collective-permute-start.2 = (bf16[160,128]{1,0:T(8,128)(2,1)}, bf16[160,128]{1,0:T(8,128)(2,1)S(1)}, u32[]{:S(2)}, u32[]{:S(2)}) collective-permute-start(bf16[160,128]{1,0:T(8,128)(2,1)} %get-tuple-element.16), channel_id=1, source_target_pairs={{0,1},{1,0},{2,3},{3,2},{4,5},{5,4},{6,7},{7,6},{8,9},{9,8},{10,11... | collective-permute-start | bytes 122888 | tf_op jit(solution)/shard_map/ppermute | solution.py:414
  10.9 0.7 %collective-permute-start.3 = (bf16[160,128]{1,0:T(8,128)(2,1)}, bf16[160,128]{1,0:T(8,128)(2,1)S(1)}, u32[]{:S(2)}, u32[]{:S(2)}) collective-permute-start(bf16[160,128]{1,0:T(8,128)(2,1)} %get-tuple-element.17), channel_id=1, source_target_pairs={{1,2},{2,1},{5,6},{6,5},{9,10},{10,9},{13,14},{14,13},{17,18},{18,... | collective-permute-start | bytes 122888 | tf_op jit(solution)/shard_map/ppermute | solution.py:415
  11.6 0.0 copy-start.6
  11.6 0.7 %copy-done.6 = f32[32,128]{1,0:T(8,128)S(1)} copy-done((f32[32,128]{1,0:T(8,128)S(1)}, f32[32,128]{1,0:T(8,128)}, u32[]{:S(2)}) %copy-start.6) | copy-done | bytes 16408
  12.3 0.2 tables.1.tab_ref
  12.6 0.1 collective-permute-done.2.ye_in
  12.7 0.0 collective-permute-done.3.yo_in
  12.7 0.0 collective-permute-done.xe_in
  12.7 4.3 %collective-permute-done.1.xo_in = bf16[1248,128]{1,0:T(8,128)(2,1)S(1)} collective-permute-done((bf16[1248,128]{1,0:T(8,128)(2,1)}, bf16[1248,128]{1,0:T(8,128)(2,1)S(1)}, u32[]{:S(2)}, u32[]{:S(2)}) %collective-permute-start.1) | collective-permute-done | bytes 319520 | tf_op jit(solution)/shard_map/ppermute | solution.py:412
  17.0 0.0 copy-done.2
  17.0 0.0 copy-done
  17.0 0.0 copy-done.3
  17.0 0.0 copy-done.5
  17.0 3.9 %middle.1 = (f32[4,36,32,128]{3,2,1,0:T(8,128)S(1)}, f32[3,16,4,128]{3,2,1,0:T(4,128)S(1)}, bf16[1248,128]{1,0:T(8,128)(2,1)S(1)}, bf16[1248,128]{1,0:T(8,128)(2...) custom-call(f32[4,36,32,128]{3,2,1,0:T(8,128)S(1)} %copy-done.1, f32[3,16,4,128]{3,2,1,0:T(4,128)S(1)} %copy-done.4, ...), custom_call_target="tpu_custom_call" | custom-call | tf_op jit(solution)/shard_map/middle/pallas_call | solution.py:466
  21.0 0.1 collective-permute-start.4
  21.1 5.3 %collective-permute-start.5 = (bf16[1248,128]{1,0:T(8,128)(2,1)S(1)}, bf16[1248,128]{1,0:T(8,128)(2,1)S(1)}, u32[]{:S(2)}, u32[]{:S(2)}) collective-permute-start(bf16[1248,128]{1,0:T(8,128)(2,1)S(1)} %get-tuple-element.21), channel_id=1, source_target_pairs={{4,8},{8,4},{12,16},{16,12},{20,24},{24,20},{5,9},{9,5},{13,17},{1... | collective-permute-start | bytes 958472 | tf_op jit(solution)/shard_map/ppermute | solution.py:412
  26.3 1.4 %collective-permute-start.6 = (bf16[160,128]{1,0:T(8,128)(2,1)S(1)}, bf16[160,128]{1,0:T(8,128)(2,1)S(1)}, u32[]{:S(2)}, u32[]{:S(2)}) collective-permute-start(bf16[160,128]{1,0:T(8,128)(2,1)S(1)} %get-tuple-element.22), channel_id=1, source_target_pairs={{0,1},{1,0},{2,3},{3,2},{4,5},{5,4},{6,7},{7,6},{8,9},{9,8},{10,11... | collective-permute-start | bytes 122888 | tf_op jit(solution)/shard_map/ppermute | solution.py:414
  27.7 0.7 %collective-permute-start.7 = (bf16[160,128]{1,0:T(8,128)(2,1)S(1)}, bf16[160,128]{1,0:T(8,128)(2,1)S(1)}, u32[]{:S(2)}, u32[]{:S(2)}) collective-permute-start(bf16[160,128]{1,0:T(8,128)(2,1)S(1)} %get-tuple-element.23), channel_id=1, source_target_pairs={{1,2},{2,1},{5,6},{6,5},{9,10},{10,9},{13,14},{14,13},{17,18},{18,... | collective-permute-start | bytes 122888 | tf_op jit(solution)/shard_map/ppermute | solution.py:415
  28.4 0.9 %collective-permute-done.6.ye_in = bf16[160,128]{1,0:T(8,128)(2,1)S(1)} collective-permute-done((bf16[160,128]{1,0:T(8,128)(2,1)S(1)}, bf16[160,128]{1,0:T(8,128)(2,1)S(1)}, u32[]{:S(2)}, u32[]{:S(2)}) %collective-permute-start.6) | collective-permute-done | bytes 40992 | tf_op jit(solution)/shard_map/ppermute | solution.py:414
  29.3 0.0 collective-permute-done.7.yo_in
  29.3 0.0 collective-permute-done.4.xe_in
  29.3 5.0 %collective-permute-done.5.xo_in = bf16[1248,128]{1,0:T(8,128)(2,1)S(1)} collective-permute-done((bf16[1248,128]{1,0:T(8,128)(2,1)S(1)}, bf16[1248,128]{1,0:T(8,128)(2,1)S(1)}, u32[]{:S(2)}, u32[]{:S(2)}) %collective-permute-start.5) | collective-permute-done | bytes 319520 | tf_op jit(solution)/shard_map/ppermute | solution.py:412
  34.3 4.6 %last.1 = (bf16[4,128,1152]{2,1,0:T(8,128)(2,1)}, f32[3,16,4,128]{3,2,1,0:T(4,128)}) custom-call(f32[4,36,32,128]{3,2,1,0:T(8,128)S(1)} %get-tuple-element.18.n_ref, f32[3,16,4,128]{3,2,1,0:T(4,128)S(1)} %get-tuple-element.19.o_ref, s32[4,128]{1,0:T(4,128)S(1)} %copy-done.5, f32[5,36,32,128]{3,2,1,0:T(8,128)S(1)} %tables.1.tab_ref, ...), custom_call_target="tpu_custom_call" | custom-call | tf_op jit(solution)/shard_map/last/pallas_call | solution.py:476
  (2 shorter events, 0.0 us)
Async XLA Ops:
  0.6 16.4 %copy-start.2 = (bf16[2,512,128]{2,1,0:T(8,128)(2,1)S(1)}, bf16[2,512,128]{2,1,0:T(8,128)(2,1)}, u32[]{:S(2)}) copy-start(bf16[2,512,128]{2,1,0:T(8,128)(2,1)} %constant.8.clone.edge_hbm.edge_ref) | copy-start | bytes 786436
  0.6 16.4 %copy-start = (bf16[2,4,256,256]{3,2,1,0:T(8,128)(2,1)S(1)}, bf16[2,4,256,256]{3,2,1,0:T(8,128)(2,1)}, u32[]{:S(2)}) copy-start(bf16[2,4,256,256]{3,2,1,0:T(8,128)(2,1)} %constant.11.clone.shift_ref) | copy-start | bytes 3145732
  0.7 16.3 %copy-start.3 = (bf16[4,16,1152]{2,1,0:T(8,128)(2,1)S(1)}, bf16[4,16,1152]{2,1,0:T(8,128)(2,1)}, u32[]{:S(2)}) copy-start(bf16[4,16,1152]{2,1,0:T(8,128)(2,1)} %constant.10.clone.w_ref) | copy-start | bytes 442372
  0.7 16.3 %copy-start.5 = (s32[4,128]{1,0:T(4,128)S(1)}, s32[4,128]{1,0:T(4,128)}, u32[]{:S(2)}) copy-start(s32[4,128]{1,0:T(4,128)} %mask_ref.3) | copy-start | bytes 6148
  0.7 16.3 %copy-start.4 = (f32[3,16,4,128]{3,2,1,0:T(4,128)S(1)}, f32[3,16,4,128]{3,2,1,0:T(4,128)}, u32[]{:S(2)}) copy-start(f32[3,16,4,128]{3,2,1,0:T(4,128)} %o_ref.1) | copy-start | bytes 294916
  4.9 12.2 %copy-start.1 = (f32[4,36,32,128]{3,2,1,0:T(8,128)S(1)}, f32[4,36,32,128]{3,2,1,0:T(8,128)}, u32[]{:S(2)}) copy-start(f32[4,36,32,128]{3,2,1,0:T(8,128)} %get-tuple-element.13.n_ref) | copy-start | bytes 7077892
  4.9 7.9 %collective-permute-start = (bf16[1248,128]{1,0:T(8,128)(2,1)}, bf16[1248,128]{1,0:T(8,128)(2,1)S(1)}, u32[]{:S(2)}, u32[]{:S(2)}) collective-permute-start(bf16[1248,128]{1,0:T(8,128)(2,1)} %get-tuple-element.14), channel_id=1, source_target_pairs={{0,4},{4,0},{8,12},{12,8},{16,20},{20,16},{24,28},{28,24},{1,5},{5... | collective-permute-start | bytes 958472 | tf_op jit(solution)/shard_map/ppermute | solution.py:413
  5.0 12.0 %collective-permute-start.1 = (bf16[1248,128]{1,0:T(8,128)(2,1)}, bf16[1248,128]{1,0:T(8,128)(2,1)S(1)}, u32[]{:S(2)}, u32[]{:S(2)}) collective-permute-start(bf16[1248,128]{1,0:T(8,128)(2,1)} %get-tuple-element.15), channel_id=1, source_target_pairs={{4,8},{8,4},{12,16},{16,12},{20,24},{24,20},{5,9},{9,5},{13,17},{1... | collective-permute-start | bytes 958472 | tf_op jit(solution)/shard_map/ppermute | solution.py:412
  9.6 3.1 %collective-permute-start.2 = (bf16[160,128]{1,0:T(8,128)(2,1)}, bf16[160,128]{1,0:T(8,128)(2,1)S(1)}, u32[]{:S(2)}, u32[]{:S(2)}) collective-permute-start(bf16[160,128]{1,0:T(8,128)(2,1)} %get-tuple-element.16), channel_id=1, source_target_pairs={{0,1},{1,0},{2,3},{3,2},{4,5},{5,4},{6,7},{7,6},{8,9},{9,8},{10,11... | collective-permute-start | bytes 122888 | tf_op jit(solution)/shard_map/ppermute | solution.py:414
  10.9 1.8 %collective-permute-start.3 = (bf16[160,128]{1,0:T(8,128)(2,1)}, bf16[160,128]{1,0:T(8,128)(2,1)S(1)}, u32[]{:S(2)}, u32[]{:S(2)}) collective-permute-start(bf16[160,128]{1,0:T(8,128)(2,1)} %get-tuple-element.17), channel_id=1, source_target_pairs={{1,2},{2,1},{5,6},{6,5},{9,10},{10,9},{13,14},{14,13},{17,18},{18,... | collective-permute-start | bytes 122888 | tf_op jit(solution)/shard_map/ppermute | solution.py:415
  11.6 0.7 %copy-start.6 = (f32[32,128]{1,0:T(8,128)S(1)}, f32[32,128]{1,0:T(8,128)}, u32[]{:S(2)}) copy-start(f32[32,128]{1,0:T(8,128)} %constant.9.clone.speed_ref) | copy-start | bytes 49156
  21.0 8.3 %collective-permute-start.4 = (bf16[1248,128]{1,0:T(8,128)(2,1)S(1)}, bf16[1248,128]{1,0:T(8,128)(2,1)S(1)}, u32[]{:S(2)}, u32[]{:S(2)}) collective-permute-start(bf16[1248,128]{1,0:T(8,128)(2,1)S(1)} %get-tuple-element.20), channel_id=1, source_target_pairs={{0,4},{4,0},{8,12},{12,8},{16,20},{20,16},{24,28},{28,24},{1,5},{5... | collective-permute-start | bytes 958472 | tf_op jit(solution)/shard_map/ppermute | solution.py:413
  21.1 13.2 %collective-permute-start.5 = (bf16[1248,128]{1,0:T(8,128)(2,1)S(1)}, bf16[1248,128]{1,0:T(8,128)(2,1)S(1)}, u32[]{:S(2)}, u32[]{:S(2)}) collective-permute-start(bf16[1248,128]{1,0:T(8,128)(2,1)S(1)} %get-tuple-element.21), channel_id=1, source_target_pairs={{4,8},{8,4},{12,16},{16,12},{20,24},{24,20},{5,9},{9,5},{13,17},{1... | collective-permute-start | bytes 958472 | tf_op jit(solution)/shard_map/ppermute | solution.py:412
  26.3 2.9 %collective-permute-start.6 = (bf16[160,128]{1,0:T(8,128)(2,1)S(1)}, bf16[160,128]{1,0:T(8,128)(2,1)S(1)}, u32[]{:S(2)}, u32[]{:S(2)}) collective-permute-start(bf16[160,128]{1,0:T(8,128)(2,1)S(1)} %get-tuple-element.22), channel_id=1, source_target_pairs={{0,1},{1,0},{2,3},{3,2},{4,5},{5,4},{6,7},{7,6},{8,9},{9,8},{10,11... | collective-permute-start | bytes 122888 | tf_op jit(solution)/shard_map/ppermute | solution.py:414
  27.7 1.6 %collective-permute-start.7 = (bf16[160,128]{1,0:T(8,128)(2,1)S(1)}, bf16[160,128]{1,0:T(8,128)(2,1)S(1)}, u32[]{:S(2)}, u32[]{:S(2)}) collective-permute-start(bf16[160,128]{1,0:T(8,128)(2,1)S(1)} %get-tuple-element.23), channel_id=1, source_target_pairs={{1,2},{2,1},{5,6},{6,5},{9,10},{10,9},{13,14},{14,13},{17,18},{18,... | collective-permute-start | bytes 122888 | tf_op jit(solution)/shard_map/ppermute | solution.py:415

commit v3 on v2

v3 whole, which is shorter than its diff:
```python
import math

import jax
import jax.numpy as jnp
import numpy as np
from jax import lax
from jax.experimental import pallas as pl
from jax.experimental.pallas import tpu as pltpu
from jax.sharding import PartitionSpec as P

NF = 32
NDIR = 36
NZ = 16
HALF = NDIR // 2
QUARTER = NDIR // 4
ROWS = 4
LANES = 128
BINS = NF * NDIR

COURANT = 0.4
RATIO = 0.93
TURN = 0.1
STRESS = 0.1
CORIOLIS = 0.2
PRESS = 0.1
VISC = 0.15
ADVECT = 0.5
DIFFUSE = 0.15

F32 = jnp.float32
BF16 = jnp.bfloat16
VM = pl.BlockSpec(memory_space=pltpu.VMEM)
HBM = pl.BlockSpec(memory_space=pl.ANY)
FIRST = pltpu.CompilerParams(vmem_limit_bytes=56 * 1024 * 1024)
PARAMS = pltpu.CompilerParams(vmem_limit_bytes=16 * 1024 * 1024)

SPECTRA = 2 * HALF * NF
OCEAN = 3 * NZ
XROWS = SPECTRA + 2 * OCEAN
YROWS = HALF * 8 + 16

ANGLES = -0.5 * math.pi + (np.arange(NDIR, dtype=np.float32) + np.float32(0.5)) * np.float32(
    2.0 * math.pi / NDIR
)
COS = np.cos(ANGLES).astype(np.float32)
SIN = np.sin(ANGLES).astype(np.float32)
SPEEDS = (COURANT * RATIO ** np.arange(NF, dtype=np.float64)).astype(np.float32)


def stress_table():
    table = np.zeros((ROWS, 16, NDIR, NF), np.float32)
    for c, part in enumerate((COS, SIN)):
        weights = np.float32(STRESS) * SPEEDS[None, :] * part[:, None]
        for x in range(ROWS):
            table[x, c * 8 + 1 + x] = weights
    return table.reshape(ROWS, 16, BINS)


def is_even(axis):
    return lax.rem(lax.axis_index(axis), 2) == 0


def inside(axis):
    i = lax.axis_index(axis)
    return jnp.logical_and(i > 0, i < lax.axis_size(axis) - 1)


def split(v):
    high = v.astype(BF16).astype(F32)
    return high, v - high


def roll(v, shift, axis):
    return pltpu.roll(v, shift % v.shape[axis], axis)


def lane_of(shape):
    return lax.broadcasted_iota(jnp.int32, shape, len(shape) - 1)


def edge_tables():
    table = np.zeros((2, ROWS, LANES, LANES), np.float32)
    for side, start in enumerate((0, LANES - 2)):
        for x in range(ROWS):
            for g in range(4):
                for j in range(2):
                    table[side, x, start + j, 8 * g + 2 * x + j] = 1.0
    return table.reshape(2, ROWS * LANES, LANES)


def shift_tables():
    table = np.zeros((2, 2 * LANES, 2 * LANES), np.float32)
    for side, sign in enumerate((1, -1)):
        for far in range(2):
            for lane in range(LANES):
                source = lane + sign * (1 + far)
                if 0 <= source < LANES:
                    table[side, source, far * LANES + lane] = 1.0
                else:
                    j = source - LANES if sign > 0 else source + 2
                    for x in range(ROWS):
                        for g in range(4):
                            table[side, LANES + 32 * x + 8 * g + 2 * x + j, far * LANES + lane] = 1.0
    return table


def pack_y_edges(n_ref, quarter, tables_ref, out_ref):
    south = quarter in (1, 2)
    first = quarter * QUARTER
    rows = [
        n_ref[x, first : first + QUARTER].reshape(QUARTER * NF, LANES).astype(BF16) for x in range(ROWS)
    ]
    found = jnp.dot(
        jnp.concatenate(rows, 1), tables_ref[1 if south else 0], preferred_element_type=F32
    ).reshape(QUARTER, 4, 8, LANES)
    group = lane_of((QUARTER, 8, LANES)) // 8
    packed = found[:, 0]
    for g in range(1, 4):
        packed = jnp.where(group == g, found[:, g], packed)
    at = 0 if quarter < 2 else QUARTER
    out_ref[1 if south else 0, at : at + QUARTER] = packed


def pack_ocean_columns(blocks, lanes):
    first = jnp.zeros((8, LANES), F32)
    last = jnp.zeros((8, LANES), F32)
    for c in range(3):
        for z in range(NZ):
            block = blocks[c][8 * z : 8 * z + 8]
            at = c * NZ + z
            first = jnp.where(lanes == at, roll(block, at, 1), first)
            last = jnp.where(lanes == at, roll(block, at - (LANES - 1), 1), last)
    return first, last


def send_x(n_ref, ocean_rows, mine_ref, low_side):
    row = jnp.where(low_side, 0, 2)
    first = jnp.where(low_side, HALF, 0)
    edge = n_ref[pl.ds(row, 2), pl.ds(first, HALF)]
    mine_ref[0:SPECTRA, :] = edge.reshape(SPECTRA, LANES).astype(BF16)
    send_ocean_row(ocean_rows, mine_ref, low_side)


def send_ocean_row(ocean_rows, mine_ref, low_side):
    low, high = ocean_rows
    whole, rest = split(jnp.where(low_side, low, high))
    mine_ref[SPECTRA : SPECTRA + OCEAN, :] = whole.astype(BF16)
    mine_ref[SPECTRA + OCEAN : XROWS, :] = rest.astype(BF16)


def send_y(edges_ref, first, last, even, outs):
    for slot, out_ref in enumerate(outs):
        takes_last = even if slot == 0 else jnp.logical_not(even)
        which = takes_last.astype(jnp.int32)
        out_ref[0 : HALF * 8, :] = edges_ref[which].reshape(HALF * 8, LANES).astype(BF16)
        whole, rest = split(jnp.where(takes_last, last, first))
        out_ref[HALF * 8 : YROWS, :] = jnp.concatenate([whole, rest], 0).astype(BF16)


def first_kernel(s_hbm, o_hbm, mask_hbm, xo_ref, s_ref, o_ref, mask_ref, t_ref, sems):
    low_side = is_even("gx")
    row = jnp.where(low_side, 0, 2)
    first = jnp.where(low_side, HALF, 0)
    copies = [pltpu.make_async_copy(s_hbm.at[row + r], s_ref.at[r], sems.at[r]) for r in range(2)]
    copies.append(pltpu.make_async_copy(mask_hbm, mask_ref, sems.at[2]))
    copies.append(pltpu.make_async_copy(o_hbm, o_ref, sems.at[3]))
    for copy in copies:
        copy.start()
    copies[2].wait()
    for r in range(2):
        copies[r].wait()
        t_ref[r] = jnp.transpose(s_ref[r].astype(F32))
        wet = mask_ref[pl.ds(row + r, 1), :].astype(F32)

        def body(kk, carry, r=r, wet=wet):
            at = pl.ds(pl.multiple_of((r * HALF + kk) * NF, NF), NF)
            xo_ref[at, :] = (t_ref[r, pl.ds(first + kk, NF, stride=NDIR), :] * wet).astype(BF16)
            return carry

        lax.fori_loop(0, HALF, body, 0, unroll=2)
    copies[3].wait()
    rows = tuple(o_ref[:, :, r, :].reshape(OCEAN, LANES) for r in (0, ROWS - 1))
    send_ocean_row(rows, xo_ref, low_side)


def start_kernel(s_ref, o_ref, mask_ref, edge_ref, speed_ref,
                 n_ref, xe_ref, ye_ref, yo_ref, tab_ref, t_ref, e_ref):
    wet = mask_ref[...].astype(F32)
    for x in range(ROWS):
        t_ref[x] = jnp.transpose(s_ref[x].astype(F32))

    def body(k, carry):
        for x in range(ROWS):
            n_ref[x, k] = t_ref[x, pl.ds(k, NF, stride=NDIR), :] * wet[x : x + 1]
        return carry

    lax.fori_loop(0, NDIR, body, 0, unroll=2)
    even_x, even_y = is_even("gx"), is_even("gy")
    rows = tuple(o_ref[:, :, r, :].reshape(OCEAN, LANES) for r in (0, ROWS - 1))
    send_x(n_ref, rows, xe_ref, jnp.logical_not(even_x))
    for quarter in range(4):
        pack_y_edges(n_ref, quarter, edge_ref, e_ref)
    pad = jnp.zeros((1, LANES), F32)
    blocks = [
        jnp.concatenate(
            [part for z in range(NZ) for part in (pad, o_ref[c, z], pad, pad, pad)], 0
        )
        for c in range(3)
    ]
    first, last = pack_ocean_columns(blocks, lane_of((8, LANES)))
    send_y(e_ref, first, last, even_y, (ye_ref, yo_ref))
    make_tables(speed_ref, tab_ref)


def make_tables(speed_ref, tab_ref):
    speed = speed_ref[...]
    for k in range(NDIR):
        cx, cy = speed * abs(float(COS[k])), speed * abs(float(SIN[k]))
        near_x, far_x = cx * (2.0 - cx), (0.5 * cx) * (cx - 1.0)
        near_y, far_y = cy * (2.0 - cy), (0.5 * cy) * (cy - 1.0)
        tab_ref[0, k] = 1.0 - ((near_x + far_x) + (near_y + far_y))
        tab_ref[1, k] = near_x
        tab_ref[2, k] = far_x
        tab_ref[3, k] = near_y
        tab_ref[4, k] = far_y


def y_spectra(even_y, ye_ref, yo_ref, yh_ref):
    shape = (HALF, 8, LANES)
    a = ye_ref[0 : HALF * 8, :].astype(F32)
    b = jnp.where(inside("gy"), yo_ref[0 : HALF * 8, :].astype(F32), 0.0)
    group = lane_of(shape) // 8
    for to, pair in ((0, (a, b)), (1, (b, a))):
        edge = jnp.where(even_y, *pair).reshape(shape)
        parts = [jnp.where(group == g, edge, 0.0)[:, None] for g in range(4)]
        yh_ref[to] = jnp.concatenate(parts, 1).reshape(HALF * NF, LANES).astype(BF16)


def y_ocean(even_y, ye_ref, yo_ref):
    def columns(ref):
        both = ref[HALF * 8 : YROWS, :].astype(F32)
        return both[0:8] + both[8:16]

    a, b = columns(ye_ref), jnp.where(inside("gy"), columns(yo_ref), 0.0)
    return jnp.where(even_y, b, a), jnp.where(even_y, a, b)


def x_ocean(even_x, xe_ref, xo_ref):
    def rows(ref):
        return ref[SPECTRA : SPECTRA + OCEAN, :].astype(F32) + ref[SPECTRA + OCEAN : XROWS, :].astype(F32)

    a, b = rows(xe_ref), jnp.where(inside("gx"), rows(xo_ref), 0.0)
    return jnp.where(even_x, b, a), jnp.where(even_x, a, b)


def extend_ocean(o_ref, left, right, ext_ref, levels=NZ):
    for c in range(3):
        for z in range(levels):
            at = c * NZ + z
            ext_ref[c, 8 * z : 8 * z + 1, :] = left[at : at + 1]
            ext_ref[c, 8 * z + 1 : 8 * z + 5, :] = o_ref[c, z]
            ext_ref[c, 8 * z + 5 : 8 * z + 6, :] = right[at : at + 1]
            ext_ref[c, 8 * z + 6 : 8 * z + 8, :] = jnp.zeros((2, LANES), F32)


def neighbours(c, q, below, above, levels):
    lanes = lane_of(q.shape)
    low = jnp.concatenate([roll(below, -(c * NZ + z), 1) for z in range(levels)], 0)
    high = jnp.concatenate([roll(above, LANES - 1 - (c * NZ + z), 1) for z in range(levels)], 0)
    return (
        roll(q, 1, 0),
        roll(q, -1, 0),
        jnp.where(lanes == 0, low, roll(q, 1, 1)),
        jnp.where(lanes == LANES - 1, high, roll(q, -1, 1)),
    )


def refraction_rates(ext_ref, below, above, rate_ref):
    grads = []
    for c in range(2):
        xm, xp, ym, yp = neighbours(c, ext_ref[c, 0:8, :], below, above, 1)
        grads.append(((xp - xm) * 0.5, (yp - ym) * 0.5))
    (ux, uy), (vx, vy) = grads
    stretch = ux - vy
    for k in range(NDIR):
        c, s = float(COS[k]), float(SIN[k])
        rate_ref[k] = (TURN * c * s) * stretch + (TURN * s * s) * vx - (TURN * c * c) * uy


def advance_ocean(ext_ref, below, above, stress, wet8, out_ref):
    zonal, north, heat = (ext_ref[c] for c in range(3))
    wet = jnp.concatenate([wet8] * NZ, 0)

    def stencil(c, q):
        xm, xp, ym, yp = neighbours(c, q, below, above, NZ)
        return (xp - xm) * 0.5, (yp - ym) * 0.5, xp + xm + yp + ym - 4.0 * q

    _, _, zonal_lap = stencil(0, zonal)
    _, _, north_lap = stencil(1, north)
    heat_x, heat_y, heat_lap = stencil(2, heat)

    def running(v):
        total = v[0:8]
        sums = [total]
        for z in range(1, NZ):
            total = total + v[8 * z : 8 * z + 8]
            sums.append(total)
        return jnp.concatenate(sums, 0)

    rest = jnp.zeros((8 * (NZ - 1), LANES), F32)
    push_u = jnp.concatenate([stress[0:8], rest], 0)
    push_v = jnp.concatenate([stress[8:16], rest], 0)
    new = (
        wet * (zonal + CORIOLIS * north - PRESS * running(heat_x) + VISC * zonal_lap + push_u),
        wet * (north - CORIOLIS * zonal - PRESS * running(heat_y) + VISC * north_lap + push_v),
        heat + wet * (DIFFUSE * heat_lap - ADVECT * (zonal * heat_x + north * heat_y)),
    )
    for c in range(3):
        for z in range(NZ):
            out_ref[c, z] = new[c][8 * z + 1 : 8 * z + 5]
    return new


def stress_of(n_ref, weights_ref):
    total = jnp.zeros((16, LANES), F32)
    for x in range(ROWS):
        cells = n_ref[x].reshape(BINS, LANES).astype(BF16)
        total = total + jnp.dot(weights_ref[x], cells, preferred_element_type=F32)
    return total


def refraction(n_ref, rate_ref, x, k):
    below = jnp.where(k == 0, NDIR - 1, k - 1)
    above = jnp.where(k == NDIR - 1, 0, k + 1)
    rate = jnp.broadcast_to(rate_ref[k, pl.ds(x + 1, 1), :], (NF, LANES))
    upwind = jnp.where(rate > 0.0, n_ref[x, below], n_ref[x, above])
    return jnp.abs(rate) * (upwind - n_ref[x, k])


def inner_waves(n_ref, yh_ref, rate_ref, wet, tab_ref, shift_ref, ys_ref, acc_ref, keep):
    size = QUARTER * NF
    for quarter in range(4):
        step = 1 if quarter >= 2 else -1
        side = 1 if quarter in (1, 2) else 0
        first = quarter * QUARTER
        edges = yh_ref[side, 0:size, :] if quarter < 2 else yh_ref[side, size : 2 * size, :]
        blank = jnp.zeros((LANES - 32, 2 * LANES), BF16)
        for x in range(ROWS):
            cells = n_ref[x, first : first + QUARTER].reshape(size, LANES).astype(BF16)
            edge_rows = shift_ref[side, LANES + 32 * x : LANES + 32 * x + 32, :]
            moves = jnp.concatenate([shift_ref[side, 0:LANES, :], edge_rows, blank], 0)
            ys_ref[x] = jnp.dot(jnp.concatenate([cells, edges], 1), moves, preferred_element_type=F32)

        def body(j, carry, first=first, step=step):
            k = first + j
            weights = [tab_ref[t, k] for t in range(5)]
            at = pl.ds(pl.multiple_of(j * NF, NF), NF)
            cells = [n_ref[x, k] for x in range(ROWS)]
            for x in range(ROWS):
                total = cells[x] * weights[0]
                for weight, other in zip(weights[1:3], (x + step, x + 2 * step)):
                    if 0 <= other < ROWS:
                        total = total + cells[other] * weight
                near_y, far_y = ys_ref[x, at, 0:LANES], ys_ref[x, at, LANES : 2 * LANES]
                total = total + (near_y * weights[3] + far_y * weights[4])
                if x in (1, 2):
                    total = total + refraction(n_ref, rate_ref, x, k)
                    if 0 <= x + 2 * step < ROWS:
                        total = keep(total * wet[x])
                acc_ref[x, k] = total
            return carry

        lax.fori_loop(0, QUARTER, body, 0)


def wet_row(mask_ref, x):
    return jnp.broadcast_to(mask_ref[pl.ds(x, 1), :].astype(F32), (NF, LANES))


def finish_far_half(n_ref, acc_ref, rate_ref, mask_ref, side, keep):
    x = 3 * side
    wet = wet_row(mask_ref, x)
    first = HALF * (1 - side)

    def body(kk, carry):
        k = first + kk
        acc_ref[x, k] = keep(wet * (acc_ref[x, k] + refraction(n_ref, rate_ref, x, k)))
        return carry

    lax.fori_loop(0, HALF, body, 0, unroll=2)


def finish_near_half(n_ref, acc_ref, rate_ref, mask_ref, tab_ref, halo_ref, known, side, keep):
    x, inner = 3 * side, 1 + side
    wet, wet_inner = wet_row(mask_ref, x), wet_row(mask_ref, inner)
    first = HALF * side

    def body(kk, carry):
        k = first + kk
        near = halo_ref[pl.ds(pl.multiple_of(((1 - side) * HALF + kk) * NF, NF), NF), :].astype(F32)
        far = halo_ref[pl.ds(pl.multiple_of((side * HALF + kk) * NF, NF), NF), :].astype(F32)
        near, far = jnp.where(known, near, 0.0), jnp.where(known, far, 0.0)
        total = acc_ref[x, k] + (near * tab_ref[1, k] + far * tab_ref[2, k])
        acc_ref[x, k] = keep(wet * (total + refraction(n_ref, rate_ref, x, k)))
        acc_ref[inner, k] = keep(wet_inner * (acc_ref[inner, k] + near * tab_ref[2, k]))
        return carry

    lax.fori_loop(0, HALF, body, 0, unroll=2)


def rounded(v):
    return v.astype(BF16).astype(F32)


def exact(v):
    return v


def wet_rows(mask_ref):
    wet = mask_ref[...].astype(F32)
    pad = jnp.zeros((1, LANES), F32)
    wet8 = jnp.concatenate([pad, wet, pad, pad, pad], 0)
    return [jnp.broadcast_to(wet[x : x + 1], (NF, LANES)) for x in range(ROWS)], wet8


def inner_kernel(n_ref, o_ref, mask_ref, tab_ref, w_ref, shift_ref, ye_in, yo_in,
                 acc_ref, stress_ref, yh_ref, ext_ref, rate_ref, ys_ref):
    even_y = is_even("gy")
    wet, _ = wet_rows(mask_ref)
    y_spectra(even_y, ye_in, yo_in, yh_ref)
    below, above = y_ocean(even_y, ye_in, yo_in)
    unknown = jnp.zeros((OCEAN, LANES), F32)
    extend_ocean(o_ref, unknown, unknown, ext_ref, 1)
    refraction_rates(ext_ref, below, above, rate_ref)
    stress_ref[...] = stress_of(n_ref, w_ref)
    inner_waves(n_ref, yh_ref, rate_ref, wet, tab_ref, shift_ref, ys_ref, acc_ref, rounded)


def send_kernel(n_ref, acc_in, o_ref, mask_ref, stress_ref, xe_in, xo_in, ye_in, yo_in,
                acc_ref, ocean_ref, rate_ref, xo_ref, xrow_ref, ycol_ref, ext_ref):
    even_x, even_y = is_even("gx"), is_even("gy")
    below, above = y_ocean(even_y, ye_in, yo_in)
    left, right = x_ocean(even_x, xe_in, xo_in)
    extend_ocean(o_ref, left, right, ext_ref)
    refraction_rates(ext_ref, below, above, rate_ref)
    finish_far_half(n_ref, acc_ref, rate_ref, mask_ref, 1 - even_x.astype(jnp.int32), rounded)
    _, wet8 = wet_rows(mask_ref)
    new = advance_ocean(ext_ref, below, above, stress_ref[...], wet8, ocean_ref)
    rows = tuple(
        jnp.concatenate([new[c][8 * z + r : 8 * z + r + 1] for c in range(3) for z in range(NZ)], 0)
        for r in (1, ROWS)
    )
    send_x(acc_ref, rows, xo_ref, even_x)
    xrow_ref[...] = jnp.where(even_x, rows[1], rows[0])
    ycol_ref[0], ycol_ref[1] = pack_ocean_columns(new, lane_of((8, LANES)))


def rest_kernel(n_ref, acc_in, mask_ref, tab_ref, rate_ref, edge_ref, xrow_ref, ycol_ref, xe_in, xo_in,
                acc_ref, xe_ref, ye_ref, yo_ref, e_ref):
    even_x, even_y = is_even("gx"), is_even("gy")
    side = even_x.astype(jnp.int32)
    finish_near_half(n_ref, acc_ref, rate_ref, mask_ref, tab_ref, xo_in, inside("gx"), 1 - side, rounded)
    finish_near_half(n_ref, acc_ref, rate_ref, mask_ref, tab_ref, xe_in, True, side, rounded)
    finish_far_half(n_ref, acc_ref, rate_ref, mask_ref, side, rounded)
    row = xrow_ref[...]
    send_x(acc_ref, (row, row), xe_ref, jnp.logical_not(even_x))
    for quarter in range(4):
        pack_y_edges(acc_ref, quarter, edge_ref, e_ref)
    send_y(e_ref, ycol_ref[0], ycol_ref[1], even_y, (ye_ref, yo_ref))


def write_rows(acc_ref, first, t_ref, block_ref, out_hbm, sems):
    copies = []
    for r in range(2):

        def body(k, carry, r=r):
            t_ref[r, pl.ds(k, NF, stride=NDIR), :] = acc_ref[first + r, k]
            return carry

        lax.fori_loop(0, NDIR, body, 0, unroll=2)
        block_ref[r] = jnp.transpose(t_ref[r]).astype(BF16)
        copies.append(pltpu.make_async_copy(block_ref.at[r], out_hbm.at[first + r], sems.at[r]))
        copies[-1].start()
    for copy in copies:
        copy.wait()


def inner_last_kernel(n_ref, o_ref, mask_ref, tab_ref, w_ref, shift_ref, xe_in, ye_in, yo_in,
                      acc_ref, stress_ref, out_hbm,
                      yh_ref, ext_ref, rate_ref, ys_ref, t_ref, block_ref, sems):
    even_x, even_y = is_even("gx"), is_even("gy")
    wet, _ = wet_rows(mask_ref)
    y_spectra(even_y, ye_in, yo_in, yh_ref)
    below, above = y_ocean(even_y, ye_in, yo_in)
    left, right = x_ocean(even_x, xe_in, xe_in)
    extend_ocean(o_ref, left, right, ext_ref, 1)
    refraction_rates(ext_ref, below, above, rate_ref)
    stress_ref[...] = stress_of(n_ref, w_ref)
    inner_waves(n_ref, yh_ref, rate_ref, wet, tab_ref, shift_ref, ys_ref, acc_ref, exact)
    side = even_x.astype(jnp.int32)
    finish_near_half(n_ref, acc_ref, rate_ref, mask_ref, tab_ref, xe_in, True, side, exact)
    finish_far_half(n_ref, acc_ref, rate_ref, mask_ref, side, exact)
    write_rows(acc_ref, 2 * side, t_ref, block_ref, out_hbm, sems)


def last_kernel(n_ref, acc_in, o_ref, mask_ref, tab_ref, stress_ref, xe_in, xo_in, ye_in, yo_in, out_in,
                acc_ref, ocean_ref, out_hbm, ext_ref, rate_ref, t_ref, block_ref, sems):
    even_x, even_y = is_even("gx"), is_even("gy")
    below, above = y_ocean(even_y, ye_in, yo_in)
    left, right = x_ocean(even_x, xe_in, xo_in)
    extend_ocean(o_ref, left, right, ext_ref)
    refraction_rates(ext_ref, below, above, rate_ref)
    side = 1 - even_x.astype(jnp.int32)
    finish_near_half(n_ref, acc_ref, rate_ref, mask_ref, tab_ref, xo_in, inside("gx"), side, exact)
    finish_far_half(n_ref, acc_ref, rate_ref, mask_ref, side, exact)
    write_rows(acc_ref, 2 * side, t_ref, block_ref, out_hbm, sems)
    _, wet8 = wet_rows(mask_ref)
    advance_ocean(ext_ref, below, above, stress_ref[...], wet8, ocean_ref)


def swap(array, axis, odd):
    nx, ny = lax.axis_size("gx"), lax.axis_size("gy")
    pairs = []
    for i in range(nx):
        for j in range(ny):
            to = (i ^ 1, j) if axis == "gx" else (i, j ^ 1)
            if odd and axis == "gx":
                to = (((i + 1) ^ 1) - 1, j) if 0 < i < nx - 1 else (i, j ^ 1)
            if odd and axis == "gy":
                to = (i, ((j + 1) ^ 1) - 1) if 0 < j < ny - 1 else (i ^ 1, j)
            pairs.append((i * ny + j, to[0] * ny + to[1]))
    return lax.ppermute(array, ("gx", "gy"), pairs)


def call(kernel, outs, ins, scratch, params=None, any_in=(), any_out=(), aliases=None, moved=8):
    places = [HBM if i in any_in else VM for i in range(len(ins))]
    return pl.pallas_call(
        kernel,
        out_shape=[jax.ShapeDtypeStruct(shape, dtype) for shape, dtype in outs],
        in_specs=places,
        out_specs=[HBM if i in any_out else VM for i in range(len(outs))],
        scratch_shapes=scratch,
        compiler_params=params or PARAMS,
        input_output_aliases=aliases or {},
        cost_estimate=pl.CostEstimate(flops=0, bytes_accessed=moved * 1024 * 1024, transcendentals=0),
        name=kernel.__name__.removesuffix("_kernel"),
    )(*ins)


GRID = ((ROWS, NDIR, NF, LANES), F32)
XEDGE = ((XROWS, LANES), BF16)
YEDGE = ((YROWS, LANES), BF16)
DRIVE = ((16, LANES), F32)
RATES = ((NDIR, 8, LANES), F32)
YH = pltpu.VMEM((2, HALF * NF, LANES), BF16)
EXT = pltpu.VMEM((3, 8 * NZ, LANES), F32)
RATE = pltpu.VMEM(*RATES)
SHIFTED = pltpu.VMEM((ROWS, QUARTER * NF, 2 * LANES), F32)
EDGES = pltpu.VMEM((2, HALF, 8, LANES), F32)
TURNED = pltpu.VMEM((2, BINS, LANES), F32)
BLOCK = pltpu.VMEM((2, LANES, BINS), BF16)


def local(spectrum, ocean_state, sea_mask):
    ocean_shape = (ocean_state.shape, F32)
    edge_table = jnp.asarray(edge_tables(), dtype=BF16)
    speed = jnp.asarray(np.broadcast_to(SPEEDS[:, None], (NF, LANES)).copy())
    weights = jnp.asarray(stress_table(), dtype=BF16)
    shift_table = jnp.asarray(shift_tables(), dtype=BF16)
    (xo,) = call(
        first_kernel,
        (XEDGE,),
        (spectrum, ocean_state, sea_mask),
        [
            pltpu.VMEM((2, *spectrum.shape[1:]), BF16),
            pltpu.VMEM(ocean_state.shape, F32),
            pltpu.VMEM(sea_mask.shape, jnp.int32),
            TURNED,
            pltpu.SemaphoreType.DMA((4,)),
        ],
        FIRST,
        any_in=(0, 1, 2),
        moved=32,
    )
    xo = swap(xo, "gx", 1)
    n, xe, ye, yo, tab = call(
        start_kernel,
        (GRID, XEDGE, YEDGE, YEDGE, ((5, NDIR, NF, LANES), F32)),
        (spectrum, ocean_state, sea_mask, edge_table, speed),
        [pltpu.VMEM((ROWS, BINS, LANES), F32), EDGES],
    )
    xe = swap(xe, "gx", 0)
    ye = swap(ye, "gy", 0)
    yo = swap(yo, "gy", 1)
    acc, stress = call(
        inner_kernel,
        (GRID, DRIVE),
        (n, ocean_state, sea_mask, tab, weights, shift_table, ye, yo),
        [YH, EXT, RATE, SHIFTED],
    )
    acc, ocean, rate, xo2, xrow, ycol = call(
        send_kernel,
        (GRID, ocean_shape, RATES, XEDGE, ((OCEAN, LANES), F32), ((2, 8, LANES), F32)),
        (n, acc, ocean_state, sea_mask, stress, xe, xo, ye, yo),
        [EXT],
        aliases={1: 0},
    )
    xo2 = swap(xo2, "gx", 1)
    n, xe, ye, yo = call(
        rest_kernel,
        (GRID, XEDGE, YEDGE, YEDGE),
        (n, acc, sea_mask, tab, rate, edge_table, xrow, ycol, xe, xo),
        [EDGES],
        aliases={1: 0},
        moved=64,
    )
    xe = swap(xe, "gx", 0)
    ye = swap(ye, "gy", 0)
    yo = swap(yo, "gy", 1)
    acc, stress, out = call(
        inner_last_kernel,
        (GRID, DRIVE, (spectrum.shape, BF16)),
        (n, ocean, sea_mask, tab, weights, shift_table, xe, ye, yo),
        [YH, EXT, RATE, SHIFTED, TURNED, BLOCK, pltpu.SemaphoreType.DMA((2,))],
        any_out=(2,),
    )
    _, ocean, out = call(
        last_kernel,
        (GRID, ocean_shape, (spectrum.shape, BF16)),
        (n, acc, ocean, sea_mask, tab, stress, xe, xo2, ye, yo, out),
        [EXT, RATE, TURNED, BLOCK, pltpu.SemaphoreType.DMA((2,))],
        any_in=(10,),
        any_out=(2,),
        aliases={1: 0, 10: 2},
    )
    return out, ocean


def solution(mesh):
    placed = (P("gx", "gy", None), P(None, None, "gx", "gy"), P("gx", "gy"))
    return jax.shard_map(
        local,
        mesh=mesh,
        in_specs=placed,
        out_specs=(P("gx", "gy", None), P(None, None, "gx", "gy")),
        check_vma=False,
    )
```

time: 39.2 us -> 35.7 us (0.911)
  the two profiles are of different devices: /device:TPU:1 before, /device:TPU:0 now
where the time goes in v3:
time: 35.7 us; the launch traced here: 35.4 us
  Pallas kernels  15.5 us (43%)
  starting transfers between devices  8.87 us (25%)
  waiting for transfers between devices  7.01 us (20%)
  local copies, waits for them, and re-layouts  3.26 us (9%)
  between operations  0.75 us (2%)
    pallas_call x7, Pallas kernels, call(): pl.pallas_call(kernel, out_shape=[jax.ShapeDtypeStruct(shape, dtype) for...  15.5 us
    ppermute x8, starting transfers between devices, swap(): return lax.ppermute(array, ('gx', 'gy'), pairs)  8.87 us
    ppermute x8, waiting for transfers between devices, swap(): return lax.ppermute(array, ('gx', 'gy'), pairs)  7.01 us
    unnamed x16, local copies, waits for them, and re-layouts  3.26 us
  transfers between devices with their start and end apart: 8, of which 2 were waited for; matrix products, arithmetic and copies ran while one was open for 0% of the time, Pallas kernels for 23%

profile of v3, /device:TPU:0, one launch (start us, length us, event | category | flops | bytes accessed | tf_op | source)
XLA Modules:
  0.0 35.4 jit_solution(1608253896744533804)
XLA Ops:
  0.6 0.0 copy-start.3
  0.6 0.0 copy-start.4
  0.7 0.0 copy-start
  0.7 2.4 %first.1 = bf16[1248,128]{1,0:T(8,128)(2,1)} custom-call(bf16[4,128,1152]{2,1,0:T(8,128)(2,1)} %s_hbm.1, f32[3,16,4,128]{3,2,1,0:T(4,128)} %o_ref.5, s32[4,128]{1,0:T(4,128)} %mask_ref.11), custom_call_target="tpu_custom_call" | custom-call | bytes 33554432 | tf_op jit(solution)/shard_map/first/pallas_call | solution.py:537
  3.1 3.1 %collective-permute-start.3 = (bf16[1248,128]{1,0:T(8,128)(2,1)}, bf16[1248,128]{1,0:T(8,128)(2,1)S(1)}, u32[]{:S(2)}, u32[]{:S(2)}) collective-permute-start(bf16[1248,128]{1,0:T(8,128)(2,1)} %first.1), channel_id=1, source_target_pairs={{0,1},{1,0},{2,3},{3,2},{4,8},{5,9},{6,10},{7,11},{8,4},{9,5},{10,... | collective-permute-start | bytes 958472 | tf_op jit(solution)/shard_map/ppermute | solution.py:532
  6.2 0.0 copy-done
  6.2 0.9 %copy-done.1 = f32[3,16,4,128]{3,2,1,0:T(4,128)S(1)} copy-done((f32[3,16,4,128]{3,2,1,0:T(4,128)S(1)}, f32[3,16,4,128]{3,2,1,0:T(4,128)}, u32[]{:S(2)}) %copy-start.1) | copy-done | bytes 98328
  7.1 0.9 %copy-done.2 = bf16[2,512,128]{2,1,0:T(8,128)(2,1)S(1)} copy-done((bf16[2,512,128]{2,1,0:T(8,128)(2,1)S(1)}, bf16[2,512,128]{2,1,0:T(8,128)(2,1)}, u32[]{:S(2)}) %copy-start.2) | copy-done | bytes 262168
  8.0 0.7 %copy-done.5 = s32[4,128]{1,0:T(4,128)S(1)} copy-done((s32[4,128]{1,0:T(4,128)S(1)}, s32[4,128]{1,0:T(4,128)}, u32[]{:S(2)}) %copy-start.5) | copy-done | bytes 2072
  8.7 0.7 %copy-done.7 = f32[32,128]{1,0:T(8,128)S(1)} copy-done((f32[32,128]{1,0:T(8,128)S(1)}, f32[32,128]{1,0:T(8,128)}, u32[]{:S(2)}) %copy-start.7) | copy-done | bytes 16408
  9.4 1.4 %start.1 = (f32[4,36,32,128]{3,2,1,0:T(8,128)S(1)}, bf16[1248,128]{1,0:T(8,128)(2,1)S(1)}, bf16[160,128]{1,0:T(8,128)(2,1)S(1)}, bf16[160,128]{1,0:T(8,128)(2,1)S(1)}, f32[5,36,32,128]{3,2,1,0:T(8,128)S(1)}) custom-call(bf16[4,128,1152]{2,1,0:T(8,128)(2,1)S(1)} %copy-done, f32[3,16,4,128]{3,2,1,0:T(4,128)S(1)} %copy-done.1, s32[4,128]{1,0:T(4,128)S(1)} %copy-done.5, ...), custom_call_target="tpu_custom_call" | custom-call | bytes 8388608 | tf_op jit(solution)/shard_map/start/pallas_call | solution.py:537
  10.8 0.1 collective-permute-start.2
  10.9 1.6 %collective-permute-start = (bf16[160,128]{1,0:T(8,128)(2,1)S(1)}, bf16[160,128]{1,0:T(8,128)(2,1)S(1)}, u32[]{:S(2)}, u32[]{:S(2)}) collective-permute-start(bf16[160,128]{1,0:T(8,128)(2,1)S(1)} %get-tuple-element.26), channel_id=1, source_target_pairs={{0,1},{1,0},{2,3},{3,2},{4,5},{5,4},{6,7},{7,6},{8,9},{9,8},{10,11... | collective-permute-start | bytes 122888 | tf_op jit(solution)/shard_map/ppermute | solution.py:532
  12.4 0.0 collective-permute-start.1
  12.4 2.5 %collective-permute-done.ye_in = bf16[160,128]{1,0:T(8,128)(2,1)S(1)} collective-permute-done((bf16[160,128]{1,0:T(8,128)(2,1)S(1)}, bf16[160,128]{1,0:T(8,128)(2,1)S(1)}, u32[]{:S(2)}, u32[]{:S(2)}) %collective-permute-start) | collective-permute-done | bytes 40992 | tf_op jit(solution)/shard_map/ppermute | solution.py:532
  14.9 0.0 collective-permute-done.1.yo_in
  14.9 2.6 %inner.1 = (f32[4,36,32,128]{3,2,1,0:T(8,128)S(1)}, f32[16,128]{1,0:T(8,128)S(1)}) custom-call(f32[4,36,32,128]{3,2,1,0:T(8,128)S(1)} %get-tuple-element.24.n_ref, f32[3,16,4,128]{3,2,1,0:T(4,128)S(1)} %copy-done.1, s32[4,128]{1,0:T(4,128)S(1)} %copy-done.5, f32[5,36,32,128]{3,2,1,0:T(8,128)S(1)} %get-tuple-element.25.tab_ref, ...), custom_call_target="tpu_custom_call" | custom-call | bytes 8388608 | tf_op jit(solution)/shard_map/inner/pallas_call | solution.py:537
  17.5 0.0 collective-permute-done.3.xo_in
  17.5 0.0 collective-permute-done.2.xe_in
  17.5 0.7 %send.1 = (f32[4,36,32,128]{3,2,1,0:T(8,128)S(1)}, f32[3,16,4,128]{3,2,1,0:T(4,128)S(1)}, f32[36,8,128]{2,1,0:T(8,128)S(1)}, bf16[1248,128]{1,0:T(8,128)(2,1)S(1...) custom-call(f32[4,36,32,128]{3,2,1,0:T(8,128)S(1)} %get-tuple-element.24.n_ref, ...), custom_call_target="tpu_custom_call", output_to_operand_aliasing={{0}: (1, {})} | custom-call | bytes 8388608 | tf_op jit(solution)/shard_map/send/pallas_call | solution.py:537
  18.3 0.0 copy-start.6
  18.3 1.4 %rest.1 = (f32[4,36,32,128]{3,2,1,0:T(8,128)S(1)}, bf16[1248,128]{1,0:T(8,128)(2,1)S(1)}, bf16[160,128]{1,0:T(8,128)(2,1)S(1)}, bf16[160,128]{1,0:T(8,128)(2,1)S(1)}) custom-call(f32[4,36,32,128]{3,2,1,0:T(8,128)S(1)} %get-tuple-element.24.n_ref, f32[4,36,32,128]{3,2,1,0:T(8,128)S(1)} %get-tuple-element.31.acc_in, ...), custom_call_target="tpu_custom_call", output_to_operand_aliasing={{0}: (1, {})} | custom-call | bytes 67108864 | tf_op jit(solution)/shard_map/rest/pallas_call | solution.py:537
  19.7 0.1 collective-permute-start.4
  19.8 2.7 %collective-permute-start.7 = (bf16[1248,128]{1,0:T(8,128)(2,1)S(1)}, bf16[1248,128]{1,0:T(8,128)(2,1)S(1)}, u32[]{:S(2)}, u32[]{:S(2)}) collective-permute-start(bf16[1248,128]{1,0:T(8,128)(2,1)S(1)} %get-tuple-element.42), channel_id=1, source_target_pairs={{0,1},{1,0},{2,3},{3,2},{4,8},{5,9},{6,10},{7,11},{8,4},{9,5},{10,... | collective-permute-start | bytes 958472 | tf_op jit(solution)/shard_map/ppermute | solution.py:532
  22.5 0.1 collective-permute-start.5
  22.6 1.2 %collective-permute-start.6 = (bf16[160,128]{1,0:T(8,128)(2,1)S(1)}, bf16[160,128]{1,0:T(8,128)(2,1)S(1)}, u32[]{:S(2)}, u32[]{:S(2)}) collective-permute-start(bf16[160,128]{1,0:T(8,128)(2,1)S(1)} %get-tuple-element.39), channel_id=1, source_target_pairs={{0,4},{1,2},{2,1},{3,7},{4,0},{5,6},{6,5},{7,3},{8,12},{9,10},{10,... | collective-permute-start | bytes 122888 | tf_op jit(solution)/shard_map/ppermute | solution.py:532
  23.8 4.5 %collective-permute-done.5.ye_in = bf16[160,128]{1,0:T(8,128)(2,1)S(1)} collective-permute-done((bf16[160,128]{1,0:T(8,128)(2,1)S(1)}, bf16[160,128]{1,0:T(8,128)(2,1)S(1)}, u32[]{:S(2)}, u32[]{:S(2)}) %collective-permute-start.5) | collective-permute-done | bytes 40992 | tf_op jit(solution)/shard_map/ppermute | solution.py:532
  28.4 0.0 collective-permute-done.6.yo_in
  28.4 0.0 collective-permute-done.4.xe_in
  28.4 4.2 %inner_last.1 = (f32[4,36,32,128]{3,2,1,0:T(8,128)S(1)}, f32[16,128]{1,0:T(8,128)S(1)}, bf16[4,128,1152]{2,1,0:T(8,128)(2,1)}) custom-call(f32[4,36,32,128]{3,2,1,0:T(8,128)S(1)} %get-tuple-element.35.n_ref, f32[3,16,4,128]{3,2,1,0:T(4,128)S(1)} %get-tuple-element.36.o_ref, s32[4,128]{1,0:T(4,128)S(1)} %copy-done.6, ...), custom_call_target="tpu_custom_call" | custom-call | bytes 8388608 | tf_op jit(solution)/shard_map/inner_last/pallas_call | solution.py:537
  32.6 0.0 collective-permute-done.7.xo_in
  32.6 2.8 %last.1 = (f32[4,36,32,128]{3,2,1,0:T(8,128)S(1)}, f32[3,16,4,128]{3,2,1,0:T(4,128)}, bf16[4,128,1152]{2,1,0:T(8,128)(2,1)}) custom-call(f32[4,36,32,128]{3,2,1,0:T(8,128)S(1)} %get-tuple-element.35.n_ref, f32[4,36,32,128]{3,2,1,0:T(8,128)S(1)} %get-tuple-element.40.acc_in, ...), custom_call_target="tpu_custom_call", output_to_operand_aliasing={{0}: (1, {}), {2}: (10, {})} | custom-call | bytes 8388608 | tf_op jit(solution)/shard_map/last/pallas_call | solution.py:537
  (7 shorter events, 0.0 us)
Async XLA Ops:
  0.6 14.3 %copy-start.3 = (bf16[2,256,256]{2,1,0:T(8,128)(2,1)S(1)}, bf16[2,256,256]{2,1,0:T(8,128)(2,1)}, u32[]{:S(2)}) copy-start(bf16[2,256,256]{2,1,0:T(8,128)(2,1)} %constant.11.clone.shift_ref) | copy-start | bytes 786436
  0.6 14.3 %copy-start.4 = (bf16[4,16,1152]{2,1,0:T(8,128)(2,1)S(1)}, bf16[4,16,1152]{2,1,0:T(8,128)(2,1)}, u32[]{:S(2)}) copy-start(bf16[4,16,1152]{2,1,0:T(8,128)(2,1)} %constant.10.clone.w_ref) | copy-start | bytes 442372
  0.7 5.5 %copy-start = (bf16[4,128,1152]{2,1,0:T(8,128)(2,1)S(1)}, bf16[4,128,1152]{2,1,0:T(8,128)(2,1)}, u32[]{:S(2)}) copy-start(bf16[4,128,1152]{2,1,0:T(8,128)(2,1)} %s_hbm.1) | copy-start | bytes 3538948
  3.1 14.5 %collective-permute-start.3 = (bf16[1248,128]{1,0:T(8,128)(2,1)}, bf16[1248,128]{1,0:T(8,128)(2,1)S(1)}, u32[]{:S(2)}, u32[]{:S(2)}) collective-permute-start(bf16[1248,128]{1,0:T(8,128)(2,1)} %first.1), channel_id=1, source_target_pairs={{0,1},{1,0},{2,3},{3,2},{4,8},{5,9},{6,10},{7,11},{8,4},{9,5},{10,... | collective-permute-start | bytes 958472 | tf_op jit(solution)/shard_map/ppermute | solution.py:532
  6.2 0.9 %copy-start.1 = (f32[3,16,4,128]{3,2,1,0:T(4,128)S(1)}, f32[3,16,4,128]{3,2,1,0:T(4,128)}, u32[]{:S(2)}) copy-start(f32[3,16,4,128]{3,2,1,0:T(4,128)} %o_ref.5) | copy-start | bytes 294916
  7.1 0.9 %copy-start.2 = (bf16[2,512,128]{2,1,0:T(8,128)(2,1)S(1)}, bf16[2,512,128]{2,1,0:T(8,128)(2,1)}, u32[]{:S(2)}) copy-start(bf16[2,512,128]{2,1,0:T(8,128)(2,1)} %constant.8.clone.edge_ref) | copy-start | bytes 786436
  8.0 0.7 %copy-start.5 = (s32[4,128]{1,0:T(4,128)S(1)}, s32[4,128]{1,0:T(4,128)}, u32[]{:S(2)}) copy-start(s32[4,128]{1,0:T(4,128)} %mask_ref.11) | copy-start | bytes 6148
  8.7 0.7 %copy-start.7 = (f32[32,128]{1,0:T(8,128)S(1)}, f32[32,128]{1,0:T(8,128)}, u32[]{:S(2)}) copy-start(f32[32,128]{1,0:T(8,128)} %constant.9.clone.speed_ref) | copy-start | bytes 49156
  10.8 6.8 %collective-permute-start.2 = (bf16[1248,128]{1,0:T(8,128)(2,1)S(1)}, bf16[1248,128]{1,0:T(8,128)(2,1)S(1)}, u32[]{:S(2)}, u32[]{:S(2)}) collective-permute-start(bf16[1248,128]{1,0:T(8,128)(2,1)S(1)} %get-tuple-element.30), channel_id=1, source_target_pairs={{0,4},{1,5},{2,6},{3,7},{4,0},{5,1},{6,2},{7,3},{8,12},{9,13},{10,... | collective-permute-start | bytes 958472 | tf_op jit(solution)/shard_map/ppermute | solution.py:532
  10.9 4.1 %collective-permute-start = (bf16[160,128]{1,0:T(8,128)(2,1)S(1)}, bf16[160,128]{1,0:T(8,128)(2,1)S(1)}, u32[]{:S(2)}, u32[]{:S(2)}) collective-permute-start(bf16[160,128]{1,0:T(8,128)(2,1)S(1)} %get-tuple-element.26), channel_id=1, source_target_pairs={{0,1},{1,0},{2,3},{3,2},{4,5},{5,4},{6,7},{7,6},{8,9},{9,8},{10,11... | collective-permute-start | bytes 122888 | tf_op jit(solution)/shard_map/ppermute | solution.py:532
  12.4 2.5 %collective-permute-start.1 = (bf16[160,128]{1,0:T(8,128)(2,1)S(1)}, bf16[160,128]{1,0:T(8,128)(2,1)S(1)}, u32[]{:S(2)}, u32[]{:S(2)}) collective-permute-start(bf16[160,128]{1,0:T(8,128)(2,1)S(1)} %get-tuple-element.27), channel_id=1, source_target_pairs={{0,4},{1,2},{2,1},{3,7},{4,0},{5,6},{6,5},{7,3},{8,12},{9,10},{10,... | collective-permute-start | bytes 122888 | tf_op jit(solution)/shard_map/ppermute | solution.py:532
  18.3 10.1 %copy-start.6 = (s32[4,128]{1,0:T(4,128)S(1)}, s32[4,128]{1,0:T(4,128)}, u32[]{:S(2)}) copy-start(s32[4,128]{1,0:T(4,128)} %mask_ref.11) | copy-start | bytes 6148
  19.7 8.7 %collective-permute-start.4 = (bf16[1248,128]{1,0:T(8,128)(2,1)S(1)}, bf16[1248,128]{1,0:T(8,128)(2,1)S(1)}, u32[]{:S(2)}, u32[]{:S(2)}) collective-permute-start(bf16[1248,128]{1,0:T(8,128)(2,1)S(1)} %get-tuple-element.37), channel_id=1, source_target_pairs={{0,4},{1,5},{2,6},{3,7},{4,0},{5,1},{6,2},{7,3},{8,12},{9,13},{10,... | collective-permute-start | bytes 958472 | tf_op jit(solution)/shard_map/ppermute | solution.py:532
  19.8 12.8 %collective-permute-start.7 = (bf16[1248,128]{1,0:T(8,128)(2,1)S(1)}, bf16[1248,128]{1,0:T(8,128)(2,1)S(1)}, u32[]{:S(2)}, u32[]{:S(2)}) collective-permute-start(bf16[1248,128]{1,0:T(8,128)(2,1)S(1)} %get-tuple-element.42), channel_id=1, source_target_pairs={{0,1},{1,0},{2,3},{3,2},{4,8},{5,9},{6,10},{7,11},{8,4},{9,5},{10,... | collective-permute-start | bytes 958472 | tf_op jit(solution)/shard_map/ppermute | solution.py:532
  22.5 5.8 %collective-permute-start.5 = (bf16[160,128]{1,0:T(8,128)(2,1)S(1)}, bf16[160,128]{1,0:T(8,128)(2,1)S(1)}, u32[]{:S(2)}, u32[]{:S(2)}) collective-permute-start(bf16[160,128]{1,0:T(8,128)(2,1)S(1)} %get-tuple-element.38), channel_id=1, source_target_pairs={{0,1},{1,0},{2,3},{3,2},{4,5},{5,4},{6,7},{7,6},{8,9},{9,8},{10,11... | collective-permute-start | bytes 122888 | tf_op jit(solution)/shard_map/ppermute | solution.py:532
  22.6 5.8 %collective-permute-start.6 = (bf16[160,128]{1,0:T(8,128)(2,1)S(1)}, bf16[160,128]{1,0:T(8,128)(2,1)S(1)}, u32[]{:S(2)}, u32[]{:S(2)}) collective-permute-start(bf16[160,128]{1,0:T(8,128)(2,1)S(1)} %get-tuple-element.39), channel_id=1, source_target_pairs={{0,4},{1,2},{2,1},{3,7},{4,0},{5,6},{6,5},{7,3},{8,12},{9,10},{10,... | collective-permute-start | bytes 122888 | tf_op jit(solution)/shard_map/ppermute | solution.py:532

commit v4 on v3

--- a/solution.py
+++ b/solution.py
@@ -78,14 +78,13 @@
     return lax.broadcasted_iota(jnp.int32, shape, len(shape) - 1)
 
 
-def edge_tables():
-    table = np.zeros((2, ROWS, LANES, LANES), np.float32)
+def make_edge_tables(table_ref):
+    source = lax.broadcasted_iota(jnp.int32, (LANES, LANES), 0)
+    lane = lane_of((LANES, LANES)) % 8
     for side, start in enumerate((0, LANES - 2)):
         for x in range(ROWS):
-            for g in range(4):
-                for j in range(2):
-                    table[side, x, start + j, 8 * g + 2 * x + j] = 1.0
-    return table.reshape(2, ROWS * LANES, LANES)
+            found = (lane == source + (2 * x - start)) & (lane >= 2 * x) & (lane < 2 * x + 2)
+            table_ref[side, LANES * x : LANES * (x + 1), :] = jnp.where(found, 1.0, 0.0).astype(BF16)
 
 
 def shift_tables():
@@ -177,14 +176,14 @@
             xo_ref[at, :] = (t_ref[r, pl.ds(first + kk, NF, stride=NDIR), :] * wet).astype(BF16)
             return carry
 
-        lax.fori_loop(0, HALF, body, 0, unroll=2)
+        lax.fori_loop(0, HALF, body, 0, unroll=6)
     copies[3].wait()
     rows = tuple(o_ref[:, :, r, :].reshape(OCEAN, LANES) for r in (0, ROWS - 1))
     send_ocean_row(rows, xo_ref, low_side)
 
 
-def start_kernel(s_ref, o_ref, mask_ref, edge_ref, speed_ref,
-                 n_ref, xe_ref, ye_ref, yo_ref, tab_ref, t_ref, e_ref):
+def start_kernel(s_ref, o_ref, mask_ref,
+                 n_ref, xe_ref, ye_ref, yo_ref, tab_ref, edge_ref, t_ref, e_ref):
     wet = mask_ref[...].astype(F32)
     for x in range(ROWS):
         t_ref[x] = jnp.transpose(s_ref[x].astype(F32))
@@ -194,10 +193,11 @@
             n_ref[x, k] = t_ref[x, pl.ds(k, NF, stride=NDIR), :] * wet[x : x + 1]
         return carry
 
-    lax.fori_loop(0, NDIR, body, 0, unroll=2)
+    lax.fori_loop(0, NDIR, body, 0, unroll=6)
     even_x, even_y = is_even("gx"), is_even("gy")
     rows = tuple(o_ref[:, :, r, :].reshape(OCEAN, LANES) for r in (0, ROWS - 1))
     send_x(n_ref, rows, xe_ref, jnp.logical_not(even_x))
+    make_edge_tables(edge_ref)
     for quarter in range(4):
         pack_y_edges(n_ref, quarter, edge_ref, e_ref)
     pad = jnp.zeros((1, LANES), F32)
@@ -209,11 +209,18 @@
     ]
     first, last = pack_ocean_columns(blocks, lane_of((8, LANES)))
     send_y(e_ref, first, last, even_y, (ye_ref, yo_ref))
-    make_tables(speed_ref, tab_ref)
-
-
-def make_tables(speed_ref, tab_ref):
-    speed = speed_ref[...]
+    make_tables(tab_ref)
+
+
+def make_tables(tab_ref):
+    row = lax.broadcasted_iota(jnp.int32, (8, LANES), 0)
+    blocks = []
+    for g in range(4):
+        block = jnp.full((8, LANES), float(SPEEDS[8 * g]), F32)
+        for i in range(1, 8):
+            block = jnp.where(row == i, float(SPEEDS[8 * g + i]), block)
+        blocks.append(block)
+    speed = jnp.concatenate(blocks, 0)
     for k in range(NDIR):
         cx, cy = speed * abs(float(COS[k])), speed * abs(float(SIN[k]))
         near_x, far_x = cx * (2.0 - cx), (0.5 * cx) * (cx - 1.0)
@@ -370,7 +377,7 @@
                 acc_ref[x, k] = total
             return carry
 
-        lax.fori_loop(0, QUARTER, body, 0)
+        lax.fori_loop(0, QUARTER, body, 0, unroll=QUARTER)
 
 
 def wet_row(mask_ref, x):
@@ -387,7 +394,7 @@
         acc_ref[x, k] = keep(wet * (acc_ref[x, k] + refraction(n_ref, rate_ref, x, k)))
         return carry
 
-    lax.fori_loop(0, HALF, body, 0, unroll=2)
+    lax.fori_loop(0, HALF, body, 0, unroll=6)
 
 
 def finish_near_half(n_ref, acc_ref, rate_ref, mask_ref, tab_ref, halo_ref, known, side, keep):
@@ -405,7 +412,7 @@
         acc_ref[inner, k] = keep(wet_inner * (acc_ref[inner, k] + near * tab_ref[2, k]))
         return carry
 
-    lax.fori_loop(0, HALF, body, 0, unroll=2)
+    lax.fori_loop(0, HALF, body, 0, unroll=6)
 
 
 def rounded(v):
@@ -451,6 +458,7 @@
         for r in (1, ROWS)
     )
     send_x(acc_ref, rows, xo_ref, even_x)
+    xo_ref[XROWS:, :] = jnp.zeros((16, LANES), BF16)
     xrow_ref[...] = jnp.where(even_x, rows[1], rows[0])
     ycol_ref[0], ycol_ref[1] = pack_ocean_columns(new, lane_of((8, LANES)))
 
@@ -477,10 +485,14 @@
             t_ref[r, pl.ds(k, NF, stride=NDIR), :] = acc_ref[first + r, k]
             return carry
 
-        lax.fori_loop(0, NDIR, body, 0, unroll=2)
+        lax.fori_loop(0, NDIR, body, 0, unroll=6)
         block_ref[r] = jnp.transpose(t_ref[r]).astype(BF16)
         copies.append(pltpu.make_async_copy(block_ref.at[r], out_hbm.at[first + r], sems.at[r]))
         copies[-1].start()
+    return copies
+
+
+def wait_all(copies):
     for copy in copies:
         copy.wait()
 
@@ -495,12 +507,13 @@
     left, right = x_ocean(even_x, xe_in, xe_in)
     extend_ocean(o_ref, left, right, ext_ref, 1)
     refraction_rates(ext_ref, below, above, rate_ref)
-    stress_ref[...] = stress_of(n_ref, w_ref)
     inner_waves(n_ref, yh_ref, rate_ref, wet, tab_ref, shift_ref, ys_ref, acc_ref, exact)
     side = even_x.astype(jnp.int32)
     finish_near_half(n_ref, acc_ref, rate_ref, mask_ref, tab_ref, xe_in, True, side, exact)
     finish_far_half(n_ref, acc_ref, rate_ref, mask_ref, side, exact)
-    write_rows(acc_ref, 2 * side, t_ref, block_ref, out_hbm, sems)
+    copies = write_rows(acc_ref, 2 * side, t_ref, block_ref, out_hbm, sems)
+    stress_ref[...] = stress_of(n_ref, w_ref)
+    wait_all(copies)
 
 
 def last_kernel(n_ref, acc_in, o_ref, mask_ref, tab_ref, stress_ref, xe_in, xo_in, ye_in, yo_in, out_in,
@@ -513,9 +526,10 @@
     side = 1 - even_x.astype(jnp.int32)
     finish_near_half(n_ref, acc_ref, rate_ref, mask_ref, tab_ref, xo_in, inside("gx"), side, exact)
     finish_far_half(n_ref, acc_ref, rate_ref, mask_ref, side, exact)
-    write_rows(acc_ref, 2 * side, t_ref, block_ref, out_hbm, sems)
+    copies = write_rows(acc_ref, 2 * side, t_ref, block_ref, out_hbm, sems)
     _, wet8 = wet_rows(mask_ref)
     advance_ocean(ext_ref, below, above, stress_ref[...], wet8, ocean_ref)
+    wait_all(copies)
 
 
 def swap(array, axis, odd):
@@ -532,7 +546,7 @@
     return lax.ppermute(array, ("gx", "gy"), pairs)
 
 
-def call(kernel, outs, ins, scratch, params=None, any_in=(), any_out=(), aliases=None, moved=8):
+def call(kernel, outs, ins, scratch, params=None, any_in=(), any_out=(), aliases=None, moved=0):
     places = [HBM if i in any_in else VM for i in range(len(ins))]
     return pl.pallas_call(
         kernel,
@@ -549,6 +563,7 @@
 
 GRID = ((ROWS, NDIR, NF, LANES), F32)
 XEDGE = ((XROWS, LANES), BF16)
+XLONG = ((XROWS + 16, LANES), BF16)
 YEDGE = ((YROWS, LANES), BF16)
 DRIVE = ((16, LANES), F32)
 RATES = ((NDIR, 8, LANES), F32)
@@ -563,8 +578,6 @@
 
 def local(spectrum, ocean_state, sea_mask):
     ocean_shape = (ocean_state.shape, F32)
-    edge_table = jnp.asarray(edge_tables(), dtype=BF16)
-    speed = jnp.asarray(np.broadcast_to(SPEEDS[:, None], (NF, LANES)).copy())
     weights = jnp.asarray(stress_table(), dtype=BF16)
     shift_table = jnp.asarray(shift_tables(), dtype=BF16)
     (xo,) = call(
@@ -583,10 +596,10 @@
         moved=32,
     )
     xo = swap(xo, "gx", 1)
-    n, xe, ye, yo, tab = call(
+    n, xe, ye, yo, tab, edge_table = call(
         start_kernel,
-        (GRID, XEDGE, YEDGE, YEDGE, ((5, NDIR, NF, LANES), F32)),
-        (spectrum, ocean_state, sea_mask, edge_table, speed),
+        (GRID, XEDGE, YEDGE, YEDGE, ((5, NDIR, NF, LANES), F32), ((2, ROWS * LANES, LANES), BF16)),
+        (spectrum, ocean_state, sea_mask),
         [pltpu.VMEM((ROWS, BINS, LANES), F32), EDGES],
     )
     xe = swap(xe, "gx", 0)
@@ -600,7 +613,7 @@
     )
     acc, ocean, rate, xo2, xrow, ycol = call(
         send_kernel,
-        (GRID, ocean_shape, RATES, XEDGE, ((OCEAN, LANES), F32), ((2, 8, LANES), F32)),
+        (GRID, ocean_shape, RATES, XLONG, ((OCEAN, LANES), F32), ((2, 8, LANES), F32)),
         (n, acc, ocean_state, sea_mask, stress, xe, xo, ye, yo),
         [EXT],
         aliases={1: 0},
@@ -612,7 +625,6 @@
         (n, acc, sea_mask, tab, rate, edge_table, xrow, ycol, xe, xo),
         [EDGES],
         aliases={1: 0},
-        moved=64,
     )
     xe = swap(xe, "gx", 0)
     ye = swap(ye, "gy", 0)

time: 35.7 us -> 29.6 us (0.83)
  Pallas kernels: 15.5 us -> 12.5 us
  local copies, waits for them, and re-layouts: 3.26 us -> 1.6 us
  waiting for transfers between devices: 7.01 us -> 5.47 us
    pallas_call x7, Pallas kernels: 15.5 us -> 12.5 us  [call(): pl.pallas_call(kernel, out_shape=[jax.ShapeDtypeStruct(shape, dtype) for...]
    unnamed x16 -> x12, local copies, waits for them, and re-layouts: 3.26 us -> 1.6 us
    ppermute x8, waiting for transfers between devices: 7.01 us -> 5.47 us  [swap(): return lax.ppermute(array, ('gx', 'gy'), pairs)]
  transfers between devices with their start and end apart: 8 -> 8, of which waited for: 2 -> 2; matrix products, arithmetic and copies ran while one was open for 0% -> 0% of each run, Pallas kernels for 23% -> 24%
where the time goes in v4:
time: 29.6 us; the launch traced here: 29.4 us
  Pallas kernels  12.5 us (42%)
  starting transfers between devices  9.12 us (31%)
  waiting for transfers between devices  5.47 us (18%)
  local copies, waits for them, and re-layouts  1.6 us (5%)
  between operations  0.74 us (2%)
    pallas_call x7, Pallas kernels, call(): pl.pallas_call(kernel, out_shape=[jax.ShapeDtypeStruct(shape, dtype) for...  12.5 us
    ppermute x8, starting transfers between devices, swap(): return lax.ppermute(array, ('gx', 'gy'), pairs)  9.12 us
    ppermute x8, waiting for transfers between devices, swap(): return lax.ppermute(array, ('gx', 'gy'), pairs)  5.47 us
    unnamed x12, local copies, waits for them, and re-layouts  1.6 us
  transfers between devices with their start and end apart: 8, of which 2 were waited for; matrix products, arithmetic and copies ran while one was open for 0% of the time, Pallas kernels for 24%

profile of v4, /device:TPU:0, one launch (start us, length us, event | category | flops | bytes accessed | tf_op | source)
XLA Modules:
  0.0 29.4 jit_solution(6171059863037808016)
XLA Ops:
  0.6 0.0 copy-start.2
  0.6 0.0 copy-start.3
  0.7 0.0 copy-start
  0.7 2.3 %first.1 = bf16[1248,128]{1,0:T(8,128)(2,1)} custom-call(bf16[4,128,1152]{2,1,0:T(8,128)(2,1)} %s_hbm.1, f32[3,16,4,128]{3,2,1,0:T(4,128)} %o_ref.5, s32[4,128]{1,0:T(4,128)} %mask_ref.11), custom_call_target="tpu_custom_call" | custom-call | bytes 33554432 | tf_op jit(solution)/shard_map/first/pallas_call | solution.py:551
  3.0 3.1 %collective-permute-start.3 = (bf16[1248,128]{1,0:T(8,128)(2,1)}, bf16[1248,128]{1,0:T(8,128)(2,1)S(1)}, u32[]{:S(2)}, u32[]{:S(2)}) collective-permute-start(bf16[1248,128]{1,0:T(8,128)(2,1)} %first.1), channel_id=1, source_target_pairs={{0,1},{1,0},{2,3},{3,2},{4,8},{5,9},{6,10},{7,11},{8,4},{9,5},{10,... | collective-permute-start | bytes 958472 | tf_op jit(solution)/shard_map/ppermute | solution.py:546
  6.1 0.0 copy-done
  6.1 0.9 %copy-done.1 = f32[3,16,4,128]{3,2,1,0:T(4,128)S(1)} copy-done((f32[3,16,4,128]{3,2,1,0:T(4,128)S(1)}, f32[3,16,4,128]{3,2,1,0:T(4,128)}, u32[]{:S(2)}) %copy-start.1) | copy-done | bytes 98328
  7.0 0.7 %copy-done.4 = s32[4,128]{1,0:T(4,128)S(1)} copy-done((s32[4,128]{1,0:T(4,128)S(1)}, s32[4,128]{1,0:T(4,128)}, u32[]{:S(2)}) %copy-start.4) | copy-done | bytes 2072
  7.7 1.3 %start.1 = (f32[4,36,32,128]{3,2,1,0:T(8,128)S(1)}, bf16[1248,128]{1,0:T(8,128)(2,1)S(1)}, bf16[160,128]{1,0:T(8,128)(2,1)S(1)}, bf16[160,128]{1,0:T(8,128)(2,1)...) custom-call(bf16[4,128,1152]{2,1,0:T(8,128)(2,1)S(1)} %copy-done, ...), custom_call_target="tpu_custom_call" | custom-call | tf_op jit(solution)/shard_map/start/pallas_call | solution.py:551
  9.0 0.1 collective-permute-start.2
  9.1 1.6 %collective-permute-start = (bf16[160,128]{1,0:T(8,128)(2,1)S(1)}, bf16[160,128]{1,0:T(8,128)(2,1)S(1)}, u32[]{:S(2)}, u32[]{:S(2)}) collective-permute-start(bf16[160,128]{1,0:T(8,128)(2,1)S(1)} %get-tuple-element.27), channel_id=1, source_target_pairs={{0,1},{1,0},{2,3},{3,2},{4,5},{5,4},{6,7},{7,6},{8,9},{9,8},{10,11... | collective-permute-start | bytes 122888 | tf_op jit(solution)/shard_map/ppermute | solution.py:546
  10.6 0.0 collective-permute-start.1
  10.6 2.5 %collective-permute-done.ye_in = bf16[160,128]{1,0:T(8,128)(2,1)S(1)} collective-permute-done((bf16[160,128]{1,0:T(8,128)(2,1)S(1)}, bf16[160,128]{1,0:T(8,128)(2,1)S(1)}, u32[]{:S(2)}, u32[]{:S(2)}) %collective-permute-start) | collective-permute-done | bytes 40992 | tf_op jit(solution)/shard_map/ppermute | solution.py:546
  13.1 0.0 collective-permute-done.1.yo_in
  13.1 0.0 copy-done.2
  13.1 0.0 copy-done.3
  13.1 0.0 copy-start.5
  13.1 1.6 %inner.1 = (f32[4,36,32,128]{3,2,1,0:T(8,128)S(1)}, f32[16,128]{1,0:T(8,128)S(1)}) custom-call(f32[4,36,32,128]{3,2,1,0:T(8,128)S(1)} %get-tuple-element.25.n_ref, f32[3,16,4,128]{3,2,1,0:T(4,128)S(1)} %copy-done.1, s32[4,128]{1,0:T(4,128)S(1)} %copy-done.4, f32[5,36,32,128]{3,2,1,0:T(8,128)S(1)} %get-tuple-element.26.tab_ref, ...), custom_call_target="tpu_custom_call" | custom-call | tf_op jit(solution)/shard_map/inner/pallas_call | solution.py:551
  14.8 0.0 collective-permute-done.3.xo_in
  14.8 0.0 collective-permute-done.2.xe_in
  14.8 0.7 %send.1 = (f32[4,36,32,128]{3,2,1,0:T(8,128)S(1)}, f32[3,16,4,128]{3,2,1,0:T(4,128)S(1)}, f32[36,8,128]{2,1,0:T(8,128)S(1)}, bf16[1264,128]{1,0:T(8,128)(2,1)S(1...) custom-call(f32[4,36,32,128]{3,2,1,0:T(8,128)S(1)} %get-tuple-element.25.n_ref, ...), custom_call_target="tpu_custom_call", output_to_operand_aliasing={{0}: (1, {})} | custom-call | tf_op jit(solution)/shard_map/send/pallas_call | solution.py:551
  15.5 2.7 %collective-permute-start.7 = (bf16[1264,128]{1,0:T(8,128)(2,1)S(1)}, bf16[1264,128]{1,0:T(8,128)(2,1)S(1)}, u32[]{:S(2)}, u32[]{:S(2)}) collective-permute-start(bf16[1264,128]{1,0:T(8,128)(2,1)S(1)} %get-tuple-element.44), channel_id=1, source_target_pairs={{0,1},{1,0},{2,3},{3,2},{4,8},{5,9},{6,10},{7,11},{8,4},{9,5},{10,... | collective-permute-start | bytes 970760 | tf_op jit(solution)/shard_map/ppermute | solution.py:546
  18.2 1.2 %rest.1 = (f32[4,36,32,128]{3,2,1,0:T(8,128)S(1)}, bf16[1248,128]{1,0:T(8,128)(2,1)S(1)}, bf16[160,128]{1,0:T(8,128)(2,1)S(1)}, bf16[160,128]{1,0:T(8,128)(2,1)S(1)}) custom-call(f32[4,36,32,128]{3,2,1,0:T(8,128)S(1)} %get-tuple-element.25.n_ref, f32[4,36,32,128]{3,2,1,0:T(8,128)S(1)} %get-tuple-element.32.acc_in, ...), custom_call_target="tpu_custom_call", output_to_operand_aliasing={{0}: (1, {})} | custom-call | tf_op jit(solution)/shard_map/rest/pallas_call | solution.py:551
  19.4 0.1 collective-permute-start.4
  19.5 1.6 %collective-permute-start.5 = (bf16[160,128]{1,0:T(8,128)(2,1)S(1)}, bf16[160,128]{1,0:T(8,128)(2,1)S(1)}, u32[]{:S(2)}, u32[]{:S(2)}) collective-permute-start(bf16[160,128]{1,0:T(8,128)(2,1)S(1)} %get-tuple-element.40), channel_id=1, source_target_pairs={{0,1},{1,0},{2,3},{3,2},{4,5},{5,4},{6,7},{7,6},{8,9},{9,8},{10,11... | collective-permute-start | bytes 122888 | tf_op jit(solution)/shard_map/ppermute | solution.py:546
  21.1 0.0 collective-permute-start.6
  21.1 3.0 %collective-permute-done.5.ye_in = bf16[160,128]{1,0:T(8,128)(2,1)S(1)} collective-permute-done((bf16[160,128]{1,0:T(8,128)(2,1)S(1)}, bf16[160,128]{1,0:T(8,128)(2,1)S(1)}, u32[]{:S(2)}, u32[]{:S(2)}) %collective-permute-start.5) | collective-permute-done | bytes 40992 | tf_op jit(solution)/shard_map/ppermute | solution.py:546
  24.0 0.0 collective-permute-done.6.yo_in
  24.1 0.0 collective-permute-done.4.xe_in
  24.1 2.9 %inner_last.1 = (f32[4,36,32,128]{3,2,1,0:T(8,128)S(1)}, f32[16,128]{1,0:T(8,128)S(1)}, bf16[4,128,1152]{2,1,0:T(8,128)(2,1)}) custom-call(f32[4,36,32,128]{3,2,1,0:T(8,128)S(1)} %get-tuple-element.37.n_ref, f32[3,16,4,128]{3,2,1,0:T(4,128)S(1)} %get-tuple-element.38.o_ref, s32[4,128]{1,0:T(4,128)S(1)} %copy-done.5, ...), custom_call_target="tpu_custom_call" | custom-call | tf_op jit(solution)/shard_map/inner_last/pallas_call | solution.py:551
  26.9 0.0 collective-permute-done.7.xo_in
  26.9 2.5 %last.1 = (f32[4,36,32,128]{3,2,1,0:T(8,128)S(1)}, f32[3,16,4,128]{3,2,1,0:T(4,128)}, bf16[4,128,1152]{2,1,0:T(8,128)(2,1)}) custom-call(f32[4,36,32,128]{3,2,1,0:T(8,128)S(1)} %get-tuple-element.37.n_ref, f32[4,36,32,128]{3,2,1,0:T(8,128)S(1)} %get-tuple-element.42.acc_in, ...), custom_call_target="tpu_custom_call", output_to_operand_aliasing={{0}: (1, {}), {2}: (10, {})} | custom-call | tf_op jit(solution)/shard_map/last/pallas_call | solution.py:551
  (3 shorter events, 0.0 us)
Async XLA Ops:
  0.6 12.5 %copy-start.2 = (bf16[2,256,256]{2,1,0:T(8,128)(2,1)S(1)}, bf16[2,256,256]{2,1,0:T(8,128)(2,1)}, u32[]{:S(2)}) copy-start(bf16[2,256,256]{2,1,0:T(8,128)(2,1)} %constant.5.clone.shift_ref) | copy-start | bytes 786436
  0.6 12.5 %copy-start.3 = (bf16[4,16,1152]{2,1,0:T(8,128)(2,1)S(1)}, bf16[4,16,1152]{2,1,0:T(8,128)(2,1)}, u32[]{:S(2)}) copy-start(bf16[4,16,1152]{2,1,0:T(8,128)(2,1)} %constant.4.clone.w_ref) | copy-start | bytes 442372
  0.7 5.4 %copy-start = (bf16[4,128,1152]{2,1,0:T(8,128)(2,1)S(1)}, bf16[4,128,1152]{2,1,0:T(8,128)(2,1)}, u32[]{:S(2)}) copy-start(bf16[4,128,1152]{2,1,0:T(8,128)(2,1)} %s_hbm.1) | copy-start | bytes 3538948
  3.0 11.8 %collective-permute-start.3 = (bf16[1248,128]{1,0:T(8,128)(2,1)}, bf16[1248,128]{1,0:T(8,128)(2,1)S(1)}, u32[]{:S(2)}, u32[]{:S(2)}) collective-permute-start(bf16[1248,128]{1,0:T(8,128)(2,1)} %first.1), channel_id=1, source_target_pairs={{0,1},{1,0},{2,3},{3,2},{4,8},{5,9},{6,10},{7,11},{8,4},{9,5},{10,... | collective-permute-start | bytes 958472 | tf_op jit(solution)/shard_map/ppermute | solution.py:546
  6.1 0.9 %copy-start.1 = (f32[3,16,4,128]{3,2,1,0:T(4,128)S(1)}, f32[3,16,4,128]{3,2,1,0:T(4,128)}, u32[]{:S(2)}) copy-start(f32[3,16,4,128]{3,2,1,0:T(4,128)} %o_ref.5) | copy-start | bytes 294916
  7.0 0.7 %copy-start.4 = (s32[4,128]{1,0:T(4,128)S(1)}, s32[4,128]{1,0:T(4,128)}, u32[]{:S(2)}) copy-start(s32[4,128]{1,0:T(4,128)} %mask_ref.11) | copy-start | bytes 6148
  9.0 5.8 %collective-permute-start.2 = (bf16[1248,128]{1,0:T(8,128)(2,1)S(1)}, bf16[1248,128]{1,0:T(8,128)(2,1)S(1)}, u32[]{:S(2)}, u32[]{:S(2)}) collective-permute-start(bf16[1248,128]{1,0:T(8,128)(2,1)S(1)} %get-tuple-element.31), channel_id=1, source_target_pairs={{0,4},{1,5},{2,6},{3,7},{4,0},{5,1},{6,2},{7,3},{8,12},{9,13},{10,... | collective-permute-start | bytes 958472 | tf_op jit(solution)/shard_map/ppermute | solution.py:546
  9.1 4.1 %collective-permute-start = (bf16[160,128]{1,0:T(8,128)(2,1)S(1)}, bf16[160,128]{1,0:T(8,128)(2,1)S(1)}, u32[]{:S(2)}, u32[]{:S(2)}) collective-permute-start(bf16[160,128]{1,0:T(8,128)(2,1)S(1)} %get-tuple-element.27), channel_id=1, source_target_pairs={{0,1},{1,0},{2,3},{3,2},{4,5},{5,4},{6,7},{7,6},{8,9},{9,8},{10,11... | collective-permute-start | bytes 122888 | tf_op jit(solution)/shard_map/ppermute | solution.py:546
  10.6 2.5 %collective-permute-start.1 = (bf16[160,128]{1,0:T(8,128)(2,1)S(1)}, bf16[160,128]{1,0:T(8,128)(2,1)S(1)}, u32[]{:S(2)}, u32[]{:S(2)}) collective-permute-start(bf16[160,128]{1,0:T(8,128)(2,1)S(1)} %get-tuple-element.28), channel_id=1, source_target_pairs={{0,4},{1,2},{2,1},{3,7},{4,0},{5,6},{6,5},{7,3},{8,12},{9,10},{10,... | collective-permute-start | bytes 122888 | tf_op jit(solution)/shard_map/ppermute | solution.py:546
  13.1 1.7 %copy-start.5 = (s32[4,128]{1,0:T(4,128)S(1)}, s32[4,128]{1,0:T(4,128)}, u32[]{:S(2)}) copy-start(s32[4,128]{1,0:T(4,128)} %mask_ref.11) | copy-start | bytes 6148
  15.5 11.5 %collective-permute-start.7 = (bf16[1264,128]{1,0:T(8,128)(2,1)S(1)}, bf16[1264,128]{1,0:T(8,128)(2,1)S(1)}, u32[]{:S(2)}, u32[]{:S(2)}) collective-permute-start(bf16[1264,128]{1,0:T(8,128)(2,1)S(1)} %get-tuple-element.44), channel_id=1, source_target_pairs={{0,1},{1,0},{2,3},{3,2},{4,8},{5,9},{6,10},{7,11},{8,4},{9,5},{10,... | collective-permute-start | bytes 970760 | tf_op jit(solution)/shard_map/ppermute | solution.py:546
  19.4 4.7 %collective-permute-start.4 = (bf16[1248,128]{1,0:T(8,128)(2,1)S(1)}, bf16[1248,128]{1,0:T(8,128)(2,1)S(1)}, u32[]{:S(2)}, u32[]{:S(2)}) collective-permute-start(bf16[1248,128]{1,0:T(8,128)(2,1)S(1)} %get-tuple-element.39), channel_id=1, source_target_pairs={{0,4},{1,5},{2,6},{3,7},{4,0},{5,1},{6,2},{7,3},{8,12},{9,13},{10,... | collective-permute-start | bytes 958472 | tf_op jit(solution)/shard_map/ppermute | solution.py:546
  19.5 4.6 %collective-permute-start.5 = (bf16[160,128]{1,0:T(8,128)(2,1)S(1)}, bf16[160,128]{1,0:T(8,128)(2,1)S(1)}, u32[]{:S(2)}, u32[]{:S(2)}) collective-permute-start(bf16[160,128]{1,0:T(8,128)(2,1)S(1)} %get-tuple-element.40), channel_id=1, source_target_pairs={{0,1},{1,0},{2,3},{3,2},{4,5},{5,4},{6,7},{7,6},{8,9},{9,8},{10,11... | collective-permute-start | bytes 122888 | tf_op jit(solution)/shard_map/ppermute | solution.py:546
  21.1 3.0 %collective-permute-start.6 = (bf16[160,128]{1,0:T(8,128)(2,1)S(1)}, bf16[160,128]{1,0:T(8,128)(2,1)S(1)}, u32[]{:S(2)}, u32[]{:S(2)}) collective-permute-start(bf16[160,128]{1,0:T(8,128)(2,1)S(1)} %get-tuple-element.41), channel_id=1, source_target_pairs={{0,4},{1,2},{2,1},{3,7},{4,0},{5,6},{6,5},{7,3},{8,12},{9,10},{10,... | collective-permute-start | bytes 122888 | tf_op jit(solution)/shard_map/ppermute | solution.py:546

commit v5 on v4

--- a/solution.py
+++ b/solution.py
@@ -182,8 +182,13 @@
     send_ocean_row(rows, xo_ref, low_side)
 
 
+def prepare_kernel(n_ref, w_ref, stress_ref, tab_ref):
+    make_tables(tab_ref)
+    stress_ref[...] = stress_of(n_ref, w_ref)
+
+
 def start_kernel(s_ref, o_ref, mask_ref,
-                 n_ref, xe_ref, ye_ref, yo_ref, tab_ref, edge_ref, t_ref, e_ref):
+                 n_ref, xe_ref, ye_ref, yo_ref, edge_ref, t_ref, e_ref):
     wet = mask_ref[...].astype(F32)
     for x in range(ROWS):
         t_ref[x] = jnp.transpose(s_ref[x].astype(F32))
@@ -209,7 +214,6 @@
     ]
     first, last = pack_ocean_columns(blocks, lane_of((8, LANES)))
     send_y(e_ref, first, last, even_y, (ye_ref, yo_ref))
-    make_tables(tab_ref)
 
 
 def make_tables(tab_ref):
@@ -344,6 +348,12 @@
     return jnp.abs(rate) * (upwind - n_ref[x, k])
 
 
+def cell_of(acc_ref, x, k):
+    if len(acc_ref.shape) == 4:
+        return x, k
+    return x, pl.ds(k, NF, stride=NDIR), slice(None)
+
+
 def inner_waves(n_ref, yh_ref, rate_ref, wet, tab_ref, shift_ref, ys_ref, acc_ref, keep):
     size = QUARTER * NF
     for quarter in range(4):
@@ -374,7 +384,7 @@
                     total = total + refraction(n_ref, rate_ref, x, k)
                     if 0 <= x + 2 * step < ROWS:
                         total = keep(total * wet[x])
-                acc_ref[x, k] = total
+                acc_ref[cell_of(acc_ref, x, k)] = total
             return carry
 
         lax.fori_loop(0, QUARTER, body, 0, unroll=QUARTER)
@@ -391,7 +401,8 @@
 
     def body(kk, carry):
         k = first + kk
-        acc_ref[x, k] = keep(wet * (acc_ref[x, k] + refraction(n_ref, rate_ref, x, k)))
+        cell = cell_of(acc_ref, x, k)
+        acc_ref[cell] = keep(wet * (acc_ref[cell] + refraction(n_ref, rate_ref, x, k)))
         return carry
 
     lax.fori_loop(0, HALF, body, 0, unroll=6)
@@ -407,9 +418,10 @@
         near = halo_ref[pl.ds(pl.multiple_of(((1 - side) * HALF + kk) * NF, NF), NF), :].astype(F32)
         far = halo_ref[pl.ds(pl.multiple_of((side * HALF + kk) * NF, NF), NF), :].astype(F32)
         near, far = jnp.where(known, near, 0.0), jnp.where(known, far, 0.0)
-        total = acc_ref[x, k] + (near * tab_ref[1, k] + far * tab_ref[2, k])
-        acc_ref[x, k] = keep(wet * (total + refraction(n_ref, rate_ref, x, k)))
-        acc_ref[inner, k] = keep(wet_inner * (acc_ref[inner, k] + near * tab_ref[2, k]))
+        cell, inner_cell = cell_of(acc_ref, x, k), cell_of(acc_ref, inner, k)
+        total = acc_ref[cell] + (near * tab_ref[1, k] + far * tab_ref[2, k])
+        acc_ref[cell] = keep(wet * (total + refraction(n_ref, rate_ref, x, k)))
+        acc_ref[inner_cell] = keep(wet_inner * (acc_ref[inner_cell] + near * tab_ref[2, k]))
         return carry
 
     lax.fori_loop(0, HALF, body, 0, unroll=6)
@@ -430,8 +442,8 @@
     return [jnp.broadcast_to(wet[x : x + 1], (NF, LANES)) for x in range(ROWS)], wet8
 
 
-def inner_kernel(n_ref, o_ref, mask_ref, tab_ref, w_ref, shift_ref, ye_in, yo_in,
-                 acc_ref, stress_ref, yh_ref, ext_ref, rate_ref, ys_ref):
+def inner_kernel(n_ref, o_ref, mask_ref, tab_ref, shift_ref, ye_in, yo_in,
+                 acc_ref, yh_ref, ext_ref, rate_ref, ys_ref):
     even_y = is_even("gy")
     wet, _ = wet_rows(mask_ref)
     y_spectra(even_y, ye_in, yo_in, yh_ref)
@@ -439,7 +451,6 @@
     unknown = jnp.zeros((OCEAN, LANES), F32)
     extend_ocean(o_ref, unknown, unknown, ext_ref, 1)
     refraction_rates(ext_ref, below, above, rate_ref)
-    stress_ref[...] = stress_of(n_ref, w_ref)
     inner_waves(n_ref, yh_ref, rate_ref, wet, tab_ref, shift_ref, ys_ref, acc_ref, rounded)
 
 
@@ -477,29 +488,9 @@
     send_y(e_ref, ycol_ref[0], ycol_ref[1], even_y, (ye_ref, yo_ref))
 
 
-def write_rows(acc_ref, first, t_ref, block_ref, out_hbm, sems):
-    copies = []
-    for r in range(2):
-
-        def body(k, carry, r=r):
-            t_ref[r, pl.ds(k, NF, stride=NDIR), :] = acc_ref[first + r, k]
-            return carry
-
-        lax.fori_loop(0, NDIR, body, 0, unroll=6)
-        block_ref[r] = jnp.transpose(t_ref[r]).astype(BF16)
-        copies.append(pltpu.make_async_copy(block_ref.at[r], out_hbm.at[first + r], sems.at[r]))
-        copies[-1].start()
-    return copies
-
-
-def wait_all(copies):
-    for copy in copies:
-        copy.wait()
-
-
 def inner_last_kernel(n_ref, o_ref, mask_ref, tab_ref, w_ref, shift_ref, xe_in, ye_in, yo_in,
-                      acc_ref, stress_ref, out_hbm,
-                      yh_ref, ext_ref, rate_ref, ys_ref, t_ref, block_ref, sems):
+                      acc_ref, stress_ref, done_ref,
+                      yh_ref, ext_ref, rate_ref, ys_ref):
     even_x, even_y = is_even("gx"), is_even("gy")
     wet, _ = wet_rows(mask_ref)
     y_spectra(even_y, ye_in, yo_in, yh_ref)
@@ -507,29 +498,37 @@
     left, right = x_ocean(even_x, xe_in, xe_in)
     extend_ocean(o_ref, left, right, ext_ref, 1)
     refraction_rates(ext_ref, below, above, rate_ref)
+    stress_ref[...] = stress_of(n_ref, w_ref)
     inner_waves(n_ref, yh_ref, rate_ref, wet, tab_ref, shift_ref, ys_ref, acc_ref, exact)
     side = even_x.astype(jnp.int32)
     finish_near_half(n_ref, acc_ref, rate_ref, mask_ref, tab_ref, xe_in, True, side, exact)
     finish_far_half(n_ref, acc_ref, rate_ref, mask_ref, side, exact)
-    copies = write_rows(acc_ref, 2 * side, t_ref, block_ref, out_hbm, sems)
-    stress_ref[...] = stress_of(n_ref, w_ref)
-    wait_all(copies)
-
-
-def last_kernel(n_ref, acc_in, o_ref, mask_ref, tab_ref, stress_ref, xe_in, xo_in, ye_in, yo_in, out_in,
-                acc_ref, ocean_ref, out_hbm, ext_ref, rate_ref, t_ref, block_ref, sems):
+    for r in range(2):
+        done_ref[r] = jnp.transpose(acc_ref[2 * side + r]).astype(BF16)
+
+
+def last_kernel(n_ref, acc_in, done_ref, o_ref, mask_ref, tab_ref, stress_ref, xe_in, xo_in, ye_in, yo_in,
+                acc_ref, ocean_ref, out_hbm, ext_ref, rate_ref, block_ref, sems):
     even_x, even_y = is_even("gx"), is_even("gy")
+    side = 1 - even_x.astype(jnp.int32)
+    done = pltpu.make_async_copy(done_ref, out_hbm.at[pl.ds(2 * (1 - side), 2)], sems.at[0])
+    done.start()
     below, above = y_ocean(even_y, ye_in, yo_in)
     left, right = x_ocean(even_x, xe_in, xo_in)
-    extend_ocean(o_ref, left, right, ext_ref)
+    extend_ocean(o_ref, left, right, ext_ref, 1)
     refraction_rates(ext_ref, below, above, rate_ref)
-    side = 1 - even_x.astype(jnp.int32)
     finish_near_half(n_ref, acc_ref, rate_ref, mask_ref, tab_ref, xo_in, inside("gx"), side, exact)
     finish_far_half(n_ref, acc_ref, rate_ref, mask_ref, side, exact)
-    copies = write_rows(acc_ref, 2 * side, t_ref, block_ref, out_hbm, sems)
+    copies = [done]
+    for r in range(2):
+        block_ref[r] = jnp.transpose(acc_ref[2 * side + r]).astype(BF16)
+        copies.append(pltpu.make_async_copy(block_ref.at[r], out_hbm.at[2 * side + r], sems.at[1 + r]))
+        copies[-1].start()
     _, wet8 = wet_rows(mask_ref)
+    extend_ocean(o_ref, left, right, ext_ref)
     advance_ocean(ext_ref, below, above, stress_ref[...], wet8, ocean_ref)
-    wait_all(copies)
+    for copy in copies:
+        copy.wait()
 
 
 def swap(array, axis, odd):
@@ -561,6 +560,7 @@
     )(*ins)
 
 
+BINNED = ((ROWS, BINS, LANES), F32)
 GRID = ((ROWS, NDIR, NF, LANES), F32)
 XEDGE = ((XROWS, LANES), BF16)
 XLONG = ((XROWS + 16, LANES), BF16)
@@ -596,19 +596,20 @@
         moved=32,
     )
     xo = swap(xo, "gx", 1)
-    n, xe, ye, yo, tab, edge_table = call(
+    n, xe, ye, yo, edge_table = call(
         start_kernel,
-        (GRID, XEDGE, YEDGE, YEDGE, ((5, NDIR, NF, LANES), F32), ((2, ROWS * LANES, LANES), BF16)),
+        (GRID, XEDGE, YEDGE, YEDGE, ((2, ROWS * LANES, LANES), BF16)),
         (spectrum, ocean_state, sea_mask),
         [pltpu.VMEM((ROWS, BINS, LANES), F32), EDGES],
     )
     xe = swap(xe, "gx", 0)
     ye = swap(ye, "gy", 0)
     yo = swap(yo, "gy", 1)
-    acc, stress = call(
+    stress, tab = call(prepare_kernel, (DRIVE, ((5, NDIR, NF, LANES), F32)), (n, weights), [])
+    (acc,) = call(
         inner_kernel,
-        (GRID, DRIVE),
-        (n, ocean_state, sea_mask, tab, weights, shift_table, ye, yo),
+        (GRID,),
+        (n, ocean_state, sea_mask, tab, shift_table, ye, yo),
         [YH, EXT, RATE, SHIFTED],
     )
     acc, ocean, rate, xo2, xrow, ycol = call(
@@ -629,21 +630,19 @@
     xe = swap(xe, "gx", 0)
     ye = swap(ye, "gy", 0)
     yo = swap(yo, "gy", 1)
-    acc, stress, out = call(
+    acc, stress, done = call(
         inner_last_kernel,
-        (GRID, DRIVE, (spectrum.shape, BF16)),
+        (BINNED, DRIVE, ((2, *spectrum.shape[1:]), BF16)),
         (n, ocean, sea_mask, tab, weights, shift_table, xe, ye, yo),
-        [YH, EXT, RATE, SHIFTED, TURNED, BLOCK, pltpu.SemaphoreType.DMA((2,))],
-        any_out=(2,),
+        [YH, EXT, RATE, SHIFTED],
     )
     _, ocean, out = call(
         last_kernel,
-        (GRID, ocean_shape, (spectrum.shape, BF16)),
-        (n, acc, ocean, sea_mask, tab, stress, xe, xo2, ye, yo, out),
-        [EXT, RATE, TURNED, BLOCK, pltpu.SemaphoreType.DMA((2,))],
-        any_in=(10,),
+        (BINNED, ocean_shape, (spectrum.shape, BF16)),
+        (n, acc, done, ocean, sea_mask, tab, stress, xe, xo2, ye, yo),
+        [EXT, RATE, BLOCK, pltpu.SemaphoreType.DMA((3,))],
         any_out=(2,),
-        aliases={1: 0, 10: 2},
+        aliases={1: 0},
     )
     return out, ocean
 

time: 29.6 us -> 28.3 us (0.956)
  Pallas kernels: 12.5 us -> 11.7 us
  waiting for transfers between devices: 5.47 us -> 4.96 us
    pallas_call x7 -> x8, Pallas kernels: 12.5 us -> 11.7 us  [call(): pl.pallas_call(kernel, out_shape=[jax.ShapeDtypeStruct(shape, dtype) for...]
    ppermute x8, waiting for transfers between devices: 5.47 us -> 4.96 us  [swap(): return lax.ppermute(array, ('gx', 'gy'), pairs)]
    unnamed x12 -> x10, local copies, waits for them, and re-layouts: 1.6 us -> 1.59 us
  transfers between devices with their start and end apart: 8 -> 8, of which waited for: 2 -> 2; matrix products, arithmetic and copies ran while one was open for 0% -> 0% of each run, Pallas kernels for 24% -> 23%
where the time goes in v5:
time: 28.3 us; the launch traced here: 28.2 us
  Pallas kernels  11.7 us (41%)
  starting transfers between devices  9.15 us (32%)
  waiting for transfers between devices  4.96 us (18%)
  local copies, waits for them, and re-layouts  1.59 us (6%)
  between operations  0.72 us (3%)
    pallas_call x8, Pallas kernels, call(): pl.pallas_call(kernel, out_shape=[jax.ShapeDtypeStruct(shape, dtype) for...  11.7 us
    ppermute x8, starting transfers between devices, swap(): return lax.ppermute(array, ('gx', 'gy'), pairs)  9.15 us
    ppermute x8, waiting for transfers between devices, swap(): return lax.ppermute(array, ('gx', 'gy'), pairs)  4.96 us
    unnamed x10, local copies, waits for them, and re-layouts  1.59 us
  transfers between devices with their start and end apart: 8, of which 2 were waited for; matrix products, arithmetic and copies ran while one was open for 0% of the time, Pallas kernels for 23%

profile of v5, /device:TPU:0, one launch (start us, length us, event | category | flops | bytes accessed | tf_op | source)
XLA Modules:
  0.0 28.2 jit_solution(14896804880329670682)
XLA Ops:
  0.6 0.0 copy-start.3
  0.6 0.0 copy-start.2
  0.7 0.0 copy-start
  0.7 2.3 %first.1 = bf16[1248,128]{1,0:T(8,128)(2,1)} custom-call(bf16[4,128,1152]{2,1,0:T(8,128)(2,1)} %s_hbm.1, f32[3,16,4,128]{3,2,1,0:T(4,128)} %o_ref.5, s32[4,128]{1,0:T(4,128)} %mask_ref.11), custom_call_target="tpu_custom_call" | custom-call | bytes 33554432 | tf_op jit(solution)/shard_map/first/pallas_call | solution.py:550
  3.0 3.1 %collective-permute-start.3 = (bf16[1248,128]{1,0:T(8,128)(2,1)}, bf16[1248,128]{1,0:T(8,128)(2,1)S(1)}, u32[]{:S(2)}, u32[]{:S(2)}) collective-permute-start(bf16[1248,128]{1,0:T(8,128)(2,1)} %first.1), channel_id=1, source_target_pairs={{0,1},{1,0},{2,3},{3,2},{4,8},{5,9},{6,10},{7,11},{8,4},{9,5},{10,... | collective-permute-start | bytes 958472 | tf_op jit(solution)/shard_map/ppermute | solution.py:545
  6.1 0.0 copy-done
  6.1 0.9 %copy-done.1 = f32[3,16,4,128]{3,2,1,0:T(4,128)S(1)} copy-done((f32[3,16,4,128]{3,2,1,0:T(4,128)S(1)}, f32[3,16,4,128]{3,2,1,0:T(4,128)}, u32[]{:S(2)}) %copy-start.1) | copy-done | bytes 98328
  7.0 0.7 %copy-done.4 = s32[4,128]{1,0:T(4,128)S(1)} copy-done((s32[4,128]{1,0:T(4,128)S(1)}, s32[4,128]{1,0:T(4,128)}, u32[]{:S(2)}) %copy-start.4) | copy-done | bytes 2072
  7.7 1.1 %start.1 = (f32[4,36,32,128]{3,2,1,0:T(8,128)S(1)}, bf16[1248,128]{1,0:T(8,128)(2,1)S(1)}, bf16[160,128]{1,0:T(8,128)(2,1)S(1)}, bf16[160,128]{1,0:T(8,128)(2,1)S(1)}, bf16[2,512,128]{2,1,0:T(8,128)(2,1)S(1)}) custom-call(bf16[4,128,1152]{2,1,0:T(8,128)(2,1)S(1)} %copy-done, f32[3,16,4,128]{3,2,1,0:T(4,128)S(1)} %copy-done.1, s32[4,128]{1,0:T(4,128)S(1)} %copy-done.4), custom_call_target="tpu_custom_call" | custom-call | tf_op jit(solution)/shard_map/start/pallas_call | solution.py:550
  8.8 0.1 collective-permute-start.2
  8.9 1.6 %collective-permute-start = (bf16[160,128]{1,0:T(8,128)(2,1)S(1)}, bf16[160,128]{1,0:T(8,128)(2,1)S(1)}, u32[]{:S(2)}, u32[]{:S(2)}) collective-permute-start(bf16[160,128]{1,0:T(8,128)(2,1)S(1)} %get-tuple-element.26), channel_id=1, source_target_pairs={{0,1},{1,0},{2,3},{3,2},{4,5},{5,4},{6,7},{7,6},{8,9},{9,8},{10,11... | collective-permute-start | bytes 122888 | tf_op jit(solution)/shard_map/ppermute | solution.py:545
  10.4 0.0 collective-permute-start.1
  10.4 0.0 copy-done.3
  10.4 0.5 %prepare.1 = (f32[16,128]{1,0:T(8,128)S(1)}, f32[5,36,32,128]{3,2,1,0:T(8,128)S(1)}) custom-call(f32[4,36,32,128]{3,2,1,0:T(8,128)S(1)} %get-tuple-element.24.n_ref, bf16[4,16,1152]{2,1,0:T(8,128)(2,1)S(1)} %copy-done.3), custom_call_target="tpu_custom_call" | custom-call | tf_op jit(solution)/shard_map/prepare/pallas_call | solution.py:550
  10.9 2.0 %collective-permute-done.ye_in = bf16[160,128]{1,0:T(8,128)(2,1)S(1)} collective-permute-done((bf16[160,128]{1,0:T(8,128)(2,1)S(1)}, bf16[160,128]{1,0:T(8,128)(2,1)S(1)}, u32[]{:S(2)}, u32[]{:S(2)}) %collective-permute-start) | collective-permute-done | bytes 40992 | tf_op jit(solution)/shard_map/ppermute | solution.py:545
  12.9 0.0 collective-permute-done.1.yo_in
  12.9 0.0 copy-done.2
  12.9 1.5 %inner.1.acc_in = f32[4,36,32,128]{3,2,1,0:T(8,128)S(1)} custom-call(f32[4,36,32,128]{3,2,1,0:T(8,128)S(1)} %get-tuple-element.24.n_ref, f32[3,16,4,128]{3,2,1,0:T(4,128)S(1)} %copy-done.1, s32[4,128]{1,0:T(4,128)S(1)} %copy-done.4, f32[5,36,32,128]{3,2,1,0:T(8,128)S(1)} %get-tuple-element.25.tab_ref, bf16[2,256,256]{2,1,0:T(8,128)(2,1)S(1)} %copy-done.2, ...), custom_call_target="tpu_custom_call" | custom-call | tf_op jit(solution)/shard_map/inner/pallas_call | solution.py:550
  14.4 0.0 collective-permute-done.3.xo_in
  14.4 0.0 collective-permute-done.2.xe_in
  14.4 0.7 %send.1 = (f32[4,36,32,128]{3,2,1,0:T(8,128)S(1)}, f32[3,16,4,128]{3,2,1,0:T(4,128)S(1)}, f32[36,8,128]{2,1,0:T(8,128)S(1)}, bf16[1264,128]{1,0:T(8,128)(2,1)S(1...) custom-call(f32[4,36,32,128]{3,2,1,0:T(8,128)S(1)} %get-tuple-element.24.n_ref, ...), custom_call_target="tpu_custom_call", output_to_operand_aliasing={{0}: (1, {})} | custom-call | tf_op jit(solution)/shard_map/send/pallas_call | solution.py:550
  15.1 2.7 %collective-permute-start.7 = (bf16[1264,128]{1,0:T(8,128)(2,1)S(1)}, bf16[1264,128]{1,0:T(8,128)(2,1)S(1)}, u32[]{:S(2)}, u32[]{:S(2)}) collective-permute-start(bf16[1264,128]{1,0:T(8,128)(2,1)S(1)} %get-tuple-element.43), channel_id=1, source_target_pairs={{0,1},{1,0},{2,3},{3,2},{4,8},{5,9},{6,10},{7,11},{8,4},{9,5},{10,... | collective-permute-start | bytes 970760 | tf_op jit(solution)/shard_map/ppermute | solution.py:545
  17.8 1.2 %rest.1 = (f32[4,36,32,128]{3,2,1,0:T(8,128)S(1)}, bf16[1248,128]{1,0:T(8,128)(2,1)S(1)}, bf16[160,128]{1,0:T(8,128)(2,1)S(1)}, bf16[160,128]{1,0:T(8,128)(2,1)S(1)}) custom-call(f32[4,36,32,128]{3,2,1,0:T(8,128)S(1)} %get-tuple-element.24.n_ref, f32[4,36,32,128]{3,2,1,0:T(8,128)S(1)} %get-tuple-element.30.acc_in, ...), custom_call_target="tpu_custom_call", output_to_operand_aliasing={{0}: (1, {})} | custom-call | tf_op jit(solution)/shard_map/rest/pallas_call | solution.py:550
  19.0 0.1 collective-permute-start.4
  19.1 1.6 %collective-permute-start.5 = (bf16[160,128]{1,0:T(8,128)(2,1)S(1)}, bf16[160,128]{1,0:T(8,128)(2,1)S(1)}, u32[]{:S(2)}, u32[]{:S(2)}) collective-permute-start(bf16[160,128]{1,0:T(8,128)(2,1)S(1)} %get-tuple-element.38), channel_id=1, source_target_pairs={{0,1},{1,0},{2,3},{3,2},{4,5},{5,4},{6,7},{7,6},{8,9},{9,8},{10,11... | collective-permute-start | bytes 122888 | tf_op jit(solution)/shard_map/ppermute | solution.py:545
  20.7 0.0 collective-permute-start.6
  20.7 3.0 %collective-permute-done.5.ye_in = bf16[160,128]{1,0:T(8,128)(2,1)S(1)} collective-permute-done((bf16[160,128]{1,0:T(8,128)(2,1)S(1)}, bf16[160,128]{1,0:T(8,128)(2,1)S(1)}, u32[]{:S(2)}, u32[]{:S(2)}) %collective-permute-start.5) | collective-permute-done | bytes 40992 | tf_op jit(solution)/shard_map/ppermute | solution.py:545
  23.7 0.0 collective-permute-done.6.yo_in
  23.7 0.0 collective-permute-done.4.xe_in
  23.7 2.2 %inner_last.1 = (f32[4,1152,128]{2,1,0:T(8,128)S(1)}, f32[16,128]{1,0:T(8,128)S(1)}, bf16[2,128,1152]{2,1,0:T(8,128)(2,1)S(1)}) custom-call(f32[4,36,32,128]{3,2,1,0:T(8,128)S(1)} %get-tuple-element.35.n_ref, f32[3,16,4,128]{3,2,1,0:T(4,128)S(1)} %get-tuple-element.36.o_ref, s32[4,128]{1,0:T(4,128)S(1)} %copy-done.4, ...), custom_call_target="tpu_custom_call" | custom-call | tf_op jit(solution)/shard_map/inner_last/pallas_call | solution.py:550
  25.9 0.0 collective-permute-done.7.xo_in
  25.9 2.3 %last.1 = (f32[4,1152,128]{2,1,0:T(8,128)S(1)}, f32[3,16,4,128]{3,2,1,0:T(4,128)}, bf16[4,128,1152]{2,1,0:T(8,128)(2,1)}) custom-call(f32[4,36,32,128]{3,2,1,0:T(8,128)S(1)} %get-tuple-element.35.n_ref, f32[4,1152,128]{2,1,0:T(8,128)S(1)} %get-tuple-element.40.acc_in, ...), custom_call_target="tpu_custom_call", output_to_operand_aliasing={{0}: (1, {})} | custom-call | tf_op jit(solution)/shard_map/last/pallas_call | solution.py:550
  (2 shorter events, 0.0 us)
Async XLA Ops:
  0.6 9.8 %copy-start.3 = (bf16[4,16,1152]{2,1,0:T(8,128)(2,1)S(1)}, bf16[4,16,1152]{2,1,0:T(8,128)(2,1)}, u32[]{:S(2)}) copy-start(bf16[4,16,1152]{2,1,0:T(8,128)(2,1)} %constant.4.clone.w_ref) | copy-start | bytes 442372
  0.6 12.3 %copy-start.2 = (bf16[2,256,256]{2,1,0:T(8,128)(2,1)S(1)}, bf16[2,256,256]{2,1,0:T(8,128)(2,1)}, u32[]{:S(2)}) copy-start(bf16[2,256,256]{2,1,0:T(8,128)(2,1)} %constant.5.clone.shift_ref) | copy-start | bytes 786436
  0.7 5.4 %copy-start = (bf16[4,128,1152]{2,1,0:T(8,128)(2,1)S(1)}, bf16[4,128,1152]{2,1,0:T(8,128)(2,1)}, u32[]{:S(2)}) copy-start(bf16[4,128,1152]{2,1,0:T(8,128)(2,1)} %s_hbm.1) | copy-start | bytes 3538948
  3.0 11.4 %collective-permute-start.3 = (bf16[1248,128]{1,0:T(8,128)(2,1)}, bf16[1248,128]{1,0:T(8,128)(2,1)S(1)}, u32[]{:S(2)}, u32[]{:S(2)}) collective-permute-start(bf16[1248,128]{1,0:T(8,128)(2,1)} %first.1), channel_id=1, source_target_pairs={{0,1},{1,0},{2,3},{3,2},{4,8},{5,9},{6,10},{7,11},{8,4},{9,5},{10,... | collective-permute-start | bytes 958472 | tf_op jit(solution)/shard_map/ppermute | solution.py:545
  6.1 0.9 %copy-start.1 = (f32[3,16,4,128]{3,2,1,0:T(4,128)S(1)}, f32[3,16,4,128]{3,2,1,0:T(4,128)}, u32[]{:S(2)}) copy-start(f32[3,16,4,128]{3,2,1,0:T(4,128)} %o_ref.5) | copy-start | bytes 294916
  7.0 0.7 %copy-start.4 = (s32[4,128]{1,0:T(4,128)S(1)}, s32[4,128]{1,0:T(4,128)}, u32[]{:S(2)}) copy-start(s32[4,128]{1,0:T(4,128)} %mask_ref.11) | copy-start | bytes 6148
  8.8 5.6 %collective-permute-start.2 = (bf16[1248,128]{1,0:T(8,128)(2,1)S(1)}, bf16[1248,128]{1,0:T(8,128)(2,1)S(1)}, u32[]{:S(2)}, u32[]{:S(2)}) collective-permute-start(bf16[1248,128]{1,0:T(8,128)(2,1)S(1)} %get-tuple-element.29), channel_id=1, source_target_pairs={{0,4},{1,5},{2,6},{3,7},{4,0},{5,1},{6,2},{7,3},{8,12},{9,13},{10,... | collective-permute-start | bytes 958472 | tf_op jit(solution)/shard_map/ppermute | solution.py:545
  8.9 4.1 %collective-permute-start = (bf16[160,128]{1,0:T(8,128)(2,1)S(1)}, bf16[160,128]{1,0:T(8,128)(2,1)S(1)}, u32[]{:S(2)}, u32[]{:S(2)}) collective-permute-start(bf16[160,128]{1,0:T(8,128)(2,1)S(1)} %get-tuple-element.26), channel_id=1, source_target_pairs={{0,1},{1,0},{2,3},{3,2},{4,5},{5,4},{6,7},{7,6},{8,9},{9,8},{10,11... | collective-permute-start | bytes 122888 | tf_op jit(solution)/shard_map/ppermute | solution.py:545
  10.4 2.5 %collective-permute-start.1 = (bf16[160,128]{1,0:T(8,128)(2,1)S(1)}, bf16[160,128]{1,0:T(8,128)(2,1)S(1)}, u32[]{:S(2)}, u32[]{:S(2)}) collective-permute-start(bf16[160,128]{1,0:T(8,128)(2,1)S(1)} %get-tuple-element.27), channel_id=1, source_target_pairs={{0,4},{1,2},{2,1},{3,7},{4,0},{5,6},{6,5},{7,3},{8,12},{9,10},{10,... | collective-permute-start | bytes 122888 | tf_op jit(solution)/shard_map/ppermute | solution.py:545
  15.1 10.8 %collective-permute-start.7 = (bf16[1264,128]{1,0:T(8,128)(2,1)S(1)}, bf16[1264,128]{1,0:T(8,128)(2,1)S(1)}, u32[]{:S(2)}, u32[]{:S(2)}) collective-permute-start(bf16[1264,128]{1,0:T(8,128)(2,1)S(1)} %get-tuple-element.43), channel_id=1, source_target_pairs={{0,1},{1,0},{2,3},{3,2},{4,8},{5,9},{6,10},{7,11},{8,4},{9,5},{10,... | collective-permute-start | bytes 970760 | tf_op jit(solution)/shard_map/ppermute | solution.py:545
  19.0 4.7 %collective-permute-start.4 = (bf16[1248,128]{1,0:T(8,128)(2,1)S(1)}, bf16[1248,128]{1,0:T(8,128)(2,1)S(1)}, u32[]{:S(2)}, u32[]{:S(2)}) collective-permute-start(bf16[1248,128]{1,0:T(8,128)(2,1)S(1)} %get-tuple-element.37), channel_id=1, source_target_pairs={{0,4},{1,5},{2,6},{3,7},{4,0},{5,1},{6,2},{7,3},{8,12},{9,13},{10,... | collective-permute-start | bytes 958472 | tf_op jit(solution)/shard_map/ppermute | solution.py:545
  19.1 4.6 %collective-permute-start.5 = (bf16[160,128]{1,0:T(8,128)(2,1)S(1)}, bf16[160,128]{1,0:T(8,128)(2,1)S(1)}, u32[]{:S(2)}, u32[]{:S(2)}) collective-permute-start(bf16[160,128]{1,0:T(8,128)(2,1)S(1)} %get-tuple-element.38), channel_id=1, source_target_pairs={{0,1},{1,0},{2,3},{3,2},{4,5},{5,4},{6,7},{7,6},{8,9},{9,8},{10,11... | collective-permute-start | bytes 122888 | tf_op jit(solution)/shard_map/ppermute | solution.py:545
  20.7 3.0 %collective-permute-start.6 = (bf16[160,128]{1,0:T(8,128)(2,1)S(1)}, bf16[160,128]{1,0:T(8,128)(2,1)S(1)}, u32[]{:S(2)}, u32[]{:S(2)}) collective-permute-start(bf16[160,128]{1,0:T(8,128)(2,1)S(1)} %get-tuple-element.39), channel_id=1, source_target_pairs={{0,4},{1,2},{2,1},{3,7},{4,0},{5,6},{6,5},{7,3},{8,12},{9,10},{10,... | collective-permute-start | bytes 122888 | tf_op jit(solution)/shard_map/ppermute | solution.py:545

commit v6 on v5

--- a/solution.py
+++ b/solution.py
@@ -132,6 +132,16 @@
     return first, last
 
 
+def ocean_blocks(o_ref):
+    pad = jnp.zeros((1, LANES), F32)
+    return [
+        jnp.concatenate(
+            [part for z in range(NZ) for part in (pad, o_ref[c, z], pad, pad, pad)], 0
+        )
+        for c in range(3)
+    ]
+
+
 def send_x(n_ref, ocean_rows, mine_ref, low_side):
     row = jnp.where(low_side, 0, 2)
     first = jnp.where(low_side, HALF, 0)
@@ -176,7 +186,7 @@
             xo_ref[at, :] = (t_ref[r, pl.ds(first + kk, NF, stride=NDIR), :] * wet).astype(BF16)
             return carry
 
-        lax.fori_loop(0, HALF, body, 0, unroll=6)
+        lax.fori_loop(0, HALF, body, 0, unroll=18)
     copies[3].wait()
     rows = tuple(o_ref[:, :, r, :].reshape(OCEAN, LANES) for r in (0, ROWS - 1))
     send_ocean_row(rows, xo_ref, low_side)
@@ -205,14 +215,7 @@
     make_edge_tables(edge_ref)
     for quarter in range(4):
         pack_y_edges(n_ref, quarter, edge_ref, e_ref)
-    pad = jnp.zeros((1, LANES), F32)
-    blocks = [
-        jnp.concatenate(
-            [part for z in range(NZ) for part in (pad, o_ref[c, z], pad, pad, pad)], 0
-        )
-        for c in range(3)
-    ]
-    first, last = pack_ocean_columns(blocks, lane_of((8, LANES)))
+    first, last = pack_ocean_columns(ocean_blocks(o_ref), lane_of((8, LANES)))
     send_y(e_ref, first, last, even_y, (ye_ref, yo_ref))
 
 
@@ -405,7 +408,7 @@
         acc_ref[cell] = keep(wet * (acc_ref[cell] + refraction(n_ref, rate_ref, x, k)))
         return carry
 
-    lax.fori_loop(0, HALF, body, 0, unroll=6)
+    lax.fori_loop(0, HALF, body, 0, unroll=18)
 
 
 def finish_near_half(n_ref, acc_ref, rate_ref, mask_ref, tab_ref, halo_ref, known, side, keep):
@@ -424,7 +427,7 @@
         acc_ref[inner_cell] = keep(wet_inner * (acc_ref[inner_cell] + near * tab_ref[2, k]))
         return carry
 
-    lax.fori_loop(0, HALF, body, 0, unroll=6)
+    lax.fori_loop(0, HALF, body, 0, unroll=18)
 
 
 def rounded(v):
@@ -455,7 +458,7 @@
 
 
 def send_kernel(n_ref, acc_in, o_ref, mask_ref, stress_ref, xe_in, xo_in, ye_in, yo_in,
-                acc_ref, ocean_ref, rate_ref, xo_ref, xrow_ref, ycol_ref, ext_ref):
+                acc_ref, ocean_ref, rate_ref, xo_ref, xrow_ref, ext_ref):
     even_x, even_y = is_even("gx"), is_even("gy")
     below, above = y_ocean(even_y, ye_in, yo_in)
     left, right = x_ocean(even_x, xe_in, xo_in)
@@ -471,10 +474,9 @@
     send_x(acc_ref, rows, xo_ref, even_x)
     xo_ref[XROWS:, :] = jnp.zeros((16, LANES), BF16)
     xrow_ref[...] = jnp.where(even_x, rows[1], rows[0])
-    ycol_ref[0], ycol_ref[1] = pack_ocean_columns(new, lane_of((8, LANES)))
-
-
-def rest_kernel(n_ref, acc_in, mask_ref, tab_ref, rate_ref, edge_ref, xrow_ref, ycol_ref, xe_in, xo_in,
+
+
+def rest_kernel(n_ref, acc_in, mask_ref, tab_ref, rate_ref, edge_ref, xrow_ref, o_ref, xe_in, xo_in,
                 acc_ref, xe_ref, ye_ref, yo_ref, e_ref):
     even_x, even_y = is_even("gx"), is_even("gy")
     side = even_x.astype(jnp.int32)
@@ -485,7 +487,8 @@
     send_x(acc_ref, (row, row), xe_ref, jnp.logical_not(even_x))
     for quarter in range(4):
         pack_y_edges(acc_ref, quarter, edge_ref, e_ref)
-    send_y(e_ref, ycol_ref[0], ycol_ref[1], even_y, (ye_ref, yo_ref))
+    first, last = pack_ocean_columns(ocean_blocks(o_ref), lane_of((8, LANES)))
+    send_y(e_ref, first, last, even_y, (ye_ref, yo_ref))
 
 
 def inner_last_kernel(n_ref, o_ref, mask_ref, tab_ref, w_ref, shift_ref, xe_in, ye_in, yo_in,
@@ -531,14 +534,14 @@
         copy.wait()
 
 
-def swap(array, axis, odd):
+def swap(array, axis, odd, wrap=False):
     nx, ny = lax.axis_size("gx"), lax.axis_size("gy")
     pairs = []
     for i in range(nx):
         for j in range(ny):
             to = (i ^ 1, j) if axis == "gx" else (i, j ^ 1)
             if odd and axis == "gx":
-                to = (((i + 1) ^ 1) - 1, j) if 0 < i < nx - 1 else (i, j ^ 1)
+                to = (((i + 1) ^ 1) - 1, j) if 0 < i < nx - 1 else ((nx - 1 - i, j) if wrap else (i, j ^ 1))
             if odd and axis == "gy":
                 to = (i, ((j + 1) ^ 1) - 1) if 0 < j < ny - 1 else (i ^ 1, j)
             pairs.append((i * ny + j, to[0] * ny + to[1]))
@@ -612,18 +615,18 @@
         (n, ocean_state, sea_mask, tab, shift_table, ye, yo),
         [YH, EXT, RATE, SHIFTED],
     )
-    acc, ocean, rate, xo2, xrow, ycol = call(
+    acc, ocean, rate, xo2, xrow = call(
         send_kernel,
-        (GRID, ocean_shape, RATES, XLONG, ((OCEAN, LANES), F32), ((2, 8, LANES), F32)),
+        (GRID, ocean_shape, RATES, XLONG, ((OCEAN, LANES), F32)),
         (n, acc, ocean_state, sea_mask, stress, xe, xo, ye, yo),
         [EXT],
         aliases={1: 0},
     )
-    xo2 = swap(xo2, "gx", 1)
+    xo2 = swap(xo2, "gx", 1, True)
     n, xe, ye, yo = call(
         rest_kernel,
         (GRID, XEDGE, YEDGE, YEDGE),
-        (n, acc, sea_mask, tab, rate, edge_table, xrow, ycol, xe, xo),
+        (n, acc, sea_mask, tab, rate, edge_table, xrow, ocean, xe, xo),
         [EDGES],
         aliases={1: 0},
     )

time: 28.3 us -> 27.8 us (0.982)
  waiting for transfers between devices: 4.96 us -> 4.66 us
    ppermute x8, waiting for transfers between devices: 4.96 us -> 4.66 us  [swap(): return lax.ppermute(array, ('gx', 'gy'), pairs)]
  transfers between devices with their start and end apart: 8 -> 8, of which waited for: 2 -> 3; matrix products, arithmetic and copies ran while one was open for 0% -> 0% of each run, Pallas kernels for 23% -> 23%
where the time goes in v6:
time: 27.8 us; the launch traced here: 27.7 us
  Pallas kernels  11.5 us (41%)
  starting transfers between devices  9.15 us (33%)
  waiting for transfers between devices  4.66 us (17%)
  local copies, waits for them, and re-layouts  1.59 us (6%)
  between operations  0.71 us (3%)
    pallas_call x8, Pallas kernels, call(): pl.pallas_call(kernel, out_shape=[jax.ShapeDtypeStruct(shape, dtype) for...  11.5 us
    ppermute x8, starting transfers between devices, swap(): return lax.ppermute(array, ('gx', 'gy'), pairs)  9.15 us
    ppermute x8, waiting for transfers between devices, swap(): return lax.ppermute(array, ('gx', 'gy'), pairs)  4.66 us
    unnamed x10, local copies, waits for them, and re-layouts  1.59 us
  transfers between devices with their start and end apart: 8, of which 3 were waited for; matrix products, arithmetic and copies ran while one was open for 0% of the time, Pallas kernels for 23%

profile of v6, /device:TPU:0, one launch (start us, length us, event | category | flops | bytes accessed | tf_op | source)
XLA Modules:
  0.0 27.7 jit_solution(12247528263943626436)
XLA Ops:
  0.6 0.0 copy-start.3
  0.6 0.0 copy-start.2
  0.7 0.0 copy-start
  0.7 2.3 %first.1 = bf16[1248,128]{1,0:T(8,128)(2,1)} custom-call(bf16[4,128,1152]{2,1,0:T(8,128)(2,1)} %s_hbm.1, f32[3,16,4,128]{3,2,1,0:T(4,128)} %o_ref.5, s32[4,128]{1,0:T(4,128)} %mask_ref.11), custom_call_target="tpu_custom_call" | custom-call | bytes 33554432 | tf_op jit(solution)/shard_map/first/pallas_call | solution.py:553
  3.0 3.1 %collective-permute-start.3 = (bf16[1248,128]{1,0:T(8,128)(2,1)}, bf16[1248,128]{1,0:T(8,128)(2,1)S(1)}, u32[]{:S(2)}, u32[]{:S(2)}) collective-permute-start(bf16[1248,128]{1,0:T(8,128)(2,1)} %first.1), channel_id=1, source_target_pairs={{0,1},{1,0},{2,3},{3,2},{4,8},{5,9},{6,10},{7,11},{8,4},{9,5},{10,... | collective-permute-start | bytes 958472 | tf_op jit(solution)/shard_map/ppermute | solution.py:548
  6.1 0.0 copy-done
  6.1 0.9 %copy-done.1 = f32[3,16,4,128]{3,2,1,0:T(4,128)S(1)} copy-done((f32[3,16,4,128]{3,2,1,0:T(4,128)S(1)}, f32[3,16,4,128]{3,2,1,0:T(4,128)}, u32[]{:S(2)}) %copy-start.1) | copy-done | bytes 98328
  7.0 0.7 %copy-done.4 = s32[4,128]{1,0:T(4,128)S(1)} copy-done((s32[4,128]{1,0:T(4,128)S(1)}, s32[4,128]{1,0:T(4,128)}, u32[]{:S(2)}) %copy-start.4) | copy-done | bytes 2072
  7.7 1.1 %start.1 = (f32[4,36,32,128]{3,2,1,0:T(8,128)S(1)}, bf16[1248,128]{1,0:T(8,128)(2,1)S(1)}, bf16[160,128]{1,0:T(8,128)(2,1)S(1)}, bf16[160,128]{1,0:T(8,128)(2,1)S(1)}, bf16[2,512,128]{2,1,0:T(8,128)(2,1)S(1)}) custom-call(bf16[4,128,1152]{2,1,0:T(8,128)(2,1)S(1)} %copy-done, f32[3,16,4,128]{3,2,1,0:T(4,128)S(1)} %copy-done.1, s32[4,128]{1,0:T(4,128)S(1)} %copy-done.4), custom_call_target="tpu_custom_call" | custom-call | tf_op jit(solution)/shard_map/start/pallas_call | solution.py:553
  8.8 0.1 collective-permute-start.2
  8.9 1.6 %collective-permute-start = (bf16[160,128]{1,0:T(8,128)(2,1)S(1)}, bf16[160,128]{1,0:T(8,128)(2,1)S(1)}, u32[]{:S(2)}, u32[]{:S(2)}) collective-permute-start(bf16[160,128]{1,0:T(8,128)(2,1)S(1)} %get-tuple-element.25), channel_id=1, source_target_pairs={{0,1},{1,0},{2,3},{3,2},{4,5},{5,4},{6,7},{7,6},{8,9},{9,8},{10,11... | collective-permute-start | bytes 122888 | tf_op jit(solution)/shard_map/ppermute | solution.py:548
  10.4 0.0 collective-permute-start.1
  10.4 0.0 copy-done.3
  10.4 0.5 %prepare.1 = (f32[16,128]{1,0:T(8,128)S(1)}, f32[5,36,32,128]{3,2,1,0:T(8,128)S(1)}) custom-call(f32[4,36,32,128]{3,2,1,0:T(8,128)S(1)} %get-tuple-element.23.n_ref, bf16[4,16,1152]{2,1,0:T(8,128)(2,1)S(1)} %copy-done.3), custom_call_target="tpu_custom_call" | custom-call | tf_op jit(solution)/shard_map/prepare/pallas_call | solution.py:553
  11.0 2.0 %collective-permute-done.ye_in = bf16[160,128]{1,0:T(8,128)(2,1)S(1)} collective-permute-done((bf16[160,128]{1,0:T(8,128)(2,1)S(1)}, bf16[160,128]{1,0:T(8,128)(2,1)S(1)}, u32[]{:S(2)}, u32[]{:S(2)}) %collective-permute-start) | collective-permute-done | bytes 40992 | tf_op jit(solution)/shard_map/ppermute | solution.py:548
  12.9 0.0 collective-permute-done.1.yo_in
  12.9 0.0 copy-done.2
  12.9 1.4 %inner.1.acc_in = f32[4,36,32,128]{3,2,1,0:T(8,128)S(1)} custom-call(f32[4,36,32,128]{3,2,1,0:T(8,128)S(1)} %get-tuple-element.23.n_ref, f32[3,16,4,128]{3,2,1,0:T(4,128)S(1)} %copy-done.1, s32[4,128]{1,0:T(4,128)S(1)} %copy-done.4, f32[5,36,32,128]{3,2,1,0:T(8,128)S(1)} %get-tuple-element.24.tab_ref, bf16[2,256,256]{2,1,0:T(8,128)(2,1)S(1)} %copy-done.2, ...), custom_call_target="tpu_custom_call" | custom-call | tf_op jit(solution)/shard_map/inner/pallas_call | solution.py:553
  14.3 0.0 collective-permute-done.3.xo_in
  14.3 0.0 collective-permute-done.2.xe_in
  14.3 0.5 %send.1 = (f32[4,36,32,128]{3,2,1,0:T(8,128)S(1)}, f32[3,16,4,128]{3,2,1,0:T(4,128)S(1)}, f32[36,8,128]{2,1,0:T(8,128)S(1)}, bf16[1264,128]{1,0:T(8,128)(2,1)S(1)}, f32[48,128]{1,0:T(8,128)S(1)}) custom-call(f32[4,36,32,128]{3,2,1,0:T(8,128)S(1)} %get-tuple-element.23.n_ref, f32[4,36,32,128]{3,2,1,0:T(8,128)S(1)} %inner.1.acc_in, ...), custom_call_target="tpu_custom_call", output_to_operand_aliasing={{0}: (1, {})} | custom-call | tf_op jit(solution)/shard_map/send/pallas_call | solution.py:553
  14.8 0.8 %collective-permute-start.7 = (bf16[1264,128]{1,0:T(8,128)(2,1)S(1)}, bf16[1264,128]{1,0:T(8,128)(2,1)S(1)}, u32[]{:S(2)}, u32[]{:S(2)}) collective-permute-start(bf16[1264,128]{1,0:T(8,128)(2,1)S(1)} %get-tuple-element.41), channel_id=1, source_target_pairs={{0,28},{1,29},{2,30},{3,31},{4,8},{5,9},{6,10},{7,11},{8,4},{9,5},... | collective-permute-start | bytes 970760 | tf_op jit(solution)/shard_map/ppermute | solution.py:548
  15.6 1.1 %rest.1 = (f32[4,36,32,128]{3,2,1,0:T(8,128)S(1)}, bf16[1248,128]{1,0:T(8,128)(2,1)S(1)}, bf16[160,128]{1,0:T(8,128)(2,1)S(1)}, bf16[160,128]{1,0:T(8,128)(2,1)S(1)}) custom-call(f32[4,36,32,128]{3,2,1,0:T(8,128)S(1)} %get-tuple-element.23.n_ref, f32[4,36,32,128]{3,2,1,0:T(8,128)S(1)} %get-tuple-element.29.acc_in, ...), custom_call_target="tpu_custom_call", output_to_operand_aliasing={{0}: (1, {})} | custom-call | tf_op jit(solution)/shard_map/rest/pallas_call | solution.py:553
  16.7 0.9 %collective-permute-start.4 = (bf16[1248,128]{1,0:T(8,128)(2,1)S(1)}, bf16[1248,128]{1,0:T(8,128)(2,1)S(1)}, u32[]{:S(2)}, u32[]{:S(2)}) collective-permute-start(bf16[1248,128]{1,0:T(8,128)(2,1)S(1)} %get-tuple-element.35), channel_id=1, source_target_pairs={{0,4},{1,5},{2,6},{3,7},{4,0},{5,1},{6,2},{7,3},{8,12},{9,13},{10,... | collective-permute-start | bytes 958472 | tf_op jit(solution)/shard_map/ppermute | solution.py:548
  17.6 2.7 %collective-permute-start.5 = (bf16[160,128]{1,0:T(8,128)(2,1)S(1)}, bf16[160,128]{1,0:T(8,128)(2,1)S(1)}, u32[]{:S(2)}, u32[]{:S(2)}) collective-permute-start(bf16[160,128]{1,0:T(8,128)(2,1)S(1)} %get-tuple-element.36), channel_id=1, source_target_pairs={{0,1},{1,0},{2,3},{3,2},{4,5},{5,4},{6,7},{7,6},{8,9},{9,8},{10,11... | collective-permute-start | bytes 122888 | tf_op jit(solution)/shard_map/ppermute | solution.py:548
  20.3 0.0 collective-permute-start.6
  20.3 2.0 %collective-permute-done.5.ye_in = bf16[160,128]{1,0:T(8,128)(2,1)S(1)} collective-permute-done((bf16[160,128]{1,0:T(8,128)(2,1)S(1)}, bf16[160,128]{1,0:T(8,128)(2,1)S(1)}, u32[]{:S(2)}, u32[]{:S(2)}) %collective-permute-start.5) | collective-permute-done | bytes 40992 | tf_op jit(solution)/shard_map/ppermute | solution.py:548
  22.3 0.0 collective-permute-done.6.yo_in
  22.3 0.0 collective-permute-done.4.xe_in
  22.3 2.4 %inner_last.1 = (f32[4,1152,128]{2,1,0:T(8,128)S(1)}, f32[16,128]{1,0:T(8,128)S(1)}, bf16[2,128,1152]{2,1,0:T(8,128)(2,1)S(1)}) custom-call(f32[4,36,32,128]{3,2,1,0:T(8,128)S(1)} %get-tuple-element.34.n_ref, f32[3,16,4,128]{3,2,1,0:T(4,128)S(1)} %get-tuple-element.33.o_ref, s32[4,128]{1,0:T(4,128)S(1)} %copy-done.4, ...), custom_call_target="tpu_custom_call" | custom-call | tf_op jit(solution)/shard_map/inner_last/pallas_call | solution.py:553
  24.7 0.7 %collective-permute-done.7.xo_in = bf16[1264,128]{1,0:T(8,128)(2,1)S(1)} collective-permute-done((bf16[1264,128]{1,0:T(8,128)(2,1)S(1)}, bf16[1264,128]{1,0:T(8,128)(2,1)S(1)}, u32[]{:S(2)}, u32[]{:S(2)}) %collective-permute-start.7) | collective-permute-done | bytes 323616 | tf_op jit(solution)/shard_map/ppermute | solution.py:548
  25.4 2.3 %last.1 = (f32[4,1152,128]{2,1,0:T(8,128)S(1)}, f32[3,16,4,128]{3,2,1,0:T(4,128)}, bf16[4,128,1152]{2,1,0:T(8,128)(2,1)}) custom-call(f32[4,36,32,128]{3,2,1,0:T(8,128)S(1)} %get-tuple-element.34.n_ref, f32[4,1152,128]{2,1,0:T(8,128)S(1)} %get-tuple-element.38.acc_in, ...), custom_call_target="tpu_custom_call", output_to_operand_aliasing={{0}: (1, {})} | custom-call | tf_op jit(solution)/shard_map/last/pallas_call | solution.py:553
  (2 shorter events, 0.0 us)
Async XLA Ops:
  0.6 9.8 %copy-start.3 = (bf16[4,16,1152]{2,1,0:T(8,128)(2,1)S(1)}, bf16[4,16,1152]{2,1,0:T(8,128)(2,1)}, u32[]{:S(2)}) copy-start(bf16[4,16,1152]{2,1,0:T(8,128)(2,1)} %constant.4.clone.w_ref) | copy-start | bytes 442372
  0.6 12.3 %copy-start.2 = (bf16[2,256,256]{2,1,0:T(8,128)(2,1)S(1)}, bf16[2,256,256]{2,1,0:T(8,128)(2,1)}, u32[]{:S(2)}) copy-start(bf16[2,256,256]{2,1,0:T(8,128)(2,1)} %constant.5.clone.shift_ref) | copy-start | bytes 786436
  0.7 5.4 %copy-start = (bf16[4,128,1152]{2,1,0:T(8,128)(2,1)S(1)}, bf16[4,128,1152]{2,1,0:T(8,128)(2,1)}, u32[]{:S(2)}) copy-start(bf16[4,128,1152]{2,1,0:T(8,128)(2,1)} %s_hbm.1) | copy-start | bytes 3538948
  3.0 11.3 %collective-permute-start.3 = (bf16[1248,128]{1,0:T(8,128)(2,1)}, bf16[1248,128]{1,0:T(8,128)(2,1)S(1)}, u32[]{:S(2)}, u32[]{:S(2)}) collective-permute-start(bf16[1248,128]{1,0:T(8,128)(2,1)} %first.1), channel_id=1, source_target_pairs={{0,1},{1,0},{2,3},{3,2},{4,8},{5,9},{6,10},{7,11},{8,4},{9,5},{10,... | collective-permute-start | bytes 958472 | tf_op jit(solution)/shard_map/ppermute | solution.py:548
  6.1 0.9 %copy-start.1 = (f32[3,16,4,128]{3,2,1,0:T(4,128)S(1)}, f32[3,16,4,128]{3,2,1,0:T(4,128)}, u32[]{:S(2)}) copy-start(f32[3,16,4,128]{3,2,1,0:T(4,128)} %o_ref.5) | copy-start | bytes 294916
  7.0 0.7 %copy-start.4 = (s32[4,128]{1,0:T(4,128)S(1)}, s32[4,128]{1,0:T(4,128)}, u32[]{:S(2)}) copy-start(s32[4,128]{1,0:T(4,128)} %mask_ref.11) | copy-start | bytes 6148
  8.8 5.6 %collective-permute-start.2 = (bf16[1248,128]{1,0:T(8,128)(2,1)S(1)}, bf16[1248,128]{1,0:T(8,128)(2,1)S(1)}, u32[]{:S(2)}, u32[]{:S(2)}) collective-permute-start(bf16[1248,128]{1,0:T(8,128)(2,1)S(1)} %get-tuple-element.28), channel_id=1, source_target_pairs={{0,4},{1,5},{2,6},{3,7},{4,0},{5,1},{6,2},{7,3},{8,12},{9,13},{10,... | collective-permute-start | bytes 958472 | tf_op jit(solution)/shard_map/ppermute | solution.py:548
  8.9 4.1 %collective-permute-start = (bf16[160,128]{1,0:T(8,128)(2,1)S(1)}, bf16[160,128]{1,0:T(8,128)(2,1)S(1)}, u32[]{:S(2)}, u32[]{:S(2)}) collective-permute-start(bf16[160,128]{1,0:T(8,128)(2,1)S(1)} %get-tuple-element.25), channel_id=1, source_target_pairs={{0,1},{1,0},{2,3},{3,2},{4,5},{5,4},{6,7},{7,6},{8,9},{9,8},{10,11... | collective-permute-start | bytes 122888 | tf_op jit(solution)/shard_map/ppermute | solution.py:548
  10.4 2.5 %collective-permute-start.1 = (bf16[160,128]{1,0:T(8,128)(2,1)S(1)}, bf16[160,128]{1,0:T(8,128)(2,1)S(1)}, u32[]{:S(2)}, u32[]{:S(2)}) collective-permute-start(bf16[160,128]{1,0:T(8,128)(2,1)S(1)} %get-tuple-element.26), channel_id=1, source_target_pairs={{0,4},{1,2},{2,1},{3,7},{4,0},{5,6},{6,5},{7,3},{8,12},{9,10},{10,... | collective-permute-start | bytes 122888 | tf_op jit(solution)/shard_map/ppermute | solution.py:548
  14.8 10.6 %collective-permute-start.7 = (bf16[1264,128]{1,0:T(8,128)(2,1)S(1)}, bf16[1264,128]{1,0:T(8,128)(2,1)S(1)}, u32[]{:S(2)}, u32[]{:S(2)}) collective-permute-start(bf16[1264,128]{1,0:T(8,128)(2,1)S(1)} %get-tuple-element.41), channel_id=1, source_target_pairs={{0,28},{1,29},{2,30},{3,31},{4,8},{5,9},{6,10},{7,11},{8,4},{9,5},... | collective-permute-start | bytes 970760 | tf_op jit(solution)/shard_map/ppermute | solution.py:548
  16.7 5.6 %collective-permute-start.4 = (bf16[1248,128]{1,0:T(8,128)(2,1)S(1)}, bf16[1248,128]{1,0:T(8,128)(2,1)S(1)}, u32[]{:S(2)}, u32[]{:S(2)}) collective-permute-start(bf16[1248,128]{1,0:T(8,128)(2,1)S(1)} %get-tuple-element.35), channel_id=1, source_target_pairs={{0,4},{1,5},{2,6},{3,7},{4,0},{5,1},{6,2},{7,3},{8,12},{9,13},{10,... | collective-permute-start | bytes 958472 | tf_op jit(solution)/shard_map/ppermute | solution.py:548
  17.6 4.7 %collective-permute-start.5 = (bf16[160,128]{1,0:T(8,128)(2,1)S(1)}, bf16[160,128]{1,0:T(8,128)(2,1)S(1)}, u32[]{:S(2)}, u32[]{:S(2)}) collective-permute-start(bf16[160,128]{1,0:T(8,128)(2,1)S(1)} %get-tuple-element.36), channel_id=1, source_target_pairs={{0,1},{1,0},{2,3},{3,2},{4,5},{5,4},{6,7},{7,6},{8,9},{9,8},{10,11... | collective-permute-start | bytes 122888 | tf_op jit(solution)/shard_map/ppermute | solution.py:548
  20.3 2.0 %collective-permute-start.6 = (bf16[160,128]{1,0:T(8,128)(2,1)S(1)}, bf16[160,128]{1,0:T(8,128)(2,1)S(1)}, u32[]{:S(2)}, u32[]{:S(2)}) collective-permute-start(bf16[160,128]{1,0:T(8,128)(2,1)S(1)} %get-tuple-element.37), channel_id=1, source_target_pairs={{0,4},{1,2},{2,1},{3,7},{4,0},{5,6},{6,5},{7,3},{8,12},{9,10},{10,... | collective-permute-start | bytes 122888 | tf_op jit(solution)/shard_map/ppermute | solution.py:548

commit v7 on v6

--- a/solution.py
+++ b/solution.py
@@ -31,7 +31,7 @@
 BF16 = jnp.bfloat16
 VM = pl.BlockSpec(memory_space=pltpu.VMEM)
 HBM = pl.BlockSpec(memory_space=pl.ANY)
-FIRST = pltpu.CompilerParams(vmem_limit_bytes=56 * 1024 * 1024)
+FIRST = pltpu.CompilerParams(vmem_limit_bytes=53 * 1024 * 1024)
 PARAMS = pltpu.CompilerParams(vmem_limit_bytes=16 * 1024 * 1024)
 
 SPECTRA = 2 * HALF * NF
@@ -427,7 +427,7 @@
         acc_ref[inner_cell] = keep(wet_inner * (acc_ref[inner_cell] + near * tab_ref[2, k]))
         return carry
 
-    lax.fori_loop(0, HALF, body, 0, unroll=18)
+    lax.fori_loop(0, HALF, body, 0, unroll=6)
 
 
 def rounded(v):

time: 27.8 us -> 27.6 us (level)
  the two profiles are of different devices: /device:TPU:0 before, /device:TPU:8 now
where the time goes in v7:
time: 27.6 us; the launch traced here: 27.4 us
  Pallas kernels  10.7 us (39%)
  starting transfers between devices  8.65 us (31%)
  waiting for transfers between devices  5.05 us (18%)
  local copies, waits for them, and re-layouts  2.25 us (8%)
  between operations  0.72 us (3%)
    pallas_call x8, Pallas kernels, call(): pl.pallas_call(kernel, out_shape=[jax.ShapeDtypeStruct(shape, dtype) for...  10.7 us
    ppermute x8, starting transfers between devices, swap(): return lax.ppermute(array, ('gx', 'gy'), pairs)  8.65 us
    ppermute x8, waiting for transfers between devices, swap(): return lax.ppermute(array, ('gx', 'gy'), pairs)  5.05 us
    unnamed x12, local copies, waits for them, and re-layouts  2.25 us
  transfers between devices with their start and end apart: 8, of which 4 were waited for; matrix products, arithmetic and copies ran while one was open for 0% of the time, Pallas kernels for 23%

profile of v7, /device:TPU:8, one launch (start us, length us, event | category | flops | bytes accessed | tf_op | source)
XLA Modules:
  0.0 27.4 jit_solution(2488921968420431868)
XLA Ops:
  0.6 0.0 copy-start.1
  0.6 0.9 %copy-done.1 = f32[3,16,4,128]{3,2,1,0:T(4,128)S(1)} copy-done((f32[3,16,4,128]{3,2,1,0:T(4,128)S(1)}, f32[3,16,4,128]{3,2,1,0:T(4,128)}, u32[]{:S(2)}) %copy-start.1) | copy-done | bytes 98328
  1.5 0.7 %copy-done.4 = s32[4,128]{1,0:T(4,128)S(1)} copy-done((s32[4,128]{1,0:T(4,128)S(1)}, s32[4,128]{1,0:T(4,128)}, u32[]{:S(2)}) %copy-start.4) | copy-done | bytes 2072
  2.2 1.6 %first.1 = bf16[1248,128]{1,0:T(8,128)(2,1)S(1)} custom-call(bf16[4,128,1152]{2,1,0:T(8,128)(2,1)} %s_hbm.1, f32[3,16,4,128]{3,2,1,0:T(4,128)S(1)} %copy-done.1, s32[4,128]{1,0:T(4,128)S(1)} %copy-done.4), custom_call_target="tpu_custom_call" | custom-call | bytes 33554432 | tf_op jit(solution)/shard_map/first/pallas_call | solution.py:553
  3.8 0.1 collective-permute-start.3
  3.9 0.0 copy-done
  3.9 0.0 copy-start.5
  3.9 0.7 %copy-done.5 = s32[4,128]{1,0:T(4,128)S(1)} copy-done((s32[4,128]{1,0:T(4,128)S(1)}, s32[4,128]{1,0:T(4,128)}, u32[]{:S(2)}) %copy-start.5) | copy-done | bytes 2072
  4.6 1.1 %start.1 = (f32[4,36,32,128]{3,2,1,0:T(8,128)S(1)}, bf16[1248,128]{1,0:T(8,128)(2,1)S(1)}, bf16[160,128]{1,0:T(8,128)(2,1)S(1)}, bf16[160,128]{1,0:T(8,128)(2,1)S(1)}, bf16[2,512,128]{2,1,0:T(8,128)(2,1)S(1)}) custom-call(bf16[4,128,1152]{2,1,0:T(8,128)(2,1)S(1)} %copy-done, f32[3,16,4,128]{3,2,1,0:T(4,128)S(1)} %copy-done.1, s32[4,128]{1,0:T(4,128)S(1)} %copy-done.5), custom_call_target="tpu_custom_call" | custom-call | tf_op jit(solution)/shard_map/start/pallas_call | solution.py:553
  5.7 1.6 %collective-permute-start.2 = (bf16[1248,128]{1,0:T(8,128)(2,1)S(1)}, bf16[1248,128]{1,0:T(8,128)(2,1)S(1)}, u32[]{:S(2)}, u32[]{:S(2)}) collective-permute-start(bf16[1248,128]{1,0:T(8,128)(2,1)S(1)} %get-tuple-element.28), channel_id=1, source_target_pairs={{0,4},{1,5},{2,6},{3,7},{4,0},{5,1},{6,2},{7,3},{8,12},{9,13},{10,... | collective-permute-start | bytes 958472 | tf_op jit(solution)/shard_map/ppermute | solution.py:548
  7.3 0.5 %collective-permute-start = (bf16[160,128]{1,0:T(8,128)(2,1)S(1)}, bf16[160,128]{1,0:T(8,128)(2,1)S(1)}, u32[]{:S(2)}, u32[]{:S(2)}) collective-permute-start(bf16[160,128]{1,0:T(8,128)(2,1)S(1)} %get-tuple-element.25), channel_id=1, source_target_pairs={{0,1},{1,0},{2,3},{3,2},{4,5},{5,4},{6,7},{7,6},{8,9},{9,8},{10,11... | collective-permute-start | bytes 122888 | tf_op jit(solution)/shard_map/ppermute | solution.py:548
  7.8 2.7 %collective-permute-start.1 = (bf16[160,128]{1,0:T(8,128)(2,1)S(1)}, bf16[160,128]{1,0:T(8,128)(2,1)S(1)}, u32[]{:S(2)}, u32[]{:S(2)}) collective-permute-start(bf16[160,128]{1,0:T(8,128)(2,1)S(1)} %get-tuple-element.26), channel_id=1, source_target_pairs={{0,4},{1,2},{2,1},{3,7},{4,0},{5,6},{6,5},{7,3},{8,12},{9,10},{10,... | collective-permute-start | bytes 122888 | tf_op jit(solution)/shard_map/ppermute | solution.py:548
  10.5 0.0 copy-done.3
  10.5 0.5 %prepare.1 = (f32[16,128]{1,0:T(8,128)S(1)}, f32[5,36,32,128]{3,2,1,0:T(8,128)S(1)}) custom-call(f32[4,36,32,128]{3,2,1,0:T(8,128)S(1)} %get-tuple-element.23.n_ref, bf16[4,16,1152]{2,1,0:T(8,128)(2,1)S(1)} %copy-done.3), custom_call_target="tpu_custom_call" | custom-call | tf_op jit(solution)/shard_map/prepare/pallas_call | solution.py:553
  11.0 0.7 %collective-permute-done.ye_in = bf16[160,128]{1,0:T(8,128)(2,1)S(1)} collective-permute-done((bf16[160,128]{1,0:T(8,128)(2,1)S(1)}, bf16[160,128]{1,0:T(8,128)(2,1)S(1)}, u32[]{:S(2)}, u32[]{:S(2)}) %collective-permute-start) | collective-permute-done | bytes 40992 | tf_op jit(solution)/shard_map/ppermute | solution.py:548
  11.8 0.7 %collective-permute-done.1.yo_in = bf16[160,128]{1,0:T(8,128)(2,1)S(1)} collective-permute-done((bf16[160,128]{1,0:T(8,128)(2,1)S(1)}, bf16[160,128]{1,0:T(8,128)(2,1)S(1)}, u32[]{:S(2)}, u32[]{:S(2)}) %collective-permute-start.1) | collective-permute-done | bytes 40992 | tf_op jit(solution)/shard_map/ppermute | solution.py:548
  12.5 0.0 copy-done.2
  12.5 1.4 %inner.1.acc_in = f32[4,36,32,128]{3,2,1,0:T(8,128)S(1)} custom-call(f32[4,36,32,128]{3,2,1,0:T(8,128)S(1)} %get-tuple-element.23.n_ref, f32[3,16,4,128]{3,2,1,0:T(4,128)S(1)} %copy-done.1, s32[4,128]{1,0:T(4,128)S(1)} %copy-done.5, f32[5,36,32,128]{3,2,1,0:T(8,128)S(1)} %get-tuple-element.24.tab_ref, bf16[2,256,256]{2,1,0:T(8,128)(2,1)S(1)} %copy-done.2, ...), custom_call_target="tpu_custom_call" | custom-call | tf_op jit(solution)/shard_map/inner/pallas_call | solution.py:553
  13.9 0.0 collective-permute-done.3.xo_in
  13.9 0.0 collective-permute-done.2.xe_in
  13.9 0.5 %send.1 = (f32[4,36,32,128]{3,2,1,0:T(8,128)S(1)}, f32[3,16,4,128]{3,2,1,0:T(4,128)S(1)}, f32[36,8,128]{2,1,0:T(8,128)S(1)}, bf16[1264,128]{1,0:T(8,128)(2,1)S(1)}, f32[48,128]{1,0:T(8,128)S(1)}) custom-call(f32[4,36,32,128]{3,2,1,0:T(8,128)S(1)} %get-tuple-element.23.n_ref, f32[4,36,32,128]{3,2,1,0:T(8,128)S(1)} %inner.1.acc_in, ...), custom_call_target="tpu_custom_call", output_to_operand_aliasing={{0}: (1, {})} | custom-call | tf_op jit(solution)/shard_map/send/pallas_call | solution.py:553
  14.4 0.4 %collective-permute-start.7 = (bf16[1264,128]{1,0:T(8,128)(2,1)S(1)}, bf16[1264,128]{1,0:T(8,128)(2,1)S(1)}, u32[]{:S(2)}, u32[]{:S(2)}) collective-permute-start(bf16[1264,128]{1,0:T(8,128)(2,1)S(1)} %get-tuple-element.41), channel_id=1, source_target_pairs={{0,28},{1,29},{2,30},{3,31},{4,8},{5,9},{6,10},{7,11},{8,4},{9,5},... | collective-permute-start | bytes 970760 | tf_op jit(solution)/shard_map/ppermute | solution.py:548
  14.7 1.2 %rest.1 = (f32[4,36,32,128]{3,2,1,0:T(8,128)S(1)}, bf16[1248,128]{1,0:T(8,128)(2,1)S(1)}, bf16[160,128]{1,0:T(8,128)(2,1)S(1)}, bf16[160,128]{1,0:T(8,128)(2,1)S(1)}) custom-call(f32[4,36,32,128]{3,2,1,0:T(8,128)S(1)} %get-tuple-element.23.n_ref, f32[4,36,32,128]{3,2,1,0:T(8,128)S(1)} %get-tuple-element.29.acc_in, ...), custom_call_target="tpu_custom_call", output_to_operand_aliasing={{0}: (1, {})} | custom-call | tf_op jit(solution)/shard_map/rest/pallas_call | solution.py:553
  15.9 1.4 %collective-permute-start.4 = (bf16[1248,128]{1,0:T(8,128)(2,1)S(1)}, bf16[1248,128]{1,0:T(8,128)(2,1)S(1)}, u32[]{:S(2)}, u32[]{:S(2)}) collective-permute-start(bf16[1248,128]{1,0:T(8,128)(2,1)S(1)} %get-tuple-element.35), channel_id=1, source_target_pairs={{0,4},{1,5},{2,6},{3,7},{4,0},{5,1},{6,2},{7,3},{8,12},{9,13},{10,... | collective-permute-start | bytes 958472 | tf_op jit(solution)/shard_map/ppermute | solution.py:548
  17.3 0.0 collective-permute-start.5
  17.3 2.0 %collective-permute-start.6 = (bf16[160,128]{1,0:T(8,128)(2,1)S(1)}, bf16[160,128]{1,0:T(8,128)(2,1)S(1)}, u32[]{:S(2)}, u32[]{:S(2)}) collective-permute-start(bf16[160,128]{1,0:T(8,128)(2,1)S(1)} %get-tuple-element.37), channel_id=1, source_target_pairs={{0,4},{1,2},{2,1},{3,7},{4,0},{5,6},{6,5},{7,3},{8,12},{9,10},{10,... | collective-permute-start | bytes 122888 | tf_op jit(solution)/shard_map/ppermute | solution.py:548
  19.3 2.0 %collective-permute-done.5.ye_in = bf16[160,128]{1,0:T(8,128)(2,1)S(1)} collective-permute-done((bf16[160,128]{1,0:T(8,128)(2,1)S(1)}, bf16[160,128]{1,0:T(8,128)(2,1)S(1)}, u32[]{:S(2)}, u32[]{:S(2)}) %collective-permute-start.5) | collective-permute-done | bytes 40992 | tf_op jit(solution)/shard_map/ppermute | solution.py:548
  21.3 0.0 collective-permute-done.6.yo_in
  21.3 0.0 collective-permute-done.4.xe_in
  21.3 2.2 %inner_last.1 = (f32[4,1152,128]{2,1,0:T(8,128)S(1)}, f32[16,128]{1,0:T(8,128)S(1)}, bf16[2,128,1152]{2,1,0:T(8,128)(2,1)S(1)}) custom-call(f32[4,36,32,128]{3,2,1,0:T(8,128)S(1)} %get-tuple-element.34.n_ref, f32[3,16,4,128]{3,2,1,0:T(4,128)S(1)} %get-tuple-element.33.o_ref, s32[4,128]{1,0:T(4,128)S(1)} %copy-done.5, ...), custom_call_target="tpu_custom_call" | custom-call | tf_op jit(solution)/shard_map/inner_last/pallas_call | solution.py:553
  23.5 1.6 %collective-permute-done.7.xo_in = bf16[1264,128]{1,0:T(8,128)(2,1)S(1)} collective-permute-done((bf16[1264,128]{1,0:T(8,128)(2,1)S(1)}, bf16[1264,128]{1,0:T(8,128)(2,1)S(1)}, u32[]{:S(2)}, u32[]{:S(2)}) %collective-permute-start.7) | collective-permute-done | bytes 323616 | tf_op jit(solution)/shard_map/ppermute | solution.py:548
  25.1 2.3 %last.1 = (f32[4,1152,128]{2,1,0:T(8,128)S(1)}, f32[3,16,4,128]{3,2,1,0:T(4,128)}, bf16[4,128,1152]{2,1,0:T(8,128)(2,1)}) custom-call(f32[4,36,32,128]{3,2,1,0:T(8,128)S(1)} %get-tuple-element.34.n_ref, f32[4,1152,128]{2,1,0:T(8,128)S(1)} %get-tuple-element.38.acc_in, ...), custom_call_target="tpu_custom_call", output_to_operand_aliasing={{0}: (1, {})} | custom-call | tf_op jit(solution)/shard_map/last/pallas_call | solution.py:553
  (4 shorter events, 0.0 us)
Async XLA Ops:
  0.6 0.9 %copy-start.1 = (f32[3,16,4,128]{3,2,1,0:T(4,128)S(1)}, f32[3,16,4,128]{3,2,1,0:T(4,128)}, u32[]{:S(2)}) copy-start(f32[3,16,4,128]{3,2,1,0:T(4,128)} %o_ref.5) | copy-start | bytes 294916
  1.5 0.7 %copy-start.4 = (s32[4,128]{1,0:T(4,128)S(1)}, s32[4,128]{1,0:T(4,128)}, u32[]{:S(2)}) copy-start(s32[4,128]{1,0:T(4,128)} %mask_ref.11) | copy-start | bytes 6148
  2.2 1.7 %copy-start = (bf16[4,128,1152]{2,1,0:T(8,128)(2,1)S(1)}, bf16[4,128,1152]{2,1,0:T(8,128)(2,1)}, u32[]{:S(2)}) copy-start(bf16[4,128,1152]{2,1,0:T(8,128)(2,1)} %s_hbm.1) | copy-start | bytes 3538948
  2.2 8.3 %copy-start.3 = (bf16[4,16,1152]{2,1,0:T(8,128)(2,1)S(1)}, bf16[4,16,1152]{2,1,0:T(8,128)(2,1)}, u32[]{:S(2)}) copy-start(bf16[4,16,1152]{2,1,0:T(8,128)(2,1)} %constant.4.clone.w_ref) | copy-start | bytes 442372
  2.2 10.3 %copy-start.2 = (bf16[2,256,256]{2,1,0:T(8,128)(2,1)S(1)}, bf16[2,256,256]{2,1,0:T(8,128)(2,1)}, u32[]{:S(2)}) copy-start(bf16[2,256,256]{2,1,0:T(8,128)(2,1)} %constant.5.clone.shift_ref) | copy-start | bytes 786436
  3.8 10.1 %collective-permute-start.3 = (bf16[1248,128]{1,0:T(8,128)(2,1)S(1)}, bf16[1248,128]{1,0:T(8,128)(2,1)S(1)}, u32[]{:S(2)}, u32[]{:S(2)}) collective-permute-start(bf16[1248,128]{1,0:T(8,128)(2,1)S(1)} %first.1), channel_id=1, source_target_pairs={{0,1},{1,0},{2,3},{3,2},{4,8},{5,9},{6,10},{7,11},{8,4},{9,5},{10,... | collective-permute-start | bytes 958472 | tf_op jit(solution)/shard_map/ppermute | solution.py:548
  3.9 0.7 %copy-start.5 = (s32[4,128]{1,0:T(4,128)S(1)}, s32[4,128]{1,0:T(4,128)}, u32[]{:S(2)}) copy-start(s32[4,128]{1,0:T(4,128)} %mask_ref.11) | copy-start | bytes 6148
  5.7 8.2 %collective-permute-start.2 = (bf16[1248,128]{1,0:T(8,128)(2,1)S(1)}, bf16[1248,128]{1,0:T(8,128)(2,1)S(1)}, u32[]{:S(2)}, u32[]{:S(2)}) collective-permute-start(bf16[1248,128]{1,0:T(8,128)(2,1)S(1)} %get-tuple-element.28), channel_id=1, source_target_pairs={{0,4},{1,5},{2,6},{3,7},{4,0},{5,1},{6,2},{7,3},{8,12},{9,13},{10,... | collective-permute-start | bytes 958472 | tf_op jit(solution)/shard_map/ppermute | solution.py:548
  7.3 4.4 %collective-permute-start = (bf16[160,128]{1,0:T(8,128)(2,1)S(1)}, bf16[160,128]{1,0:T(8,128)(2,1)S(1)}, u32[]{:S(2)}, u32[]{:S(2)}) collective-permute-start(bf16[160,128]{1,0:T(8,128)(2,1)S(1)} %get-tuple-element.25), channel_id=1, source_target_pairs={{0,1},{1,0},{2,3},{3,2},{4,5},{5,4},{6,7},{7,6},{8,9},{9,8},{10,11... | collective-permute-start | bytes 122888 | tf_op jit(solution)/shard_map/ppermute | solution.py:548
  7.8 4.6 %collective-permute-start.1 = (bf16[160,128]{1,0:T(8,128)(2,1)S(1)}, bf16[160,128]{1,0:T(8,128)(2,1)S(1)}, u32[]{:S(2)}, u32[]{:S(2)}) collective-permute-start(bf16[160,128]{1,0:T(8,128)(2,1)S(1)} %get-tuple-element.26), channel_id=1, source_target_pairs={{0,4},{1,2},{2,1},{3,7},{4,0},{5,6},{6,5},{7,3},{8,12},{9,10},{10,... | collective-permute-start | bytes 122888 | tf_op jit(solution)/shard_map/ppermute | solution.py:548
  14.4 10.8 %collective-permute-start.7 = (bf16[1264,128]{1,0:T(8,128)(2,1)S(1)}, bf16[1264,128]{1,0:T(8,128)(2,1)S(1)}, u32[]{:S(2)}, u32[]{:S(2)}) collective-permute-start(bf16[1264,128]{1,0:T(8,128)(2,1)S(1)} %get-tuple-element.41), channel_id=1, source_target_pairs={{0,28},{1,29},{2,30},{3,31},{4,8},{5,9},{6,10},{7,11},{8,4},{9,5},... | collective-permute-start | bytes 970760 | tf_op jit(solution)/shard_map/ppermute | solution.py:548
  15.9 5.4 %collective-permute-start.4 = (bf16[1248,128]{1,0:T(8,128)(2,1)S(1)}, bf16[1248,128]{1,0:T(8,128)(2,1)S(1)}, u32[]{:S(2)}, u32[]{:S(2)}) collective-permute-start(bf16[1248,128]{1,0:T(8,128)(2,1)S(1)} %get-tuple-element.35), channel_id=1, source_target_pairs={{0,4},{1,5},{2,6},{3,7},{4,0},{5,1},{6,2},{7,3},{8,12},{9,13},{10,... | collective-permute-start | bytes 958472 | tf_op jit(solution)/shard_map/ppermute | solution.py:548
  17.3 4.0 %collective-permute-start.5 = (bf16[160,128]{1,0:T(8,128)(2,1)S(1)}, bf16[160,128]{1,0:T(8,128)(2,1)S(1)}, u32[]{:S(2)}, u32[]{:S(2)}) collective-permute-start(bf16[160,128]{1,0:T(8,128)(2,1)S(1)} %get-tuple-element.36), channel_id=1, source_target_pairs={{0,1},{1,0},{2,3},{3,2},{4,5},{5,4},{6,7},{7,6},{8,9},{9,8},{10,11... | collective-permute-start | bytes 122888 | tf_op jit(solution)/shard_map/ppermute | solution.py:548
  17.3 4.0 %collective-permute-start.6 = (bf16[160,128]{1,0:T(8,128)(2,1)S(1)}, bf16[160,128]{1,0:T(8,128)(2,1)S(1)}, u32[]{:S(2)}, u32[]{:S(2)}) collective-permute-start(bf16[160,128]{1,0:T(8,128)(2,1)S(1)} %get-tuple-element.37), channel_id=1, source_target_pairs={{0,4},{1,2},{2,1},{3,7},{4,0},{5,6},{6,5},{7,3},{8,12},{9,10},{10,... | collective-permute-start | bytes 122888 | tf_op jit(solution)/shard_map/ppermute | solution.py:548
